TPU v7x, 32 devices: a whole 2x2x4 slice. The times are simulated.
32 devices in a mesh: group: 2 (over y), tensor: 4 (over z), dp: 4 (over x, core).
Axes of the slice: x: 2, y: 2, z: 4, core: 2. Of those that a mesh axis runs over, the one named last changes fastest.
Arguments:
- tokens: bfloat16 [1024, 8192], P(('group', 'dp'), 'tensor'), parts along dimension 0, may hold values from -6 to 6
- key_output_gradient: bfloat16 [1024, 1024], P(('group', 'dp'), 'tensor'), parts along dimension 0, may hold values from -6 to 6
- value_output_gradient: bfloat16 [1024, 1024], P(('group', 'dp'), 'tensor'), parts along dimension 0, may hold values from -6 to 6
- frozen_key_weight: bfloat16 [8192, 1024], P(None, 'tensor'), may hold values from -0.09375 to 0.09375
- frozen_value_weight: bfloat16 [8192, 1024], P(None, 'tensor'), may hold values from -0.09375 to 0.09375
- key_down_matrices: bfloat16 [64, 16, 8192], P(None, None, 'tensor'), may hold values from -0.0625 to 0.0625
- value_down_matrices: bfloat16 [64, 16, 8192], P(None, None, 'tensor'), may hold values from -0.0625 to 0.0625
- key_up_matrices: bfloat16 [64, 16, 1024], P(None, None, 'tensor'), may hold values from -0.1875 to 0.1875
- value_up_matrices: bfloat16 [64, 16, 1024], P(None, None, 'tensor'), may hold values from -0.1875 to 0.1875
- segment_length: int32 [8, 16], P(('group', 'dp')), parts along dimension 0, may hold values from 1 to 32, 128 in all within a row
- segment_tenant: int32 [8, 16], P(('group', 'dp')), parts along dimension 0, may hold values from 0 to 63, as said below
- adapter_output_slot: int32 [128], P('group'), parts along dimension 0, may hold values from 0 to 63, as said below
Outputs:
- input_gradient: bfloat16 [1024, 8192], P(('group', 'dp'), 'tensor'), parts along dimension 0
- key_grad_a: float32 [128, 16, 8192], P(('group', 'dp'), None, 'tensor'), parts along dimension 0
- value_grad_a: float32 [128, 16, 8192], P(('group', 'dp'), None, 'tensor'), parts along dimension 0
- key_grad_b: float32 [128, 16, 1024], P(('group', 'dp'), None, 'tensor'), parts along dimension 0
- value_grad_b: float32 [128, 16, 1024], P(('group', 'dp'), None, 'tensor'), parts along dimension 0
There are 2 independent parts, one for each index of `group`. A program takes and returns all parts, laid end to end along the dimension named above; an argument that names none is the same for every part. Nothing has to cross between parts.
Inputs may be any that keep to these rules, and one draw needn't show every extreme that they name: `segment_length`: each row of blocks sums to 128, and its largest entry is 32. `segment_tenant`: call slots q * 16 to (q + 1) * 16 - 1 the range of q. In each block at most 4 segments have tenants whose adapter_output_slot lies in one range, and in every block some range receives exactly 4. `adapter_output_slot`: each of 0 to 63 appears once.
All inputs are finite; a program needn't handle non-finite values.
Results may differ from a plain program's by a relative error of at most 0.013.
Values may be sent and summed in bfloat16 or wider, within the bound.
No kernel may reach another device: no remote copies, remote signals or barrier semaphores. Data moves between devices by JAX's collectives and lax.ppermute only.
A program may use at most 128 MiB of HBM per device.

v0:
```python
import jax
import jax.numpy as jnp
from jax import lax
from jax.sharding import PartitionSpec as P

ADAPTER_SCALE = 2.0
LOSS_UNSCALE = 0.125


def contract_cols(former, latter):
    return lax.dot_general(
        former, latter, (((1,), (1,)), ((), ())), preferred_element_type=jnp.float32
    )


def contracted_rows(former, latter):
    return lax.dot_general(
        former, latter, (((0,), (0,)), ((), ())), preferred_element_type=jnp.float32
    )


def exact_dot(former, latter):
    return jnp.dot(former, latter, precision=lax.Precision.HIGHEST)


def local(
    tokens,
    key_output_gradient,
    value_output_gradient,
    frozen_key_weight,
    frozen_value_weight,
    key_down_matrices,
    value_down_matrices,
    key_up_matrices,
    value_up_matrices,
    segment_length,
    segment_tenant,
    adapter_output_slot,
):
    row_count = tokens.shape[0]
    tenant_list = segment_tenant[0]
    segment_count = tenant_list.shape[0]
    adapter_rank_size = key_down_matrices.shape[1]
    segment_lengths = segment_length[0]
    seg_ends = jnp.cumsum(segment_lengths)
    starts = seg_ends - segment_lengths
    position = jnp.arange(row_count, dtype=jnp.int32)[:, None]
    member = ((position >= starts[None, :]) & (position < seg_ends[None, :])).astype(jnp.float32)

    def collapse(values):
        return jnp.sum(
            values.reshape(row_count, segment_count, adapter_rank_size) * member[:, :, None], axis=1
        )

    def spread_rows(values):
        widened = member[:, :, None] * values.astype(jnp.float32)[:, None, :]
        return widened.reshape(row_count, segment_count * adapter_rank_size).astype(jnp.bfloat16)

    key_down_rows = key_down_matrices[tenant_list].reshape(segment_count * adapter_rank_size, -1)
    value_down_rows = value_down_matrices[tenant_list].reshape(
        segment_count * adapter_rank_size, -1
    )
    key_up_rows = key_up_matrices[tenant_list].reshape(segment_count * adapter_rank_size, -1)
    value_up_rows = value_up_matrices[tenant_list].reshape(segment_count * adapter_rank_size, -1)
    key_down_gradient = collapse(contract_cols(tokens, key_down_rows))
    value_down_gradient = collapse(contract_cols(tokens, value_down_rows))
    back_key = collapse(contract_cols(key_output_gradient, key_up_rows))
    back_value = collapse(contract_cols(value_output_gradient, value_up_rows))
    key_down_gradient, value_down_gradient, back_key, back_value = (
        lax.psum(key_down_gradient.astype(jnp.bfloat16), "tensor").astype(jnp.float32),
        lax.psum(value_down_gradient.astype(jnp.bfloat16), "tensor").astype(jnp.float32),
        lax.psum(back_key.astype(jnp.bfloat16), "tensor").astype(jnp.float32),
        lax.psum(back_value.astype(jnp.bfloat16), "tensor").astype(jnp.float32),
    )
    key_back_spread = spread_rows(back_key.astype(jnp.bfloat16))
    value_back_spread = spread_rows(back_value.astype(jnp.bfloat16))
    key_down_spread = spread_rows(key_down_gradient.astype(jnp.bfloat16))
    value_down_spread = spread_rows(value_down_gradient.astype(jnp.bfloat16))
    local_adapter = jnp.dot(
        key_back_spread, key_down_rows, preferred_element_type=jnp.float32
    ) + jnp.dot(value_back_spread, value_down_rows, preferred_element_type=jnp.float32)
    partial_grad = contract_cols(key_output_gradient, frozen_key_weight) + contract_cols(
        value_output_gradient, frozen_value_weight
    )
    frozen_gradient = lax.psum_scatter(
        partial_grad.astype(jnp.bfloat16), "tensor", scatter_dimension=1, tiled=True
    ).astype(jnp.float32)
    input_gradient = (frozen_gradient + ADAPTER_SCALE * local_adapter).astype(jnp.bfloat16)
    key_down_partial = ADAPTER_SCALE * contracted_rows(key_back_spread, tokens).reshape(
        segment_count, -1
    )
    value_down_partial = ADAPTER_SCALE * contracted_rows(value_back_spread, tokens).reshape(
        segment_count, -1
    )
    key_up_partial = ADAPTER_SCALE * contracted_rows(key_down_spread, key_output_gradient).reshape(
        segment_count, -1
    )
    value_up_partial = ADAPTER_SCALE * contracted_rows(
        value_down_spread, value_output_gradient
    ).reshape(segment_count, -1)
    owners = lax.axis_size("dp")
    adapter_list = key_down_matrices.shape[0]
    per_owner = adapter_list // owners
    target = adapter_output_slot[tenant_list]
    capacity = max(2, (segment_count + owners - 1) // owners)
    owner_of = target // per_owner
    seg_order = jnp.arange(segment_count, dtype=jnp.int32)
    earlier = seg_order[None, :] < seg_order[:, None]
    same_owner = owner_of[:, None] == owner_of[None, :]
    order_within = jnp.sum((earlier & same_owner).astype(jnp.int32), axis=1)
    slot_index = owner_of * capacity + order_within
    placing = (
        jnp.arange(owners * capacity, dtype=jnp.int32)[:, None] == slot_index[None, :]
    ).astype(jnp.float32)
    local_target = exact_dot(placing, (target % per_owner + 1).astype(jnp.float32)) - 1.0
    incoming = (
        lax.all_to_all(
            exact_dot(placing, key_down_partial).astype(jnp.bfloat16),
            "dp",
            split_axis=0,
            concat_axis=0,
            tiled=True,
        ).astype(jnp.float32),
        lax.all_to_all(
            exact_dot(placing, value_down_partial).astype(jnp.bfloat16),
            "dp",
            split_axis=0,
            concat_axis=0,
            tiled=True,
        ).astype(jnp.float32),
        lax.all_to_all(
            exact_dot(placing, key_up_partial).astype(jnp.bfloat16),
            "dp",
            split_axis=0,
            concat_axis=0,
            tiled=True,
        ).astype(jnp.float32),
        lax.all_to_all(
            exact_dot(placing, value_up_partial).astype(jnp.bfloat16),
            "dp",
            split_axis=0,
            concat_axis=0,
            tiled=True,
        ).astype(jnp.float32),
        lax.all_to_all(
            local_target.astype(jnp.bfloat16), "dp", split_axis=0, concat_axis=0, tiled=True
        ).astype(local_target.dtype),
    )
    picking = (incoming[4][None, :] == jnp.arange(per_owner, dtype=jnp.float32)[:, None]).astype(
        jnp.float32
    )
    summed = [exact_dot(picking, received_part) for received_part in incoming[:4]]
    key_grad_a = (LOSS_UNSCALE * summed[0]).reshape(per_owner, adapter_rank_size, -1)
    value_grad_a = (LOSS_UNSCALE * summed[1]).reshape(per_owner, adapter_rank_size, -1)
    key_grad_b = (LOSS_UNSCALE * summed[2]).reshape(per_owner, adapter_rank_size, -1)
    value_grad_b = (LOSS_UNSCALE * summed[3]).reshape(per_owner, adapter_rank_size, -1)
    return (input_gradient, key_grad_a, value_grad_a, key_grad_b, value_grad_b)


def solution(mesh):
    placed = (
        P(("group", "dp"), "tensor"),
        P(("group", "dp"), "tensor"),
        P(("group", "dp"), "tensor"),
        P(None, "tensor"),
        P(None, "tensor"),
        P(None, None, "tensor"),
        P(None, None, "tensor"),
        P(None, None, "tensor"),
        P(None, None, "tensor"),
        P(("group", "dp"), None),
        P(("group", "dp"), None),
        P("group"),
    )
    return jax.shard_map(
        local,
        mesh=mesh,
        in_specs=placed,
        out_specs=(
            P(("group", "dp"), "tensor"),
            P(("group", "dp"), None, "tensor"),
            P(("group", "dp"), None, "tensor"),
            P(("group", "dp"), None, "tensor"),
            P(("group", "dp"), None, "tensor"),
        ),
        check_vma=False,
    )
```

profile of v0, /device:TPU:0, one launch (start us, length us, event | category | flops | bytes accessed | tf_op | source)
XLA Modules:
  0.0 123.9 jit_solution(5145256834462906866)
XLA Ops:
  7.2 3.9 %fusion.31 = f32[128,8192]{1,0:T(8,128)S(1)} fusion(bf16[128,256]{1,0:T(8,128)(2,1)} %param.13, bf16[8192,256]{1,0:T(8,128)(2,1)} %param.15), kind=kOutput, calls=%fused_computation.75 | convolution fusion | flops 536870912 | bytes 8454144 | tf_op jit(solution)/shard_map/dot_general | solution.py:11
  11.1 2.9 %fusion = bf16[128,8192]{1,0:T(8,128)(2,1)} fusion(f32[128,8192]{1,0:T(8,128)S(1)} %fusion.31, bf16[128,256]{1,0:T(8,128)(2,1)S(1)} %copy-done.5, bf16[8192,256]{1,0:T(8,128)(2,1)S(1)} %copy-done.3), kind=kOutput, calls=%fused_computation.10 | convolution fusion | flops 538968064 | bytes 10551296 | tf_op jit(solution)/shard_map/dot_general | solution.py:11
  16.4 4.2 %all-to-all-start = ((bf16[4,4,1]{1,2,0:T(2,128)(2,1)}), bf16[4,4,1]{1,2,0:T(2,128)(2,1)S(1)}, u32[]{:S(2)}, u32[]{:S(2)}) async-start(bf16[4,4,1]{1,2,0:T(2,128)(2,1)} %all_to_all.52), calls=%async_computation.1 | async-start | bytes 4096 | tf_op jit(solution)/shard_map/all_to_all | solution.py:145
  20.6 2.8 %gather_fusion.3 = bf16[16,16,2048]{2,1,0:T(8,128)(2,1)S(1)} fusion(bf16[64,16,2048]{2,1,0:T(8,128)(2,1)} %param.18, s32[1024]{0:T(1024)S(1)} %pad_clamp_fusion), kind=kCustom, calls=%fused_computation.3 | custom fusion | bytes 2097216 | tf_op jit(solution)/shard_map/gather | solution.py:60
  23.7 1.6 %gather_fusion.2 = bf16[16,16,256]{2,1,0:T(8,128)(2,1)S(1)} fusion(bf16[64,16,256]{2,1,0:T(8,128)(2,1)} %param.20, s32[1024]{0:T(1024)S(1)} %pad_clamp_fusion), kind=kCustom, calls=%fused_computation.2 | custom fusion | bytes 262208 | tf_op jit(solution)/shard_map/gather | solution.py:64
  25.4 1.6 %gather_fusion = bf16[16,16,256]{2,1,0:T(8,128)(2,1)S(1)} fusion(bf16[64,16,256]{2,1,0:T(8,128)(2,1)} %param.19, s32[1024]{0:T(1024)S(1)} %pad_clamp_fusion), kind=kCustom, calls=%fused_computation | custom fusion | bytes 262208 | tf_op jit(solution)/shard_map/gather | solution.py:63
  27.8 2.8 %gather_fusion.1 = bf16[16,16,2048]{2,1,0:T(8,128)(2,1)S(1)} fusion(bf16[64,16,2048]{2,1,0:T(8,128)(2,1)} %param.17, s32[1024]{0:T(1024)S(1)} %pad_clamp_fusion), kind=kCustom, calls=%fused_computation.1 | custom fusion | bytes 2097216 | tf_op jit(solution)/shard_map/gather | solution.py:59
  31.1 20.9 %all-reduce = (bf16[128,16]{0,1:T(8,128)(2,1)S(1)}, bf16[128,16]{0,1:T(8,128)(2,1)S(1)}, bf16[128,16]{0,1:T(8,128)(2,1)S(1)}, bf16[128,16]{0,1:T(8,128)(2,1)S(1)}) all-reduce(bf16[128,16]{0,1:T(8,128)(2,1)S(1)} %get-tuple-element.6, bf16[128,16]{0,1:T(8,128)(2,1)S(1)} %get-tuple-element.8, ...), channel_id=1, replica_groups=mesh['group'=2,'tensor'=4,'dp'=4] {'tensor'}, use_global_device_ids=true, to_apply=%region_5.6 | all-reduce | flops 8192 | bytes 32768 | tf_op jit(solution)/shard_map/psum | solution.py:73
  53.5 1.7 %convolution_multiply_fusion.5 = f32[256,2048]{1,0:T(8,128)} fusion(bf16[128,256]{0,1:T(8,128)(2,1)S(1)} %bitcast.109, bf16[128,2048]{1,0:T(8,128)(2,1)S(1)} %copy-done), kind=kOutput, calls=%fused_computation.16 | convolution fusion | flops 134742016 | bytes 2686976 | tf_op jit(solution)/shard_map/dot_general | solution.py:17
  55.3 3.7 %all-to-all-start.3 = ((bf16[4,4,4096]{2,1,0:T(4,128)(2,1)}), bf16[4,4,4096]{2,1,0:T(4,128)(2,1)S(1)}, u32[]{:S(2)}, u32[]{:S(2)}) async-start(bf16[4,4,4096]{2,1,0:T(4,128)(2,1)} %all_to_all.46), calls=%async_computation.4 | async-start | bytes 262144 | tf_op jit(solution)/shard_map/all_to_all | solution.py:131
  59.2 2.7 %mul.140 = f32[16,32768]{1,0:T(8,128)} reshape(f32[256,2048]{1,0:T(8,128)} %convolution_multiply_fusion.5) | data formatting | bytes 4194304 | tf_op jit(solution)/shard_map/mul | solution.py:89
  62.6 0.9 all-to-all-done.3
  63.6 3.3 %all-to-all-start.4 = ((bf16[4,4,4096]{2,1,0:T(4,128)(2,1)}), bf16[4,4,4096]{2,1,0:T(4,128)(2,1)S(1)}, u32[]{:S(2)}, u32[]{:S(2)}) async-start(bf16[4,4,4096]{2,1,0:T(4,128)(2,1)} %all_to_all.49), calls=%async_computation.5 | async-start | bytes 262144 | tf_op jit(solution)/shard_map/all_to_all | solution.py:138
  66.9 3.7 %convolution_convert_fusion.1 = bf16[16,32768]{1,0:T(8,128)(2,1)} fusion(f32[16,32768]{1,0:T(8,128)} %mul.140, s32[16]{0:T(128)S(1)} %multiply_add_fusion), kind=kOutput, calls=%fused_computation.8 | convolution fusion | flops 101187840 | bytes 3145792 | tf_op jit(solution)/shard_map/dot_general | solution.py:23
  70.6 2.3 %all_to_all.40 = bf16[4,4,32768]{2,1,0:T(4,128)(2,1)} reshape(bf16[16,32768]{1,0:T(8,128)(2,1)} %convolution_convert_fusion.1) | data formatting | bytes 2097152 | tf_op jit(solution)/shard_map/all_to_all | solution.py:117
  72.8 4.3 %all-to-all-start.1 = ((bf16[4,4,32768]{2,1,0:T(4,128)(2,1)}), bf16[4,4,32768]{2,1,0:T(4,128)(2,1)}, u32[]{:S(2)}, u32[]{:S(2)}) async-start(bf16[4,4,32768]{2,1,0:T(4,128)(2,1)} %all_to_all.40), calls=%async_computation.2 | async-start | bytes 2097152 | tf_op jit(solution)/shard_map/all_to_all | solution.py:117
  77.1 1.7 %convolution_multiply_fusion.4 = f32[256,2048]{1,0:T(8,128)} fusion(bf16[128,256]{0,1:T(8,128)(2,1)S(1)} %bitcast.108, bf16[128,2048]{1,0:T(8,128)(2,1)S(1)} %copy-done), kind=kOutput, calls=%fused_computation.15 | convolution fusion | flops 134742016 | bytes 2686976 | tf_op jit(solution)/shard_map/dot_general | solution.py:17
  78.8 2.7 %mul.143 = f32[16,32768]{1,0:T(8,128)} reshape(f32[256,2048]{1,0:T(8,128)} %convolution_multiply_fusion.4) | data formatting | bytes 4194304 | tf_op jit(solution)/shard_map/mul | solution.py:92
  81.6 3.7 %convolution_convert_fusion = bf16[16,32768]{1,0:T(8,128)(2,1)} fusion(f32[16,32768]{1,0:T(8,128)} %mul.143, s32[16]{0:T(128)S(1)} %multiply_add_fusion), kind=kOutput, calls=%fused_computation.7 | convolution fusion | flops 101187840 | bytes 3145792 | tf_op jit(solution)/shard_map/dot_general | solution.py:23
  85.2 2.2 %all_to_all.43 = bf16[4,4,32768]{2,1,0:T(4,128)(2,1)} reshape(bf16[16,32768]{1,0:T(8,128)(2,1)} %convolution_convert_fusion) | data formatting | bytes 2097152 | tf_op jit(solution)/shard_map/all_to_all | solution.py:124
  87.5 1.3 %convolution_bitcast_fusion = f32[128,2048]{1,0:T(8,128)} fusion(bf16[16,16,2048]{2,1,0:T(8,128)(2,1)S(1)} %gather_fusion.3, f32[128,16]{0,1:T(8,128)S(1)} %convert_element_type.118, f32[128,16]{0,1:T(8,128)S(1)} %fusion.8), kind=kOutput, calls=%fused_computation.17 | convolution fusion | flops 134283264 | bytes 2113536 | tf_op jit(solution)/shard_map/dot_general | solution.py:81
  88.8 2.8 %all-to-all-done.1 = bf16[4,4,32768]{2,1,0:T(4,128)(2,1)} async-done(((bf16[4,4,32768]{2,1,0:T(4,128)(2,1)}), bf16[4,4,32768]{2,1,0:T(4,128)(2,1)}, u32[]{:S(2)}, u32[]{:S(2)}) %all-to-all-start.1) | async-done | bytes 1048608 | tf_op jit(solution)/shard_map/all_to_all | solution.py:117
  91.6 3.7 %all-to-all-start.2 = ((bf16[4,4,32768]{2,1,0:T(4,128)(2,1)}), bf16[4,4,32768]{2,1,0:T(4,128)(2,1)S(1)}, u32[]{:S(2)}, u32[]{:S(2)}) async-start(bf16[4,4,32768]{2,1,0:T(4,128)(2,1)} %all_to_all.43), calls=%async_computation.3 | async-start | bytes 2097152 | tf_op jit(solution)/shard_map/all_to_all | solution.py:124
  95.6 0.8 copy.25
  97.4 2.1 %all_to_all.42 = bf16[16,32768]{1,0:T(8,128)(2,1)} reshape(bf16[4,4,32768]{2,1,0:T(4,128)(2,1)} %all-to-all-done.1) | data formatting | bytes 2097152 | tf_op jit(solution)/shard_map/all_to_all | solution.py:117
  99.6 1.6 %convolution_multiply_fusion.1 = f32[16,32768]{1,0:T(8,128)S(1)} fusion(bf16[16,32768]{1,0:T(8,128)(2,1)} %all_to_all.42, f32[16]{0:T(128)S(1)} %reshape.234), kind=kOutput, calls=%fused_computation.6 | convolution fusion | flops 17301760 | bytes 3145792 | tf_op jit(solution)/shard_map/dot_general | solution.py:23
  101.2 2.5 %copy.23 = f32[2,8,16,2048]{3,2,1,0:T(8,128)} copy(f32[2,8,16,2048]{3,1,2,0:T(8,128)S(1)} %bitcast.93) | data formatting | bytes 4194304
  103.8 5.8 %all-to-all-done.2 = bf16[4,4,32768]{2,1,0:T(4,128)(2,1)S(1)} async-done(((bf16[4,4,32768]{2,1,0:T(4,128)(2,1)}), bf16[4,4,32768]{2,1,0:T(4,128)(2,1)S(1)}, u32[]{:S(2)}, u32[]{:S(2)}) %all-to-all-start.2) | async-done | bytes 1048608 | tf_op jit(solution)/shard_map/all_to_all | solution.py:124
  109.6 1.1 all_to_all.45
  110.7 1.6 %convolution_multiply_fusion = f32[16,32768]{1,0:T(8,128)S(1)} fusion(bf16[16,32768]{1,0:T(8,128)(2,1)} %all_to_all.45, f32[16]{0:T(128)S(1)} %reshape.234), kind=kOutput, calls=%fused_computation.5 | convolution fusion | flops 17301760 | bytes 3145792 | tf_op jit(solution)/shard_map/dot_general | solution.py:23
  112.3 2.5 %copy.24 = f32[2,8,16,2048]{3,2,1,0:T(8,128)} copy(f32[2,8,16,2048]{3,1,2,0:T(8,128)S(1)} %bitcast.92) | data formatting | bytes 4194304
  114.9 2.2 %fusion.4 = bf16[128,2048]{1,0:T(8,128)(2,1)} fusion(f32[128,2048]{1,0:T(8,128)S(1)} %copy-done.2, bf16[16,16,2048]{2,1,0:T(8,128)(2,1)S(1)} %gather_fusion.1, bf16[128,2048]{1,0:T(8,128)(2,1)} %reduce-scatter.2.cloned.1.call-done, f32[128,16]{0,1:T(8,128)S(1)} %convert_element_type.115, f32[128,16]{0,1:T(8,128)S(1)} %fusion.8), kind=kOutput, calls=%fused_computation.22 | convolution fusion | flops 135593984 | bytes 3162112 | tf_op jit(solution)/shard_map/dot_general | solution.py:79
  (59 shorter events, 7.7 us)
Async XLA Ops:
  7.2 20.1 %copy-start = (bf16[128,2048]{1,0:T(8,128)(2,1)S(1)}, bf16[128,2048]{1,0:T(8,128)(2,1)}, u32[]{:S(2)}) copy-start(bf16[128,2048]{1,0:T(8,128)(2,1)} %param.12) | copy-start | bytes 1572868
  7.2 3.9 %copy-start.5 = (bf16[128,256]{1,0:T(8,128)(2,1)S(1)}, bf16[128,256]{1,0:T(8,128)(2,1)}, u32[]{:S(2)}) copy-start(bf16[128,256]{1,0:T(8,128)(2,1)} %param.14) | copy-start | bytes 196612
  7.2 107.7 %reduce-scatter.2.cloned.1.call-start = ((), (), s32[]{:S(2)}) async-start(), calls=%async_computation.6 | async-start | bytes 2621440 | tf_op jit(solution)/shard_map/reduce_scatter | solution.py:85
  7.2 3.9 %copy-start.3 = (bf16[8192,256]{1,0:T(8,128)(2,1)S(1)}, bf16[8192,256]{1,0:T(8,128)(2,1)}, u32[]{:S(2)}) copy-start(bf16[8192,256]{1,0:T(8,128)(2,1)} %param.16) | copy-start | bytes 12582916
  14.0 0.7 copy-start.7
  14.0 0.7 copy-start.1
  14.0 9.4 %copy-start.6 = (s32[1,16]{1,0:T(1,128)S(1)}, s32[1,16]{1,0:T(1,128)}, u32[]{:S(2)}) copy-start(s32[1,16]{1,0:T(1,128)} %param.21) | copy-start | bytes 196
  14.7 12.4 %copy-start.4 = (bf16[128,256]{1,0:T(8,128)(2,1)S(1)}, bf16[128,256]{1,0:T(8,128)(2,1)}, u32[]{:S(2)}) copy-start(bf16[128,256]{1,0:T(8,128)(2,1)} %param.13) | copy-start | bytes 196612
  16.4 38.9 %all-to-all-start = ((bf16[4,4,1]{1,2,0:T(2,128)(2,1)}), bf16[4,4,1]{1,2,0:T(2,128)(2,1)S(1)}, u32[]{:S(2)}, u32[]{:S(2)}) async-start(bf16[4,4,1]{1,2,0:T(2,128)(2,1)} %all_to_all.52), calls=%async_computation.1 | async-start | bytes 4096 | tf_op jit(solution)/shard_map/all_to_all | solution.py:145
  55.3 8.3 %all-to-all-start.3 = ((bf16[4,4,4096]{2,1,0:T(4,128)(2,1)}), bf16[4,4,4096]{2,1,0:T(4,128)(2,1)S(1)}, u32[]{:S(2)}, u32[]{:S(2)}) async-start(bf16[4,4,4096]{2,1,0:T(4,128)(2,1)} %all_to_all.46), calls=%async_computation.4 | async-start | bytes 262144 | tf_op jit(solution)/shard_map/all_to_all | solution.py:131
  63.6 9.3 %all-to-all-start.4 = ((bf16[4,4,4096]{2,1,0:T(4,128)(2,1)}), bf16[4,4,4096]{2,1,0:T(4,128)(2,1)S(1)}, u32[]{:S(2)}, u32[]{:S(2)}) async-start(bf16[4,4,4096]{2,1,0:T(4,128)(2,1)} %all_to_all.49), calls=%async_computation.5 | async-start | bytes 262144 | tf_op jit(solution)/shard_map/all_to_all | solution.py:138
  72.8 18.8 %all-to-all-start.1 = ((bf16[4,4,32768]{2,1,0:T(4,128)(2,1)}), bf16[4,4,32768]{2,1,0:T(4,128)(2,1)}, u32[]{:S(2)}, u32[]{:S(2)}) async-start(bf16[4,4,32768]{2,1,0:T(4,128)(2,1)} %all_to_all.40), calls=%async_computation.2 | async-start | bytes 2097152 | tf_op jit(solution)/shard_map/all_to_all | solution.py:117
  91.6 18.0 %all-to-all-start.2 = ((bf16[4,4,32768]{2,1,0:T(4,128)(2,1)}), bf16[4,4,32768]{2,1,0:T(4,128)(2,1)S(1)}, u32[]{:S(2)}, u32[]{:S(2)}) async-start(bf16[4,4,32768]{2,1,0:T(4,128)(2,1)} %all_to_all.43), calls=%async_computation.3 | async-start | bytes 2097152 | tf_op jit(solution)/shard_map/all_to_all | solution.py:124
  112.3 2.6 %copy-start.2 = (f32[128,2048]{1,0:T(8,128)S(1)}, f32[128,2048]{1,0:T(8,128)}, u32[]{:S(2)}) copy-start(f32[128,2048]{1,0:T(8,128)} %convolution_bitcast_fusion) | copy-start | bytes 3145732
Sparse Core Ops, SparseCore 0:
  14.2 47.0 reduce-scatter.1
where the time goes:
time: 125 us; the launch traced here: 124 us
  local copies, waits for them, and re-layouts  32.5 us (26%)
  matrix products  26.9 us (22%)
  blocking collectives  20.9 us (17%)
  starting transfers between devices  19.2 us (15%)
  between operations  14.3 us (11%)
  waiting for transfers between devices  9.58 us (8%)
    psum x1, blocking collectives, local(): lax.psum(back_value.astype(jnp.bfloat16), 'tensor').astype(jnp.float32)  20.9 us
    dot_general x9, matrix products, exact_dot(): return jnp.dot(former, latter, precision=lax.Precision.HIGHEST)  11.6 us
    dot_general x6, matrix products, contract_cols(): lax.dot_general(former, latter, (((1,), (1,)), ((), ())), preferred_eleme...  7.94 us
    unnamed x20, local copies, waits for them, and re-layouts  7.3 us
    all_to_all x1, waiting for transfers between devices, local(): lax.all_to_all(exact_dot(placing, value_down_partial).astype(jnp.bfloat16...  5.81 us
    all_to_all x2, local copies, waits for them, and re-layouts, local(): lax.all_to_all(exact_dot(placing, key_down_partial).astype(jnp.bfloat16),...  4.4 us
    all_to_all x1, starting transfers between devices, local(): lax.all_to_all(exact_dot(placing, key_down_partial).astype(jnp.bfloat16),...  4.26 us
    all_to_all x1, starting transfers between devices, local(): lax.all_to_all(local_target.astype(jnp.bfloat16), 'dp', split_axis=0, con...  4.21 us
  transfers between devices with their start and end apart: 6, of which 3 were waited for; matrix products, arithmetic and copies ran while one was open for 33% of the time, Pallas kernels for 0%

commit v1 on v0

v1 whole, which is shorter than its diff:
```python
import functools

import jax
import jax.numpy as jnp
from jax import lax
from jax.experimental import pallas as pl
from jax.experimental.pallas import tpu as pltpu
from jax.sharding import PartitionSpec as P

ADAPTER_SCALE = 2.0
LOSS_UNSCALE = 0.125
VMEM_BYTES = 48 * 1024 * 1024
SLOT_ROWS = 16

f32 = jnp.float32
bf16 = jnp.bfloat16


def dot_nt(former, latter):
    return lax.dot_general(former, latter, (((1,), (1,)), ((), ())), preferred_element_type=f32)


def dot_nn(former, latter):
    return lax.dot_general(former, latter, (((1,), (0,)), ((), ())), preferred_element_type=f32)


def dot_tn(former, latter):
    return lax.dot_general(former, latter, (((0,), (0,)), ((), ())), preferred_element_type=f32)


def params():
    return pltpu.CompilerParams(vmem_limit_bytes=VMEM_BYTES)


def frozen_kernel(block_ref, gk_ref, gv_ref, wk_ref, wv_ref, out_ref):
    del block_ref
    value = dot_nt(gk_ref[...], wk_ref[...]) + dot_nt(gv_ref[...], wv_ref[...])
    out_ref[...] = value.astype(out_ref.dtype)


def frozen_block(block, gk, gv, wk, wv, width, dtype, steps=4):
    rows, feats = gk.shape
    part = width // steps
    return pl.pallas_call(
        frozen_kernel,
        grid_spec=pltpu.PrefetchScalarGridSpec(
            num_scalar_prefetch=1,
            grid=(steps,),
            in_specs=[
                pl.BlockSpec((rows, feats), lambda i, b: (0, 0)),
                pl.BlockSpec((rows, feats), lambda i, b: (0, 0)),
                pl.BlockSpec((part, feats), lambda i, b: (b[0] * steps + i, 0)),
                pl.BlockSpec((part, feats), lambda i, b: (b[0] * steps + i, 0)),
            ],
            out_specs=pl.BlockSpec((rows, part), lambda i, b: (0, i)),
        ),
        out_shape=jax.ShapeDtypeStruct((rows, width), dtype),
        compiler_params=params(),
        cost_estimate=pl.CostEstimate(
            flops=4 * rows * feats * width, bytes_accessed=4 * feats * width, transcendentals=0
        ),
        name="frozen_block",
    )(block, gk, gv, wk, wv)


def segment_masks(len_ref, rows, segments, rank):
    shape = (segments * rank, rows)
    row = lax.broadcasted_iota(jnp.int32, shape, 1)
    seg = lax.broadcasted_iota(jnp.int32, shape, 0) // rank
    start = jnp.zeros(shape, jnp.int32)
    end = jnp.zeros(shape, jnp.int32)
    total = jnp.int32(0)
    for k in range(segments):
        begin = total
        total = total + len_ref[0, k]
        start = jnp.where(seg == k, begin, start)
        end = jnp.where(seg == k, total, end)
    return (row >= start) & (row < end)


def lowrank_kernel(
    len_ref, tenant_ref, slot_ref, tok_hbm, gk_hbm, gv_hbm, kd_hbm, vd_hbm, ku_hbm, vu_hbm,
    out_ref, tok, gk, gv, down, up, sems,
):
    segments = tenant_ref.shape[1]
    rank = kd_hbm.shape[1]
    rows = tok.shape[0]
    half = segments * rank
    copies = [
        pltpu.make_async_copy(tok_hbm, tok, sems.at[0, 0]),
        pltpu.make_async_copy(gk_hbm, gk, sems.at[0, 1]),
        pltpu.make_async_copy(gv_hbm, gv, sems.at[0, 2]),
    ]
    for k in range(segments):
        tenant = tenant_ref[0, k]
        at = pl.ds(k * rank, rank)
        after = pl.ds(half + k * rank, rank)
        copies.append(pltpu.make_async_copy(kd_hbm.at[tenant], down.at[at], sems.at[1, k]))
        copies.append(pltpu.make_async_copy(vd_hbm.at[tenant], down.at[after], sems.at[2, k]))
        copies.append(pltpu.make_async_copy(ku_hbm.at[tenant], up.at[at], sems.at[3, k]))
        copies.append(pltpu.make_async_copy(vu_hbm.at[tenant], up.at[after], sems.at[4, k]))
    for copy in copies:
        copy.start()
    mask = segment_masks(len_ref, rows, segments, rank)
    slot_of = jnp.zeros((SLOT_ROWS, rows), f32)
    position = lax.broadcasted_iota(jnp.int32, (SLOT_ROWS, rows), 1)
    total = jnp.int32(0)
    for k in range(segments):
        begin = total
        total = total + len_ref[0, k]
        slot = slot_ref[tenant_ref[0, k]].astype(f32)
        slot_of = jnp.where((position >= begin) & (position < total), slot, slot_of)
    out_ref[4 * rank :, :] = slot_of.astype(bf16)
    for copy in copies:
        copy.wait()

    def fold(values):
        kept = jnp.where(mask, values, 0.0)
        return jnp.sum(kept.reshape(segments, rank, rows), axis=0).astype(bf16)

    out_ref[0:rank, :] = fold(dot_nt(down[:half], tok[...]))
    out_ref[rank : 2 * rank, :] = fold(dot_nt(down[half:], tok[...]))
    out_ref[2 * rank : 3 * rank, :] = fold(dot_nt(up[:half], gk[...]))
    out_ref[3 * rank : 4 * rank, :] = fold(dot_nt(up[half:], gv[...]))


def lowrank(tokens, gk, gv, kd, vd, ku, vu, lengths, tenants, slots):
    rows, width = tokens.shape
    feats = gk.shape[1]
    segments = tenants.shape[1]
    rank = kd.shape[1]
    both = 2 * segments * rank
    smem = pl.BlockSpec(memory_space=pltpu.SMEM)
    anywhere = pl.BlockSpec(memory_space=pl.ANY)
    return pl.pallas_call(
        lowrank_kernel,
        in_specs=[smem] * 3 + [anywhere] * 7,
        out_specs=pl.BlockSpec(memory_space=pltpu.VMEM),
        out_shape=jax.ShapeDtypeStruct((4 * rank + SLOT_ROWS, rows), bf16),
        scratch_shapes=[
            pltpu.VMEM((rows, width), bf16),
            pltpu.VMEM((rows, feats), bf16),
            pltpu.VMEM((rows, feats), bf16),
            pltpu.VMEM((both, width), bf16),
            pltpu.VMEM((both, feats), bf16),
            pltpu.SemaphoreType.DMA((5, segments)),
        ],
        compiler_params=params(),
        cost_estimate=pl.CostEstimate(
            flops=2 * rows * both * (width + feats),
            bytes_accessed=2 * (rows + both) * (width + feats),
            transcendentals=0,
        ),
        name="lowrank",
    )(lengths, tenants, slots, tokens, gk, gv, kd, vd, ku, vu)


def own_kernel(
    len_ref, tenant_ref, z_ref, gk_ref, gv_ref, sums_ref, wk_hbm, wv_hbm, kd_hbm, vd_hbm,
    out_ref, wk, wv, down, sems,
):
    segments = tenant_ref.shape[1]
    rank = kd_hbm.shape[1]
    rows, width = out_ref.shape
    half = segments * rank
    block = pl.ds(pl.multiple_of(z_ref[0] * width, width), width)
    copies = [
        pltpu.make_async_copy(wk_hbm.at[block], wk, sems.at[0, 0]),
        pltpu.make_async_copy(wv_hbm.at[block], wv, sems.at[0, 1]),
    ]
    for k in range(segments):
        tenant = tenant_ref[0, k]
        at = pl.ds(k * rank, rank)
        after = pl.ds(half + k * rank, rank)
        copies.append(pltpu.make_async_copy(kd_hbm.at[tenant], down.at[at], sems.at[1, k]))
        copies.append(pltpu.make_async_copy(vd_hbm.at[tenant], down.at[after], sems.at[2, k]))
    for copy in copies:
        copy.start()
    mask = segment_masks(len_ref, rows, segments, rank)

    def spread(first):
        values = sums_ref[first : first + rank, :].astype(f32)
        tiled = jnp.concatenate([values] * segments, axis=0)
        return jnp.where(mask, ADAPTER_SCALE * tiled, 0.0).astype(bf16)

    back = jnp.concatenate([spread(2 * rank), spread(3 * rank)], axis=0)
    for copy in copies:
        copy.wait()
    out_ref[...] = (
        dot_nt(gk_ref[...], wk[...]) + dot_nt(gv_ref[...], wv[...]) + dot_tn(back, down[...])
    )


def own_columns(z, gk, gv, sums, wk, wv, kd, vd, lengths, tenants):
    rows, feats = gk.shape
    width = kd.shape[2]
    segments = tenants.shape[1]
    rank = kd.shape[1]
    both = 2 * segments * rank
    smem = pl.BlockSpec(memory_space=pltpu.SMEM)
    vmem = pl.BlockSpec(memory_space=pltpu.VMEM)
    anywhere = pl.BlockSpec(memory_space=pl.ANY)
    return pl.pallas_call(
        own_kernel,
        in_specs=[smem] * 3 + [vmem] * 3 + [anywhere] * 4,
        out_specs=vmem,
        out_shape=jax.ShapeDtypeStruct((rows, width), f32),
        scratch_shapes=[
            pltpu.VMEM((width, feats), bf16),
            pltpu.VMEM((width, feats), bf16),
            pltpu.VMEM((both, width), bf16),
            pltpu.SemaphoreType.DMA((3, segments)),
        ],
        compiler_params=params(),
        cost_estimate=pl.CostEstimate(
            flops=2 * rows * width * (2 * feats + both),
            bytes_accessed=2 * width * (2 * feats + both + 2 * rows),
            transcendentals=0,
        ),
        name="own_columns",
    )(lengths, tenants, z, gk, gv, sums, wk, wv, kd, vd)


def grads_kernel(count, rank, per_owner, first_ref, *refs):
    sums = refs[:count]
    chunks = refs[count : 2 * count]
    ends = refs[2 * count : 3 * count]
    ka_ref, va_ref, kb_ref, vb_ref, spread_ref = refs[3 * count :]
    size = per_owner * rank
    scale = ADAPTER_SCALE * LOSS_UNSCALE

    @pl.when(pl.program_id(0) == 0)
    def _():
        feats = kb_ref.shape[2]
        rows = sums[0].shape[1]
        wanted = lax.broadcasted_iota(jnp.int32, (size, rows), 0) // rank + first_ref[0]
        b_key = jnp.zeros((size, feats), f32)
        b_value = jnp.zeros((size, feats), f32)
        for n in range(count):
            slot = sums[n][4 * rank : 4 * rank + 1, :].astype(f32).astype(jnp.int32)
            mask = wanted == slot

            def spread(index):
                values = sums[n][index * rank : (index + 1) * rank, :].astype(f32)
                tiled = jnp.concatenate([values] * per_owner, axis=0)
                return jnp.where(mask, tiled, 0.0).astype(bf16)

            columns = slice(n * rows, (n + 1) * rows)
            spread_ref[0:size, columns] = spread(2)
            spread_ref[size:, columns] = spread(3)
            b_key += dot_nn(spread(0), ends[n][:, :feats])
            b_value += dot_nn(spread(1), ends[n][:, feats:])
        kb_ref[...] = (scale * b_key).reshape(kb_ref.shape)
        vb_ref[...] = (scale * b_value).reshape(vb_ref.shape)

    tokens = jnp.concatenate([chunk[...] for chunk in chunks], axis=0)
    product = scale * dot_nn(spread_ref[...], tokens)
    ka_ref[...] = product[:size].reshape(ka_ref.shape)
    va_ref[...] = product[size:].reshape(va_ref.shape)


def adapter_grads(first, sums, sent, rank, per_owner, width, feats):
    count = len(sums)
    rows = sent[0].shape[0]
    chunk = 2 * feats
    steps = width // chunk
    a_spec = pl.BlockSpec((per_owner, rank, chunk), lambda i: (0, 0, i))
    b_spec = pl.BlockSpec((per_owner, rank, feats), lambda i: (0, 0, 0))
    return pl.pallas_call(
        functools.partial(grads_kernel, count, rank, per_owner),
        grid=(steps,),
        in_specs=[pl.BlockSpec(memory_space=pltpu.SMEM)]
        + [pl.BlockSpec(sums[0].shape, lambda i: (0, 0))] * count
        + [pl.BlockSpec((rows, chunk), lambda i: (0, i))] * count
        + [pl.BlockSpec((rows, chunk), lambda i: (0, steps))] * count,
        out_specs=[a_spec, a_spec, b_spec, b_spec],
        out_shape=[
            jax.ShapeDtypeStruct((per_owner, rank, width), f32),
            jax.ShapeDtypeStruct((per_owner, rank, width), f32),
            jax.ShapeDtypeStruct((per_owner, rank, feats), f32),
            jax.ShapeDtypeStruct((per_owner, rank, feats), f32),
        ],
        scratch_shapes=[pltpu.VMEM((2 * per_owner * rank, count * rows), bf16)],
        compiler_params=params(),
        cost_estimate=pl.CostEstimate(
            flops=4 * per_owner * rank * count * rows * (width + feats),
            bytes_accessed=8 * per_owner * rank * (width + feats) + 2 * count * rows * width,
            transcendentals=0,
        ),
        name="adapter_grads",
    )(first, *sums, *sent, *sent)


def swap(values, axis, bit, size):
    return lax.ppermute(values, axis, [(i, i ^ bit) for i in range(size)])


def local(
    tokens, gk, gv, wk, wv, kd, vd, ku, vu, segment_length, segment_tenant, adapter_output_slot
):
    rows, width = tokens.shape
    feats = gk.shape[1]
    adapters, rank, _ = kd.shape
    n_tensor = lax.axis_size("tensor")
    n_dp = lax.axis_size("dp")
    per_owner = adapters // n_dp
    z = lax.axis_index("tensor")
    first = (lax.axis_index("dp") * per_owner).astype(jnp.int32).reshape(1)
    z_index = z.astype(jnp.int32).reshape(1)

    sent = jnp.concatenate([tokens, gk, gv], axis=1)

    if n_tensor == 4:
        odd = z_index % 2
        edge = (z_index == 0) | (z_index == 3)
        x0 = frozen_block(jnp.where(odd == 1, 0, 3), gk, gv, wk, wv, width, bf16)
        r1 = swap(x0, "tensor", 1, 4)
        x1 = frozen_block(jnp.where(odd == 1, 2, 1), gk, gv, wk, wv, width, bf16)
        r2 = lax.ppermute(x1, "tensor", [(1, 2), (2, 1)])
        r4 = lax.ppermute(x1, "tensor", [(0, 1), (3, 2)])
        x2 = frozen_block(z_index ^ 2, gk, gv, wk, wv, width, f32)
        x2 = jnp.where(edge[0], x2, x2 + r1.astype(f32)).astype(bf16)
        r3 = swap(x2, "tensor", 2, 4)

    part = lowrank(
        tokens, gk, gv, kd, vd, ku, vu, segment_length, segment_tenant, adapter_output_slot
    )
    products, slot_rows = part[: 4 * rank], part[4 * rank :]
    if n_tensor == 4:
        total = products.astype(f32)
        for bit in (1, 2, 3):
            total = total + swap(products, "tensor", bit, 4).astype(f32)
    else:
        total = lax.psum(products.astype(f32), "tensor")
    sums = jnp.concatenate([total.astype(bf16), slot_rows], axis=0)

    if n_dp == 4:
        across = swap(sent, "dp", 2, 4)
        all_sent = [sent, across, swap(sent, "dp", 1, 4), swap(across, "dp", 1, 4)]
        across = swap(sums, "dp", 2, 4)
        all_sums = [sums, across, swap(sums, "dp", 1, 4), swap(across, "dp", 1, 4)]
    else:
        gathered = lax.all_gather(sent, "dp")
        all_sent = [gathered[i] for i in range(n_dp)]
        gathered = lax.all_gather(sums, "dp")
        all_sums = [gathered[i] for i in range(n_dp)]

    own = own_columns(
        z_index, gk, gv, sums, wk, wv, kd, vd, segment_length, segment_tenant
    )
    if n_tensor == 4:
        near = r2.astype(f32) + r4.astype(f32)
        own = own + jnp.where(edge[0], r1.astype(f32), near)
        input_gradient = (own + r3.astype(f32)).astype(bf16)
    else:
        blocks = [
            frozen_block(jnp.full((1,), b, jnp.int32), gk, gv, wk, wv, width, bf16)
            for b in range(n_tensor)
        ]
        mine = lax.psum_scatter(
            jnp.concatenate(blocks, axis=1), "tensor", scatter_dimension=1, tiled=True
        )
        term = frozen_block(z_index, gk, gv, wk, wv, width, f32)
        input_gradient = (own - term + mine.astype(f32)).astype(bf16)

    grads = adapter_grads(first, all_sums, all_sent, rank, per_owner, width, feats)
    return (input_gradient, *grads)


def solution(mesh):
    placed = (
        P(("group", "dp"), "tensor"),
        P(("group", "dp"), "tensor"),
        P(("group", "dp"), "tensor"),
        P(None, "tensor"),
        P(None, "tensor"),
        P(None, None, "tensor"),
        P(None, None, "tensor"),
        P(None, None, "tensor"),
        P(None, None, "tensor"),
        P(("group", "dp"), None),
        P(("group", "dp"), None),
        P("group"),
    )
    return jax.shard_map(
        local,
        mesh=mesh,
        in_specs=placed,
        out_specs=(
            P(("group", "dp"), "tensor"),
            P(("group", "dp"), None, "tensor"),
            P(("group", "dp"), None, "tensor"),
            P(("group", "dp"), None, "tensor"),
            P(("group", "dp"), None, "tensor"),
        ),
        check_vma=False,
    )
```

time: 125 us -> 81.6 us (0.65)
  matrix products: 26.9 us -> 0 us
  local copies, waits for them, and re-layouts: 32.5 us -> 6.16 us
  Pallas kernels: 0 us -> 22 us
  waiting for transfers between devices: 9.58 us -> 30.7 us
  blocking collectives: 20.9 us -> 0 us
  between operations: 14.3 us -> 0.88 us
  other arithmetic: 0.58 us -> 3.5 us
  starting transfers between devices: 19.2 us -> 17.8 us
    ppermute x0 -> x13, waiting for transfers between devices: none -> 30.7 us  [the longest x11 30.7 us: swap(): return lax.ppermute(values, axis, [(i, i ^ bit) for i in range(size)])]
    dot_general x21 -> x0, matrix products: 26.9 us -> none  [the longest x9 11.6 us: exact_dot(): return jnp.dot(former, latter, precision=lax.Precision.HIGHEST)]
    pallas_call x0 -> x6, Pallas kernels: none -> 22 us  [the longest x3 9.25 us: frozen_block(): pl.pallas_call(frozen_kernel, grid_spec=pltpu.PrefetchScalarGridSpec(num_...]
    psum x1 -> x0, blocking collectives: 20.9 us -> none  [local(): lax.psum(back_value.astype(jnp.bfloat16), 'tensor').astype(jnp.float32)]
    all_to_all x5 -> x0, starting transfers between devices: 19.2 us -> none  [the longest x1 4.26 us: local(): lax.all_to_all(exact_dot(placing, key_down_partial).astype(jnp.bfloat16),...]
    ppermute x0 -> x13, starting transfers between devices: none -> 17.8 us  [the longest x11 13.6 us: swap(): return lax.ppermute(values, axis, [(i, i ^ bit) for i in range(size)])]
    all_to_all x9 -> x0, local copies, waits for them, and re-layouts: 9.93 us -> none  [the longest x2 4.4 us: local(): lax.all_to_all(exact_dot(placing, key_down_partial).astype(jnp.bfloat16),...]
    all_to_all x5 -> x0, waiting for transfers between devices: 9.56 us -> none  [the longest x1 5.81 us: local(): lax.all_to_all(exact_dot(placing, value_down_partial).astype(jnp.bfloat16...]
  transfers between devices with their start and end apart: 6 -> 13, of which waited for: 3 -> 4; matrix products, arithmetic and copies ran while one was open for 33% -> 4% of each run, Pallas kernels for 0% -> 19%
where the time goes in v1:
time: 81.6 us; the launch traced here: 81 us
  waiting for transfers between devices  30.7 us (38%)
  Pallas kernels  22 us (27%)
  starting transfers between devices  17.8 us (22%)
  local copies, waits for them, and re-layouts  6.16 us (8%)
  other arithmetic  3.5 us (4%)
  between operations  0.88 us (1%)
    ppermute x11, waiting for transfers between devices, swap(): return lax.ppermute(values, axis, [(i, i ^ bit) for i in range(size)])  30.7 us
    ppermute x11, starting transfers between devices, swap(): return lax.ppermute(values, axis, [(i, i ^ bit) for i in range(size)])  13.6 us
    pallas_call x3, Pallas kernels, frozen_block(): pl.pallas_call(frozen_kernel, grid_spec=pltpu.PrefetchScalarGridSpec(num_...  9.25 us
    unnamed x32, local copies, waits for them, and re-layouts  6.14 us
    pallas_call x1, Pallas kernels, lowrank(): pl.pallas_call(lowrank_kernel, in_specs=[smem] * 3 + [anywhere] * 7, out_...  4.88 us
    pallas_call x1, Pallas kernels, adapter_grads(): pl.pallas_call(functools.partial(grads_kernel, count, rank, per_owner), g...  3.99 us
    pallas_call x1, Pallas kernels, own_columns(): pl.pallas_call(own_kernel, in_specs=[smem] * 3 + [vmem] * 3 + [anywhere]...  3.91 us
    ppermute x1, starting transfers between devices, local(): r4 = lax.ppermute(x1, 'tensor', [(0, 1), (3, 2)])  2.77 us
  transfers between devices with their start and end apart: 13, of which 4 were waited for; matrix products, arithmetic and copies ran while one was open for 4% of the time, Pallas kernels for 19%

profile of v1, /device:TPU:0, one launch (start us, length us, event | category | flops | bytes accessed | tf_op | source)
XLA Modules:
  0.0 81.0 jit_solution(8611331894551246820)
XLA Ops:
  0.6 0.0 copy-start
  0.7 2.2 %copy-done = bf16[8192,256]{1,0:T(8,128)(2,1)S(1)} copy-done((bf16[8192,256]{1,0:T(8,128)(2,1)S(1)}, bf16[8192,256]{1,0:T(8,128)(2,1)}, u32[]{:S(2)}) %copy-start) | copy-done | bytes 4194328
  2.8 0.8 %copy-done.3 = bf16[128,256]{1,0:T(8,128)(2,1)S(1)} copy-done((bf16[128,256]{1,0:T(8,128)(2,1)S(1)}, bf16[128,256]{1,0:T(8,128)(2,1)}, u32[]{:S(2)}) %copy-start.3) | copy-done | bytes 65560
  3.7 0.8 %copy-done.5 = bf16[128,256]{1,0:T(8,128)(2,1)S(1)} copy-done((bf16[128,256]{1,0:T(8,128)(2,1)S(1)}, bf16[128,256]{1,0:T(8,128)(2,1)}, u32[]{:S(2)}) %copy-start.5) | copy-done | bytes 65560
  4.5 2.9 %frozen_block.3 = bf16[128,2048]{1,0:T(8,128)(2,1)S(1)} custom-call(s32[1]{0:T(128)S(6)} %select_n.28.block_ref, bf16[128,256]{1,0:T(8,128)(2,1)S(1)} %copy-done.3, bf16[128,256]{1,0:T(8,128)(2,1)S(1)} %copy-done.5, bf16[8192,256]{1,0:T(8,128)(2,1)S(1)} %copy-done, bf16[8192,256]{1,0:T(8,128)(2,1)} %wv_ref.5), custom_call_target="tpu_custom_call" | custom-call | flops 268435456 | bytes 2097152 | tf_op jit(solution)/shard_map/frozen_block/pallas_call | solution.py:44
  7.4 3.1 %collective-permute-start.3 = (bf16[128,2048]{1,0:T(8,128)(2,1)S(1)}, bf16[128,2048]{1,0:T(8,128)(2,1)S(1)}, u32[]{:S(2)}, u32[]{:S(2)}) collective-permute-start(bf16[128,2048]{1,0:T(8,128)(2,1)S(1)} %frozen_block.3), channel_id=1, source_target_pairs={{0,4},{4,0},{8,12},{12,8},{1,5},{5,1},{9,13},{13,9},{2,6},{6,2},{1... | collective-permute-start | bytes 1572872 | tf_op jit(solution)/shard_map/ppermute | solution.py:295
  10.5 3.0 %frozen_block.4 = bf16[128,2048]{1,0:T(8,128)(2,1)S(1)} custom-call(s32[1]{0:T(128)S(6)} %select_n.29.block_ref, bf16[128,256]{1,0:T(8,128)(2,1)S(1)} %copy-done.3, bf16[128,256]{1,0:T(8,128)(2,1)S(1)} %copy-done.5, bf16[8192,256]{1,0:T(8,128)(2,1)S(1)} %copy-done, bf16[8192,256]{1,0:T(8,128)(2,1)} %wv_ref.5), custom_call_target="tpu_custom_call" | custom-call | flops 268435456 | bytes 2097152 | tf_op jit(solution)/shard_map/frozen_block/pallas_call | solution.py:44
  13.5 2.8 %collective-permute-start.5 = (bf16[128,2048]{1,0:T(8,128)(2,1)S(1)}, bf16[128,2048]{1,0:T(8,128)(2,1)}, u32[]{:S(2)}, u32[]{:S(2)}) collective-permute-start(bf16[128,2048]{1,0:T(8,128)(2,1)S(1)} %frozen_block.4), channel_id=1, source_target_pairs={{0,4},{12,8},{1,5},{13,9},{2,6},{14,10},{3,7},{15,11},{16,20},{28,... | collective-permute-start | bytes 1572872 | tf_op jit(solution)/shard_map/ppermute | solution.py:320
  16.3 1.4 %collective-permute-start.4 = (bf16[128,2048]{1,0:T(8,128)(2,1)S(1)}, bf16[128,2048]{1,0:T(8,128)(2,1)}, u32[]{:S(2)}, u32[]{:S(2)}) collective-permute-start(bf16[128,2048]{1,0:T(8,128)(2,1)S(1)} %frozen_block.4), channel_id=1, source_target_pairs={{4,8},{8,4},{5,9},{9,5},{6,10},{10,6},{7,11},{11,7},{20,24},{24,20... | collective-permute-start | bytes 1572872 | tf_op jit(solution)/shard_map/ppermute | solution.py:319
  17.8 2.0 %collective-permute-start.10 = (bf16[128,2560]{1,0:T(8,128)(2,1)S(1)}, bf16[128,2560]{1,0:T(8,128)(2,1)S(1)}, u32[]{:S(2)}, u32[]{:S(2)}) collective-permute-start(bf16[128,2560]{1,0:T(8,128)(2,1)S(1)} %constant_dynamic-update-slice_fusion.refs_4_.refs_8_), channel_id=1, source_target_pairs={{0,2},{1,3},{2,0},{3,1},{4,6},{5,7},{6,4},{7,5},{8,10},{9,11},{10,... | collective-permute-start | bytes 1966088 | tf_op jit(solution)/shard_map/ppermute | solution.py:295
  19.8 0.0 copy-start.9
  19.8 0.0 copy-start.10
  19.8 0.0 copy-start.11
  19.8 0.0 copy-start.12
  19.8 3.4 %frozen_block.5 = f32[128,2048]{1,0:T(8,128)S(1)} custom-call(s32[1]{0:T(128)S(6)} %xor.3.block_ref, bf16[128,256]{1,0:T(8,128)(2,1)S(1)} %copy-done.3, bf16[128,256]{1,0:T(8,128)(2,1)S(1)} %copy-done.5, bf16[8192,256]{1,0:T(8,128)(2,1)S(1)} %copy-done, bf16[8192,256]{1,0:T(8,128)(2,1)} %wv_ref.5), custom_call_target="tpu_custom_call" | custom-call | flops 268435456 | bytes 2097152 | tf_op jit(solution)/shard_map/frozen_block/pallas_call | solution.py:44
  23.2 1.0 %fusion.3 = bf16[128,2048]{1,0:T(8,128)(2,1)} fusion(f32[128,2048]{1,0:T(8,128)S(1)} %frozen_block.5, bf16[128,2048]{1,0:T(8,128)(2,1)S(1)} %collective-permute-done.3, pred[]{:T(512)} %bitcast.1), kind=kLoop, calls=%fused_computation.5 | loop fusion | flops 1048576 | bytes 2097153 | tf_op jit(solution)/shard_map/convert_element_type | solution.py:322
  24.2 3.1 %collective-permute-start.6 = (bf16[128,2048]{1,0:T(8,128)(2,1)}, bf16[128,2048]{1,0:T(8,128)(2,1)}, u32[]{:S(2)}, u32[]{:S(2)}) collective-permute-start(bf16[128,2048]{1,0:T(8,128)(2,1)} %fusion.3), channel_id=1, source_target_pairs={{0,8},{4,12},{8,0},{12,4},{1,9},{5,13},{9,1},{13,5},{2,10},{6,14},... | collective-permute-start | bytes 1572872 | tf_op jit(solution)/shard_map/ppermute | solution.py:295
  27.4 4.9 %lowrank.1 = bf16[80,128]{1,0:T(8,128)(2,1)S(1)} custom-call(s32[1,16]{1,0:T(1,128)S(1)} %copy-done.10, s32[1,16]{1,0:T(1,128)S(1)} %copy-done.11, s32[64]{0:T(128)S(1)} %copy-done.12, bf16[128,2048]{1,0:T(8,128)(2,1)S(1)} %copy-done.7, bf16[128,256]{1,0:T(8,128)(2,1)S(1)} %copy-done.4, bf16[128,256]{1,0:T(8,128)(2,1)S(1)} %copy-done.6, ...), custom_call_target="tpu_custom_call" | custom-call | flops 301989888 | bytes 2949120 | tf_op jit(solution)/shard_map/lowrank/pallas_call | solution.py:135
  32.3 0.1 collective-permute-start.1
  32.4 21.7 %collective-permute-done.1 = bf16[64,128]{1,0:T(8,128)(2,1)S(1)} collective-permute-done((bf16[64,128]{1,0:T(8,128)(2,1)S(1)}, bf16[64,128]{1,0:T(8,128)(2,1)S(1)}, u32[]{:S(2)}, u32[]{:S(2)}) %collective-permute-start.1) | collective-permute-done | bytes 16416 | tf_op jit(solution)/shard_map/ppermute | solution.py:295
  54.1 3.7 %collective-permute-done = bf16[64,128]{1,0:T(8,128)(2,1)S(1)} collective-permute-done((bf16[64,128]{1,0:T(8,128)(2,1)S(1)}, bf16[64,128]{1,0:T(8,128)(2,1)S(1)}, u32[]{:S(2)}, u32[]{:S(2)}) %collective-permute-start) | collective-permute-done | bytes 16416 | tf_op jit(solution)/shard_map/ppermute | solution.py:295
  57.8 2.6 %collective-permute-start.2 = (bf16[64,128]{1,0:T(8,128)(2,1)S(1)}, bf16[64,128]{1,0:T(8,128)(2,1)S(1)}, u32[]{:S(2)}, u32[]{:S(2)}) collective-permute-start(bf16[64,128]{1,0:T(8,128)(2,1)S(1)} %slice.8), channel_id=1, source_target_pairs={{0,12},{4,8},{8,4},{12,0},{1,13},{5,9},{9,5},{13,1},{2,14},{6,10},... | collective-permute-start | bytes 49160 | tf_op jit(solution)/shard_map/ppermute | solution.py:295
  60.5 2.9 %collective-permute-done.2 = bf16[64,128]{1,0:T(8,128)(2,1)S(1)} collective-permute-done((bf16[64,128]{1,0:T(8,128)(2,1)S(1)}, bf16[64,128]{1,0:T(8,128)(2,1)S(1)}, u32[]{:S(2)}, u32[]{:S(2)}) %collective-permute-start.2) | collective-permute-done | bytes 16416 | tf_op jit(solution)/shard_map/ppermute | solution.py:295
  63.4 1.6 %collective-permute-start.7 = (bf16[80,128]{1,0:T(8,128)(2,1)S(1)}, bf16[80,128]{1,0:T(8,128)(2,1)S(1)}, u32[]{:S(2)}, u32[]{:S(2)}) collective-permute-start(bf16[80,128]{1,0:T(8,128)(2,1)S(1)} %pad_maximum_fusion.sums_ref.refs_0_), channel_id=1, source_target_pairs={{0,2},{1,3},{2,0},{3,1},{4,6},{5,7},{6,4},{7,5},{8,10},{9,11},{10,... | collective-permute-start | bytes 61448 | tf_op jit(solution)/shard_map/ppermute | solution.py:295
  65.0 2.3 %collective-permute-done.7.refs_1_ = bf16[80,128]{1,0:T(8,128)(2,1)S(1)} collective-permute-done((bf16[80,128]{1,0:T(8,128)(2,1)S(1)}, bf16[80,128]{1,0:T(8,128)(2,1)S(1)}, u32[]{:S(2)}, u32[]{:S(2)}) %collective-permute-start.7) | collective-permute-done | bytes 20512 | tf_op jit(solution)/shard_map/ppermute | solution.py:295
  67.3 0.5 collective-permute-start.12
  67.8 2.2 %copy-done.1 = bf16[8192,256]{1,0:T(8,128)(2,1)S(1)} copy-done((bf16[8192,256]{1,0:T(8,128)(2,1)S(1)}, bf16[8192,256]{1,0:T(8,128)(2,1)}, u32[]{:S(2)}) %copy-start.1) | copy-done | bytes 4194328
  70.0 3.9 %own_columns.1 = f32[128,2048]{1,0:T(8,128)S(1)} custom-call(s32[1,16]{1,0:T(1,128)S(1)} %copy-done.10, s32[1,16]{1,0:T(1,128)S(1)} %copy-done.11, s32[1]{0:T(128)} %bitcast.z_ref, bf16[128,256]{1,0:T(8,128)(2,1)S(1)} %copy-done.4, bf16[128,256]{1,0:T(8,128)(2,1)S(1)} %copy-done.6, bf16[80,128]{1,0:T(8,128)(2,1)S(1)} %pad_maximum_fusion.sums_ref.refs_0_, ...), custom_call_target="tpu_custom_call" | custom-call | flops 536870912 | bytes 5242880 | tf_op jit(solution)/shard_map/own_columns/pallas_call | solution.py:203
  73.9 0.1 collective-permute-start.8
  74.0 0.5 collective-permute-start.9
  74.5 2.5 %fusion.2 = bf16[128,2048]{1,0:T(8,128)(2,1)} fusion(f32[128,2048]{1,0:T(8,128)S(1)} %own_columns.1, bf16[128,2048]{1,0:T(8,128)(2,1)S(1)} %copy-done.14, bf16[128,2048]{1,0:T(8,128)(2,1)} %collective-permute-done.6, bf16[128,2048]{1,0:T(8,128)(2,1)} %collective-permute-done.5, bf16[128,2048]{1,0:T(8,128)(2,1)} %collective-permute-done.4, pred[]{:T(512)} %bitcast.1), kind=kLoop, calls=%fused_computation.4 | loop fusion | flops 2359296 | bytes 3670017 | tf_op jit(solution)/shard_map/convert_element_type | solution.py:354
  77.0 4.0 %adapter_grads.1 = (f32[16,16,2048]{2,1,0:T(8,128)}, f32[16,16,2048]{2,1,0:T(8,128)}, f32[16,16,256]{2,1,0:T(8,128)}, f32[16,16,256]{2,1,0:T(8,128)}) custom-call(s32[1]{0:T(128)} %bitcast.2.first_ref, bf16[80,128]{1,0:T(8,128)(2,1)S(1)} %pad_maximum_fusion.sums_ref.refs_0_, bf16[80,128]{1,0:T(8,128)(2,1)S(1)} %collective-permute-done.7.refs_1_, ...), custom_call_target="tpu_custom_call" | custom-call | flops 1207959552 | bytes 6815744 | tf_op jit(solution)/shard_map/adapter_grads/pallas_call | solution.py:269
  (39 shorter events, 0.1 us)
Async XLA Ops:
  0.6 2.2 %copy-start = (bf16[8192,256]{1,0:T(8,128)(2,1)S(1)}, bf16[8192,256]{1,0:T(8,128)(2,1)}, u32[]{:S(2)}) copy-start(bf16[8192,256]{1,0:T(8,128)(2,1)} %wk_ref.5) | copy-start | bytes 12582916
  2.8 0.8 %copy-start.3 = (bf16[128,256]{1,0:T(8,128)(2,1)S(1)}, bf16[128,256]{1,0:T(8,128)(2,1)}, u32[]{:S(2)}) copy-start(bf16[128,256]{1,0:T(8,128)(2,1)} %gk_ref.7) | copy-start | bytes 196612
  3.7 0.8 %copy-start.5 = (bf16[128,256]{1,0:T(8,128)(2,1)S(1)}, bf16[128,256]{1,0:T(8,128)(2,1)}, u32[]{:S(2)}) copy-start(bf16[128,256]{1,0:T(8,128)(2,1)} %gv_ref.7) | copy-start | bytes 196612
  7.4 15.8 %collective-permute-start.3 = (bf16[128,2048]{1,0:T(8,128)(2,1)S(1)}, bf16[128,2048]{1,0:T(8,128)(2,1)S(1)}, u32[]{:S(2)}, u32[]{:S(2)}) collective-permute-start(bf16[128,2048]{1,0:T(8,128)(2,1)S(1)} %frozen_block.3), channel_id=1, source_target_pairs={{0,4},{4,0},{8,12},{12,8},{1,5},{5,1},{9,13},{13,9},{2,6},{6,2},{1... | collective-permute-start | bytes 1572872 | tf_op jit(solution)/shard_map/ppermute | solution.py:295
  10.5 7.2 %copy-start.7 = (bf16[128,2048]{1,0:T(8,128)(2,1)S(1)}, bf16[128,2048]{1,0:T(8,128)(2,1)}, u32[]{:S(2)}) copy-start(bf16[128,2048]{1,0:T(8,128)(2,1)} %tok_hbm.1) | copy-start | bytes 1572868
  13.5 60.4 %collective-permute-start.5 = (bf16[128,2048]{1,0:T(8,128)(2,1)S(1)}, bf16[128,2048]{1,0:T(8,128)(2,1)}, u32[]{:S(2)}, u32[]{:S(2)}) collective-permute-start(bf16[128,2048]{1,0:T(8,128)(2,1)S(1)} %frozen_block.4), channel_id=1, source_target_pairs={{0,4},{12,8},{1,5},{13,9},{2,6},{14,10},{3,7},{15,11},{16,20},{28,... | collective-permute-start | bytes 1572872 | tf_op jit(solution)/shard_map/ppermute | solution.py:320
  16.3 57.7 %collective-permute-start.4 = (bf16[128,2048]{1,0:T(8,128)(2,1)S(1)}, bf16[128,2048]{1,0:T(8,128)(2,1)}, u32[]{:S(2)}, u32[]{:S(2)}) collective-permute-start(bf16[128,2048]{1,0:T(8,128)(2,1)S(1)} %frozen_block.4), channel_id=1, source_target_pairs={{4,8},{8,4},{5,9},{9,5},{6,10},{10,6},{7,11},{11,7},{20,24},{24,20... | collective-permute-start | bytes 1572872 | tf_op jit(solution)/shard_map/ppermute | solution.py:319
  17.8 49.5 %collective-permute-start.10 = (bf16[128,2560]{1,0:T(8,128)(2,1)S(1)}, bf16[128,2560]{1,0:T(8,128)(2,1)S(1)}, u32[]{:S(2)}, u32[]{:S(2)}) collective-permute-start(bf16[128,2560]{1,0:T(8,128)(2,1)S(1)} %constant_dynamic-update-slice_fusion.refs_4_.refs_8_), channel_id=1, source_target_pairs={{0,2},{1,3},{2,0},{3,1},{4,6},{5,7},{6,4},{7,5},{8,10},{9,11},{10,... | collective-permute-start | bytes 1966088 | tf_op jit(solution)/shard_map/ppermute | solution.py:295
  19.8 7.6 %copy-start.2 = (bf16[64,16,2048]{2,1,0:T(8,128)(2,1)S(1)}, bf16[64,16,2048]{2,1,0:T(8,128)(2,1)}, u32[]{:S(2)}) copy-start(bf16[64,16,2048]{2,1,0:T(8,128)(2,1)} %kd_hbm.3) | copy-start | bytes 12582916
  19.8 7.6 %copy-start.4 = (bf16[128,256]{1,0:T(8,128)(2,1)S(1)}, bf16[128,256]{1,0:T(8,128)(2,1)}, u32[]{:S(2)}) copy-start(bf16[128,256]{1,0:T(8,128)(2,1)} %gk_ref.7) | copy-start | bytes 196612
  19.8 7.6 %copy-start.6 = (bf16[128,256]{1,0:T(8,128)(2,1)S(1)}, bf16[128,256]{1,0:T(8,128)(2,1)}, u32[]{:S(2)}) copy-start(bf16[128,256]{1,0:T(8,128)(2,1)} %gv_ref.7) | copy-start | bytes 196612
  19.8 7.6 %copy-start.8 = (bf16[64,16,256]{2,1,0:T(8,128)(2,1)S(1)}, bf16[64,16,256]{2,1,0:T(8,128)(2,1)}, u32[]{:S(2)}) copy-start(bf16[64,16,256]{2,1,0:T(8,128)(2,1)} %ku_hbm.1) | copy-start | bytes 1572868
  19.8 7.6 %copy-start.9 = (bf16[64,16,256]{2,1,0:T(8,128)(2,1)S(1)}, bf16[64,16,256]{2,1,0:T(8,128)(2,1)}, u32[]{:S(2)}) copy-start(bf16[64,16,256]{2,1,0:T(8,128)(2,1)} %vu_hbm.1) | copy-start | bytes 1572868
  19.8 7.6 %copy-start.10 = (s32[1,16]{1,0:T(1,128)S(1)}, s32[1,16]{1,0:T(1,128)}, u32[]{:S(2)}) copy-start(s32[1,16]{1,0:T(1,128)} %len_ref.3) | copy-start | bytes 196
  19.8 7.6 %copy-start.11 = (s32[1,16]{1,0:T(1,128)S(1)}, s32[1,16]{1,0:T(1,128)}, u32[]{:S(2)}) copy-start(s32[1,16]{1,0:T(1,128)} %tenant_ref.3) | copy-start | bytes 196
  19.8 7.6 %copy-start.12 = (s32[64]{0:T(128)S(1)}, s32[64]{0:T(128)}, u32[]{:S(2)}) copy-start(s32[64]{0:T(128)} %slot_ref.1) | copy-start | bytes 772
  23.2 9.0 %copy-start.13 = (bf16[128,2048]{1,0:T(8,128)(2,1)}, bf16[128,2048]{1,0:T(8,128)(2,1)S(1)}, u32[]{:S(2)}) copy-start(bf16[128,2048]{1,0:T(8,128)(2,1)S(1)} %collective-permute-done.3) | copy-start | bytes 1572868
  24.2 50.3 %collective-permute-start.6 = (bf16[128,2048]{1,0:T(8,128)(2,1)}, bf16[128,2048]{1,0:T(8,128)(2,1)}, u32[]{:S(2)}, u32[]{:S(2)}) collective-permute-start(bf16[128,2048]{1,0:T(8,128)(2,1)} %fusion.3), channel_id=1, source_target_pairs={{0,8},{4,12},{8,0},{12,4},{1,9},{5,13},{9,1},{13,5},{2,10},{6,14},... | collective-permute-start | bytes 1572872 | tf_op jit(solution)/shard_map/ppermute | solution.py:295
  32.3 21.8 %collective-permute-start.1 = (bf16[64,128]{1,0:T(8,128)(2,1)S(1)}, bf16[64,128]{1,0:T(8,128)(2,1)S(1)}, u32[]{:S(2)}, u32[]{:S(2)}) collective-permute-start(bf16[64,128]{1,0:T(8,128)(2,1)S(1)} %slice.8), channel_id=1, source_target_pairs={{0,8},{4,12},{8,0},{12,4},{1,9},{5,13},{9,1},{13,5},{2,10},{6,14},... | collective-permute-start | bytes 49160 | tf_op jit(solution)/shard_map/ppermute | solution.py:295
  54.1 3.7 %collective-permute-start = (bf16[64,128]{1,0:T(8,128)(2,1)S(1)}, bf16[64,128]{1,0:T(8,128)(2,1)S(1)}, u32[]{:S(2)}, u32[]{:S(2)}) collective-permute-start(bf16[64,128]{1,0:T(8,128)(2,1)S(1)} %slice.8), channel_id=1, source_target_pairs={{0,4},{4,0},{8,12},{12,8},{1,5},{5,1},{9,13},{13,9},{2,6},{6,2},{1... | collective-permute-start | bytes 49160 | tf_op jit(solution)/shard_map/ppermute | solution.py:295
  57.8 5.5 %collective-permute-start.2 = (bf16[64,128]{1,0:T(8,128)(2,1)S(1)}, bf16[64,128]{1,0:T(8,128)(2,1)S(1)}, u32[]{:S(2)}, u32[]{:S(2)}) collective-permute-start(bf16[64,128]{1,0:T(8,128)(2,1)S(1)} %slice.8), channel_id=1, source_target_pairs={{0,12},{4,8},{8,4},{12,0},{1,13},{5,9},{9,5},{13,1},{2,14},{6,10},... | collective-permute-start | bytes 49160 | tf_op jit(solution)/shard_map/ppermute | solution.py:295
  63.4 3.8 %collective-permute-start.7 = (bf16[80,128]{1,0:T(8,128)(2,1)S(1)}, bf16[80,128]{1,0:T(8,128)(2,1)S(1)}, u32[]{:S(2)}, u32[]{:S(2)}) collective-permute-start(bf16[80,128]{1,0:T(8,128)(2,1)S(1)} %pad_maximum_fusion.sums_ref.refs_0_), channel_id=1, source_target_pairs={{0,2},{1,3},{2,0},{3,1},{4,6},{5,7},{6,4},{7,5},{8,10},{9,11},{10,... | collective-permute-start | bytes 61448 | tf_op jit(solution)/shard_map/ppermute | solution.py:295
  67.3 9.8 %collective-permute-start.11 = (bf16[128,2560]{1,0:T(8,128)(2,1)S(1)}, bf16[128,2560]{1,0:T(8,128)(2,1)S(1)}, u32[]{:S(2)}, u32[]{:S(2)}) collective-permute-start(bf16[128,2560]{1,0:T(8,128)(2,1)S(1)} %constant_dynamic-update-slice_fusion.refs_4_.refs_8_), channel_id=1, source_target_pairs={{0,1},{1,0},{2,3},{3,2},{4,5},{5,4},{6,7},{7,6},{8,9},{9,8},{10,11... | collective-permute-start | bytes 1966088 | tf_op jit(solution)/shard_map/ppermute | solution.py:295
  67.3 9.8 %collective-permute-start.12 = (bf16[128,2560]{1,0:T(8,128)(2,1)S(1)}, bf16[128,2560]{1,0:T(8,128)(2,1)S(1)}, u32[]{:S(2)}, u32[]{:S(2)}) collective-permute-start(bf16[128,2560]{1,0:T(8,128)(2,1)S(1)} %collective-permute-done.10.refs_5_.refs_9_), channel_id=1, source_target_pairs={{0,1},{1,0},{2,3},{3,2},{4,5},{5,4},{6,7},{7,6},{8,9},{9,8},{10,11... | collective-permute-start | bytes 1966088 | tf_op jit(solution)/shard_map/ppermute | solution.py:295
  67.8 2.2 %copy-start.1 = (bf16[8192,256]{1,0:T(8,128)(2,1)S(1)}, bf16[8192,256]{1,0:T(8,128)(2,1)}, u32[]{:S(2)}) copy-start(bf16[8192,256]{1,0:T(8,128)(2,1)} %wk_ref.5) | copy-start | bytes 12582916
  70.0 4.5 %copy-start.14 = (bf16[128,2048]{1,0:T(8,128)(2,1)S(1)}, bf16[128,2048]{1,0:T(8,128)(2,1)}, u32[]{:S(2)}) copy-start(bf16[128,2048]{1,0:T(8,128)(2,1)} %copy-done.13) | copy-start | bytes 1572868
  73.9 3.1 %collective-permute-start.8 = (bf16[80,128]{1,0:T(8,128)(2,1)S(1)}, bf16[80,128]{1,0:T(8,128)(2,1)S(1)}, u32[]{:S(2)}, u32[]{:S(2)}) collective-permute-start(bf16[80,128]{1,0:T(8,128)(2,1)S(1)} %pad_maximum_fusion.sums_ref.refs_0_), channel_id=1, source_target_pairs={{0,1},{1,0},{2,3},{3,2},{4,5},{5,4},{6,7},{7,6},{8,9},{9,8},{10,11... | collective-permute-start | bytes 61448 | tf_op jit(solution)/shard_map/ppermute | solution.py:295
  74.0 3.0 %collective-permute-start.9 = (bf16[80,128]{1,0:T(8,128)(2,1)S(1)}, bf16[80,128]{1,0:T(8,128)(2,1)S(1)}, u32[]{:S(2)}, u32[]{:S(2)}) collective-permute-start(bf16[80,128]{1,0:T(8,128)(2,1)S(1)} %collective-permute-done.7.refs_1_), channel_id=1, source_target_pairs={{0,1},{1,0},{2,3},{3,2},{4,5},{5,4},{6,7},{7,6},{8,9},{9,8},{10,11... | collective-permute-start | bytes 61448 | tf_op jit(solution)/shard_map/ppermute | solution.py:295

commit v2 on v1

v2 whole, which is shorter than its diff:
```python
import functools

import jax
import jax.numpy as jnp
from jax import lax
from jax.experimental import pallas as pl
from jax.experimental.pallas import tpu as pltpu
from jax.sharding import PartitionSpec as P

ADAPTER_SCALE = 2.0
LOSS_UNSCALE = 0.125
VMEM_BYTES = 48 * 1024 * 1024
COST = pl.CostEstimate(flops=0, bytes_accessed=0, transcendentals=0)

f32 = jnp.float32
bf16 = jnp.bfloat16


def dot_nt(former, latter):
    return lax.dot_general(former, latter, (((1,), (1,)), ((), ())), preferred_element_type=f32)


def dot_nn(former, latter):
    return lax.dot_general(former, latter, (((1,), (0,)), ((), ())), preferred_element_type=f32)


def dot_tn(former, latter):
    return lax.dot_general(former, latter, (((0,), (0,)), ((), ())), preferred_element_type=f32)


def params():
    return pltpu.CompilerParams(vmem_limit_bytes=VMEM_BYTES)


def frozen_part(gk, gv, wk, wv):
    return dot_nt(gk, wk) + dot_nt(gv, wv)


def frozen_copies(block, width, wk_hbm, wv_hbm, wk, wv, sems):
    rows = pl.ds(pl.multiple_of(block * width, width), width)
    return [
        pltpu.make_async_copy(wk_hbm.at[rows], wk, sems.at[0]),
        pltpu.make_async_copy(wv_hbm.at[rows], wv, sems.at[1]),
    ]


def frozen_kernel(gk_hbm, gv_hbm, wk_hbm, wv_hbm, *refs):
    *outs, gk, gv, wk, wv, sems = refs
    width = outs[0].shape[1]
    z = lax.axis_index("tensor")
    head = [
        pltpu.make_async_copy(gk_hbm, gk, sems.at[len(outs), 0]),
        pltpu.make_async_copy(gv_hbm, gv, sems.at[len(outs), 1]),
    ]
    body = [
        frozen_copies(block, width, wk_hbm, wv_hbm, wk.at[n], wv.at[n], sems.at[n])
        for n, block in enumerate((z ^ 2, z ^ 1, z))
    ]
    for copies in (head, *body):
        for copy in copies:
            copy.start()
    for copy in head:
        copy.wait()
    for n, out in enumerate(outs):
        for copy in body[n]:
            copy.wait()
        out[...] = frozen_part(gk[...], gv[...], wk[n], wv[n]).astype(out.dtype)


def frozen_blocks(gk, gv, wk, wv, width, dtypes):
    rows, feats = gk.shape
    count = len(dtypes)
    hbm = pl.BlockSpec(memory_space=pltpu.HBM)
    vmem = pl.BlockSpec(memory_space=pltpu.VMEM)
    return pl.pallas_call(
        frozen_kernel,
        in_specs=[hbm] * 4,
        out_specs=[vmem] * count,
        out_shape=[jax.ShapeDtypeStruct((rows, width), dtype) for dtype in dtypes],
        scratch_shapes=[
            pltpu.VMEM((rows, feats), bf16),
            pltpu.VMEM((rows, feats), bf16),
            pltpu.VMEM((count, width, feats), bf16),
            pltpu.VMEM((count, width, feats), bf16),
            pltpu.SemaphoreType.DMA((count + 1, 2)),
        ],
        compiler_params=params(),
        cost_estimate=COST,
        name="frozen_blocks",
    )(gk, gv, wk, wv)


def segment_masks(len_ref, shape, segments):
    position = lax.broadcasted_iota(jnp.int32, shape, 1)
    masks = []
    total = jnp.int32(0)
    for k in range(segments):
        begin = total
        total = total + len_ref[0, k]
        masks.append((position >= begin) & (position < total))
    return masks


def first_kernel(
    frozen, len_hbm, tenant_hbm, slot_hbm, tok_hbm, gk_hbm, gv_hbm, kd_hbm, vd_hbm, ku_hbm, vu_hbm,
    wk_hbm, wv_hbm, out_ref, term_ref, len_ref, tenant_ref, slot_ref, tok, gk, gv, down, key_up,
    value_up, wk, wv, products, sems,
):
    segments = tenant_ref.shape[1]
    rank = kd_hbm.shape[1]
    rows, width = tok.shape
    half = segments * rank
    scalars = [
        pltpu.make_async_copy(tenant_hbm, tenant_ref, sems.at[0, 0]),
        pltpu.make_async_copy(len_hbm, len_ref, sems.at[0, 1]),
        pltpu.make_async_copy(slot_hbm, slot_ref, sems.at[0, 2]),
    ]
    grads = [
        pltpu.make_async_copy(gk_hbm, gk, sems.at[0, 3]),
        pltpu.make_async_copy(gv_hbm, gv, sems.at[0, 4]),
    ]
    weights = []
    if frozen:
        weights = frozen_copies(
            lax.axis_index("tensor") ^ 3, width, wk_hbm, wv_hbm, wk, wv, sems.at[3]
        )
    ups = [
        pltpu.make_async_copy(ku_hbm, key_up, sems.at[0, 5]),
        pltpu.make_async_copy(vu_hbm, value_up, sems.at[0, 6]),
    ]
    downs = [pltpu.make_async_copy(tok_hbm, tok, sems.at[0, 7])]
    for copy in scalars + grads + weights + ups + downs:
        copy.start()
    for copy in scalars:
        copy.wait()
    for k in range(segments):
        tenant = tenant_ref[0, k]
        at = pl.ds(k * rank, rank)
        after = pl.ds(half + k * rank, rank)
        downs.append(pltpu.make_async_copy(kd_hbm.at[tenant], down.at[at], sems.at[1, k]))
        downs.append(pltpu.make_async_copy(vd_hbm.at[tenant], down.at[after], sems.at[2, k]))
    for copy in downs[1:]:
        copy.start()
    masks = segment_masks(len_ref, (rank, rows), segments)
    slot_of = jnp.zeros((rank, rows), f32)
    for k in range(segments):
        slot = slot_ref[tenant_ref[0, k]].astype(f32)
        slot_of = jnp.where(masks[k], slot, slot_of)
    out_ref[4 * rank :, :] = slot_of.astype(bf16)

    def fold(take):
        total = jnp.zeros((rank, rows), f32)
        for k in range(segments):
            total = jnp.where(masks[k], take(k), total)
        return total.astype(bf16)

    def by_tenant(k):
        return products[pl.ds(pl.multiple_of(tenant_ref[0, k] * rank, rank), rank), :]

    for copy in grads + weights:
        copy.wait()
    if frozen:
        term_ref[...] = frozen_part(gk[...], gv[...], wk[...], wv[...]).astype(term_ref.dtype)
    for copy in ups:
        copy.wait()
    for at, up, grad in ((2, key_up, gk), (3, value_up, gv)):
        products[...] = dot_nt(up[...].reshape(products.shape[0], up.shape[2]), grad[...])
        out_ref[at * rank : (at + 1) * rank, :] = fold(by_tenant)
    for copy in downs:
        copy.wait()
    both = dot_nt(down[...], tok[...])
    for at in (0, 1):
        out_ref[at * rank : (at + 1) * rank, :] = fold(
            lambda k: both[at * half + k * rank : at * half + (k + 1) * rank]
        )


def first_products(frozen, tokens, gk, gv, kd, vd, ku, vu, wk, wv, lengths, tenants, slots):
    rows, width = tokens.shape
    feats = gk.shape[1]
    segments = tenants.shape[1]
    rank = kd.shape[1]
    both = 2 * segments * rank
    hbm = pl.BlockSpec(memory_space=pltpu.HBM)
    vmem = pl.BlockSpec(memory_space=pltpu.VMEM)
    term = (rows, width) if frozen else (16, 128)
    return pl.pallas_call(
        functools.partial(first_kernel, frozen),
        in_specs=[hbm] * 12,
        out_specs=[vmem, vmem],
        out_shape=[
            jax.ShapeDtypeStruct((5 * rank, rows), bf16),
            jax.ShapeDtypeStruct(term, bf16),
        ],
        scratch_shapes=[
            pltpu.SMEM(lengths.shape, jnp.int32),
            pltpu.SMEM(tenants.shape, jnp.int32),
            pltpu.SMEM(slots.shape, jnp.int32),
            pltpu.VMEM((rows, width), bf16),
            pltpu.VMEM((rows, feats), bf16),
            pltpu.VMEM((rows, feats), bf16),
            pltpu.VMEM((both, width), bf16),
            pltpu.VMEM(ku.shape, bf16),
            pltpu.VMEM(vu.shape, bf16),
            pltpu.VMEM((width, feats), bf16),
            pltpu.VMEM((width, feats), bf16),
            pltpu.VMEM((ku.shape[0] * rank, rows), f32),
            pltpu.SemaphoreType.DMA((4, max(segments, 8))),
        ],
        compiler_params=params(),
        cost_estimate=COST,
        name="first_products",
    )(lengths, tenants, slots, tokens, gk, gv, kd, vd, ku, vu, wk, wv)


def adapter_kernel(
    len_ref, tenant_ref, sums_ref, term_ref, kd_hbm, vd_hbm, out_ref, down, back, sems
):
    segments = tenant_ref.shape[1]
    rank = kd_hbm.shape[1]
    rows = out_ref.shape[0]
    half = segments * rank
    copies = []
    for k in range(segments):
        tenant = tenant_ref[0, k]
        at = pl.ds(k * rank, rank)
        after = pl.ds(half + k * rank, rank)
        copies.append(pltpu.make_async_copy(kd_hbm.at[tenant], down.at[at], sems.at[0, k]))
        copies.append(pltpu.make_async_copy(vd_hbm.at[tenant], down.at[after], sems.at[1, k]))
    for copy in copies:
        copy.start()
    masks = segment_masks(len_ref, (rank, rows), segments)
    for at in (0, 1):
        values = ADAPTER_SCALE * sums_ref[(2 + at) * rank : (3 + at) * rank, :].astype(f32)
        for k in range(segments):
            start = at * half + k * rank
            back[start : start + rank, :] = jnp.where(masks[k], values, 0.0).astype(bf16)
    for copy in copies:
        copy.wait()
    out_ref[...] = term_ref[...] + dot_tn(back[...], down[...])


def add_adapters(term, sums, kd, vd, lengths, tenants):
    rows, width = term.shape
    segments = tenants.shape[1]
    rank = kd.shape[1]
    both = 2 * segments * rank
    smem = pl.BlockSpec(memory_space=pltpu.SMEM)
    vmem = pl.BlockSpec(memory_space=pltpu.VMEM)
    hbm = pl.BlockSpec(memory_space=pltpu.HBM)
    return pl.pallas_call(
        adapter_kernel,
        in_specs=[smem, smem, vmem, vmem, hbm, hbm],
        out_specs=vmem,
        out_shape=jax.ShapeDtypeStruct((rows, width), f32),
        scratch_shapes=[
            pltpu.VMEM((both, width), bf16),
            pltpu.VMEM((both, rows), bf16),
            pltpu.SemaphoreType.DMA((2, segments)),
        ],
        compiler_params=params(),
        cost_estimate=COST,
        name="add_adapters",
    )(lengths, tenants, sums, term, kd, vd)


def grads_kernel(count, rank, per_owner, first_ref, *refs):
    sums = refs[:count]
    chunks = refs[count : 2 * count]
    ends = refs[2 * count : 3 * count]
    ka_ref, va_ref, kb_ref, vb_ref, spread_ref = refs[3 * count :]
    size = per_owner * rank
    scale = ADAPTER_SCALE * LOSS_UNSCALE

    @pl.when(pl.program_id(0) == 0)
    def _():
        feats = kb_ref.shape[2]
        rows = sums[0].shape[1]
        wanted = lax.broadcasted_iota(jnp.int32, (size, rows), 0) // rank + first_ref[0]
        b_key = jnp.zeros((size, feats), f32)
        b_value = jnp.zeros((size, feats), f32)
        for n in range(count):
            slot = sums[n][4 * rank : 4 * rank + 1, :].astype(f32).astype(jnp.int32)
            mask = wanted == slot

            def spread(index):
                values = sums[n][index * rank : (index + 1) * rank, :].astype(f32)
                tiled = jnp.concatenate([values] * per_owner, axis=0)
                return jnp.where(mask, tiled, 0.0).astype(bf16)

            columns = slice(n * rows, (n + 1) * rows)
            spread_ref[0:size, columns] = spread(2)
            spread_ref[size:, columns] = spread(3)
            b_key += dot_nn(spread(0), ends[n][:, :feats])
            b_value += dot_nn(spread(1), ends[n][:, feats:])
        kb_ref[...] = (scale * b_key).reshape(kb_ref.shape)
        vb_ref[...] = (scale * b_value).reshape(vb_ref.shape)

    tokens = jnp.concatenate([chunk[...] for chunk in chunks], axis=0)
    product = scale * dot_nn(spread_ref[...], tokens)
    ka_ref[...] = product[:size].reshape(ka_ref.shape)
    va_ref[...] = product[size:].reshape(va_ref.shape)


def adapter_grads(first, sums, sent, rank, per_owner, width, feats):
    count = len(sums)
    rows = sent[0].shape[0]
    chunk = 2 * feats
    steps = width // chunk
    a_spec = pl.BlockSpec((per_owner, rank, chunk), lambda i: (0, 0, i))
    b_spec = pl.BlockSpec((per_owner, rank, feats), lambda i: (0, 0, 0))
    return pl.pallas_call(
        functools.partial(grads_kernel, count, rank, per_owner),
        grid=(steps,),
        in_specs=[pl.BlockSpec(memory_space=pltpu.SMEM)]
        + [pl.BlockSpec(sums[0].shape, lambda i: (0, 0))] * count
        + [pl.BlockSpec((rows, chunk), lambda i: (0, i))] * count
        + [pl.BlockSpec((rows, chunk), lambda i: (0, steps))] * count,
        out_specs=[a_spec, a_spec, b_spec, b_spec],
        out_shape=[
            jax.ShapeDtypeStruct((per_owner, rank, width), f32),
            jax.ShapeDtypeStruct((per_owner, rank, width), f32),
            jax.ShapeDtypeStruct((per_owner, rank, feats), f32),
            jax.ShapeDtypeStruct((per_owner, rank, feats), f32),
        ],
        scratch_shapes=[pltpu.VMEM((2 * per_owner * rank, count * rows), bf16)],
        compiler_params=params(),
        cost_estimate=COST,
        name="adapter_grads",
    )(first, *sums, *sent, *sent)


def swap(values, axis, bit, size):
    return lax.ppermute(values, axis, [(i, i ^ bit) for i in range(size)])


def local(
    tokens, gk, gv, wk, wv, kd, vd, ku, vu, segment_length, segment_tenant, adapter_output_slot
):
    rows, width = tokens.shape
    feats = gk.shape[1]
    adapters, rank, _ = kd.shape
    n_tensor = lax.axis_size("tensor")
    n_dp = lax.axis_size("dp")
    per_owner = adapters // n_dp
    first = (lax.axis_index("dp") * per_owner).astype(jnp.int32).reshape(1)
    in_hbm = functools.partial(pltpu.with_memory_space_constraint, memory_space=pltpu.HBM)
    kd, vd = in_hbm(kd), in_hbm(vd)
    large = [in_hbm(array) for array in (gk, gv, wk, wv)]
    halving = n_tensor == 4

    part, x0 = first_products(
        halving, in_hbm(tokens), large[0], large[1], kd, vd, in_hbm(ku), in_hbm(vu), *large[2:],
        in_hbm(segment_length), in_hbm(segment_tenant), in_hbm(adapter_output_slot),
    )
    products, slot_rows = part[: 4 * rank], part[4 * rank :]
    if halving:
        r1 = swap(x0, "tensor", 1, 4)
        others = [swap(products, "tensor", bit, 4) for bit in (1, 2, 3)]
        tokens, wk, x0 = lax.optimization_barrier((tokens, wk, x0))
        sent = jnp.concatenate([tokens, gk, gv], axis=1)
        x2, x1, own = frozen_blocks(large[0], large[1], in_hbm(wk), large[3], width, (f32, bf16, f32))
        x2, x1, r1, *others = lax.optimization_barrier((x2, x1, r1, *others))
        x2 = (x2 + r1.astype(f32)).astype(bf16)
        r3 = swap(x2, "tensor", 2, 4)
        total = products.astype(f32)
        for other in others:
            total = total + other.astype(f32)
    else:
        sent = jnp.concatenate([tokens, gk, gv], axis=1)
        total = lax.psum(products.astype(f32), "tensor")
        term = dot_nt(gk, wk) + dot_nt(gv, wv)
        own = lax.psum_scatter(
            term.astype(bf16), "tensor", scatter_dimension=1, tiled=True
        ).astype(f32)
    sums = jnp.concatenate([total.astype(bf16), slot_rows], axis=0)
    if halving:
        x1, sums = lax.optimization_barrier((x1, sums))
        r4 = swap(x1, "tensor", 1, 4)

    if n_dp == 4:
        sent_across, sent_core = swap(sent, "dp", 2, 4), swap(sent, "dp", 1, 4)
        pair = jnp.concatenate([sums, swap(sums, "dp", 1, 4)], axis=0)
        pairs = [pair, swap(pair, "dp", 2, 4)]
        all_sums = [half[n * sums.shape[0] : (n + 1) * sums.shape[0]] for half in pairs for n in (0, 1)]
        all_sent = [sent, sent_core, sent_across, swap(sent_across, "dp", 1, 4)]
    else:
        gathered = lax.all_gather(sent, "dp")
        all_sent = [gathered[i] for i in range(n_dp)]
        gathered = lax.all_gather(sums, "dp")
        all_sums = [gathered[i] for i in range(n_dp)]

    own = add_adapters(own, sums, kd, vd, segment_length, segment_tenant)
    grads = adapter_grads(first, all_sums, all_sent, rank, per_owner, width, feats)
    if halving:
        own, *grads = lax.optimization_barrier((own, *grads))
        own = own + r3.astype(f32) + r4.astype(f32)
    input_gradient = own.astype(bf16)
    return (input_gradient, *grads)


def solution(mesh):
    placed = (
        P(("group", "dp"), "tensor"),
        P(("group", "dp"), "tensor"),
        P(("group", "dp"), "tensor"),
        P(None, "tensor"),
        P(None, "tensor"),
        P(None, None, "tensor"),
        P(None, None, "tensor"),
        P(None, None, "tensor"),
        P(None, None, "tensor"),
        P(("group", "dp"), None),
        P(("group", "dp"), None),
        P("group"),
    )
    return jax.shard_map(
        local,
        mesh=mesh,
        in_specs=placed,
        out_specs=(
            P(("group", "dp"), "tensor"),
            P(("group", "dp"), None, "tensor"),
            P(("group", "dp"), None, "tensor"),
            P(("group", "dp"), None, "tensor"),
            P(("group", "dp"), None, "tensor"),
        ),
        check_vma=False,
    )
```

time: 81.6 us -> 55.4 us (0.68)
  waiting for transfers between devices: 30.7 us -> 20.5 us
  Pallas kernels: 22 us -> 15.8 us
  local copies, waits for them, and re-layouts: 6.16 us -> 1.31 us
  starting transfers between devices: 17.8 us -> 13.6 us
    ppermute x11, waiting for transfers between devices: 30.7 us -> 20.5 us  [swap(): return lax.ppermute(values, axis, [(i, i ^ bit) for i in range(size)])]
    pallas_call x5 -> x3, Pallas kernels: 18 us -> 11.8 us  [the longest x1 4.79 us: first_products(): pl.pallas_call(functools.partial(first_kernel, frozen), in_specs=[hbm] *...]
    unnamed x32 -> x16, local copies, waits for them, and re-layouts: 6.14 us -> 1.3 us
    ppermute x2 -> x0, starting transfers between devices: 4.22 us -> none  [the longest x1 2.77 us: local(): r4 = lax.ppermute(x1, 'tensor', [(0, 1), (3, 2)])]
  transfers between devices with their start and end apart: 13 -> 11, of which waited for: 4 -> 5; matrix products, arithmetic and copies ran while one was open for 4% -> 2% of each run, Pallas kernels for 19% -> 20%
where the time goes in v2:
time: 55.4 us; the launch traced here: 55.1 us
  waiting for transfers between devices  20.5 us (37%)
  Pallas kernels  15.8 us (29%)
  starting transfers between devices  13.6 us (25%)
  other arithmetic  3.13 us (6%)
  local copies, waits for them, and re-layouts  1.31 us (2%)
  between operations  0.79 us (1%)
    ppermute x11, waiting for transfers between devices, swap(): return lax.ppermute(values, axis, [(i, i ^ bit) for i in range(size)])  20.5 us
    ppermute x11, starting transfers between devices, swap(): return lax.ppermute(values, axis, [(i, i ^ bit) for i in range(size)])  13.6 us
    pallas_call x1, Pallas kernels, first_products(): pl.pallas_call(functools.partial(first_kernel, frozen), in_specs=[hbm] *...  4.79 us
    pallas_call x1, Pallas kernels, frozen_blocks(): pl.pallas_call(frozen_kernel, in_specs=[hbm] * 4, out_specs=[vmem] * coun...  4.13 us
    pallas_call x1, Pallas kernels, adapter_grads(): pl.pallas_call(functools.partial(grads_kernel, count, rank, per_owner), g...  3.99 us
    pallas_call x1, Pallas kernels, add_adapters(): pl.pallas_call(adapter_kernel, in_specs=[smem, smem, vmem, vmem, hbm, hbm...  2.85 us
    convert_element_type x1, other arithmetic, local(): input_gradient = own.astype(bf16)  2.21 us
    unnamed x16, local copies, waits for them, and re-layouts  1.3 us
  transfers between devices with their start and end apart: 11, of which 5 were waited for; matrix products, arithmetic and copies ran while one was open for 2% of the time, Pallas kernels for 20%

profile of v2, /device:TPU:0, one launch (start us, length us, event | category | flops | bytes accessed | tf_op | source)
XLA Modules:
  0.0 55.1 jit_solution(9105500045416694084)
XLA Ops:
  0.6 0.0 copy-start.6
  0.6 0.0 copy-start.5
  0.7 4.8 %first_products.1 = (bf16[80,128]{1,0:T(8,128)(2,1)S(1)}, bf16[128,2048]{1,0:T(8,128)(2,1)S(1)}) custom-call(s32[1,16]{1,0:T(1,128)} %len_ref.1, s32[1,16]{1,0:T(1,128)} %tenant_ref.1, s32[64]{0:T(128)} %slot_hbm.1, bf16[128,2048]{1,0:T(8,128)(2,1)} %tok_hbm.1, bf16[128,256]{1,0:T(8,128)(2,1)} %gk_hbm.3, bf16[128,256]{1,0:T(8,128)(2,1)} %gv_hbm.3, ...), custom_call_target="tpu_custom_call" | custom-call | tf_op jit(solution)/shard_map/first_products/pallas_call | solution.py:187
  5.5 3.1 %collective-permute-start = (bf16[128,2048]{1,0:T(8,128)(2,1)S(1)}, bf16[128,2048]{1,0:T(8,128)(2,1)S(1)}, u32[]{:S(2)}, u32[]{:S(2)}) collective-permute-start(bf16[128,2048]{1,0:T(8,128)(2,1)S(1)} %get-tuple-element.29), channel_id=1, source_target_pairs={{0,4},{4,0},{8,12},{12,8},{1,5},{5,1},{9,13},{13,9},{2,6},{6,2},{1... | collective-permute-start | bytes 1572872 | tf_op jit(solution)/shard_map/ppermute | solution.py:334
  8.7 1.6 %collective-permute-start.7 = (bf16[128,2560]{1,0:T(8,128)(2,1)S(1)}, bf16[128,2560]{1,0:T(8,128)(2,1)S(1)}, u32[]{:S(2)}, u32[]{:S(2)}) collective-permute-start(bf16[128,2560]{1,0:T(8,128)(2,1)S(1)} %constant_dynamic-update-slice_fusion.refs_4_.refs_8_), channel_id=1, source_target_pairs={{0,2},{1,3},{2,0},{3,1},{4,6},{5,7},{6,4},{7,5},{8,10},{9,11},{10,... | collective-permute-start | bytes 1966088 | tf_op jit(solution)/shard_map/ppermute | solution.py:334
  10.2 2.5 %collective-permute-start.3 = (bf16[64,128]{1,0:T(8,128)(2,1)S(1)}, bf16[64,128]{1,0:T(8,128)(2,1)S(1)}, u32[]{:S(2)}, u32[]{:S(2)}) collective-permute-start(bf16[64,128]{1,0:T(8,128)(2,1)S(1)} %slice.12), channel_id=1, source_target_pairs={{0,12},{4,8},{8,4},{12,0},{1,13},{5,9},{9,5},{13,1},{2,14},{6,10},... | collective-permute-start | bytes 49160 | tf_op jit(solution)/shard_map/ppermute | solution.py:334
  12.7 0.1 collective-permute-start.2
  12.8 1.8 %collective-permute-start.1 = (bf16[64,128]{1,0:T(8,128)(2,1)S(1)}, bf16[64,128]{1,0:T(8,128)(2,1)S(1)}, u32[]{:S(2)}, u32[]{:S(2)}) collective-permute-start(bf16[64,128]{1,0:T(8,128)(2,1)S(1)} %slice.12), channel_id=1, source_target_pairs={{0,4},{4,0},{8,12},{12,8},{1,5},{5,1},{9,13},{13,9},{2,6},{6,2},{1... | collective-permute-start | bytes 49160 | tf_op jit(solution)/shard_map/ppermute | solution.py:334
  14.6 4.1 %frozen_blocks.1 = (f32[128,2048]{1,0:T(8,128)S(1)}, bf16[128,2048]{1,0:T(8,128)(2,1)S(1)}, f32[128,2048]{1,0:T(8,128)S(1)}) custom-call(bf16[128,256]{1,0:T(8,128)(2,1)} %gk_hbm.3, bf16[128,256]{1,0:T(8,128)(2,1)} %gv_hbm.3, bf16[8192,256]{1,0:T(8,128)(2,1)} %wk_hbm.2, bf16[8192,256]{1,0:T(8,128)(2,1)} %wv_hbm.3), custom_call_target="tpu_custom_call" | custom-call | tf_op jit(solution)/shard_map/frozen_blocks/pallas_call | solution.py:75
  18.7 0.0 copy-start
  18.8 4.6 %collective-permute-done.3 = bf16[64,128]{1,0:T(8,128)(2,1)S(1)} collective-permute-done((bf16[64,128]{1,0:T(8,128)(2,1)S(1)}, bf16[64,128]{1,0:T(8,128)(2,1)S(1)}, u32[]{:S(2)}, u32[]{:S(2)}) %collective-permute-start.3) | collective-permute-done | bytes 16416 | tf_op jit(solution)/shard_map/ppermute | solution.py:334
  23.4 0.0 collective-permute-start.6
  23.4 0.0 collective-permute-done.2
  23.4 0.0 collective-permute-done.1
  23.4 0.0 collective-permute-done
  23.4 0.9 %add_convert_fusion.1 = bf16[128,2048]{1,0:T(8,128)(2,1)} fusion(f32[128,2048]{1,0:T(8,128)S(1)} %get-tuple-element.46, bf16[128,2048]{1,0:T(8,128)(2,1)S(1)} %collective-permute-done), kind=kLoop, calls=%fused_computation.1 | loop fusion | flops 786432 | bytes 2097152 | tf_op jit(solution)/shard_map/convert_element_type | solution.py:364
  24.3 0.6 %collective-permute-done.7.refs_6_.refs_10_ = bf16[128,2560]{1,0:T(8,128)(2,1)S(1)} collective-permute-done((bf16[128,2560]{1,0:T(8,128)(2,1)S(1)}, bf16[128,2560]{1,0:T(8,128)(2,1)S(1)}, u32[]{:S(2)}, u32[]{:S(2)}) %collective-permute-start.7) | collective-permute-done | bytes 655392 | tf_op jit(solution)/shard_map/ppermute | solution.py:334
  24.9 0.0 collective-permute-start.8
  24.9 2.7 %collective-permute-start.9 = (bf16[128,2048]{1,0:T(8,128)(2,1)}, bf16[128,2048]{1,0:T(8,128)(2,1)}, u32[]{:S(2)}, u32[]{:S(2)}) collective-permute-start(bf16[128,2048]{1,0:T(8,128)(2,1)} %add_convert_fusion.1), channel_id=1, source_target_pairs={{0,8},{4,12},{8,0},{12,4},{1,9},{5,13},{9,1},{13,5},{2,10},{6,14},... | collective-permute-start | bytes 1572872 | tf_op jit(solution)/shard_map/ppermute | solution.py:334
  27.6 0.4 collective-permute-start.10
  28.0 0.0 collective-permute-start.4
  28.0 1.2 %collective-permute-done.4.refs_1_ = bf16[80,128]{1,0:T(8,128)(2,1)S(1)} collective-permute-done((bf16[80,128]{1,0:T(8,128)(2,1)S(1)}, bf16[80,128]{1,0:T(8,128)(2,1)S(1)}, u32[]{:S(2)}, u32[]{:S(2)}) %collective-permute-start.4) | collective-permute-done | bytes 20512 | tf_op jit(solution)/shard_map/ppermute | solution.py:334
  29.2 1.5 %collective-permute-start.5 = (bf16[160,128]{1,0:T(8,128)(2,1)S(1)}, bf16[160,128]{1,0:T(8,128)(2,1)S(1)}, u32[]{:S(2)}, u32[]{:S(2)}) collective-permute-start(bf16[160,128]{1,0:T(8,128)(2,1)S(1)} %pad_maximum_fusion), channel_id=1, source_target_pairs={{0,2},{1,3},{2,0},{3,1},{4,6},{5,7},{6,4},{7,5},{8,10},{9,11},{10,... | collective-permute-start | bytes 122888 | tf_op jit(solution)/shard_map/ppermute | solution.py:334
  30.7 1.2 %copy-done.1 = f32[128,2048]{1,0:T(8,128)S(1)} copy-done((f32[128,2048]{1,0:T(8,128)S(1)}, f32[128,2048]{1,0:T(8,128)}, u32[]{:S(2)}) %copy-start.1) | copy-done | bytes 1048600
  32.0 2.9 %add_adapters.1 = f32[128,2048]{1,0:T(8,128)S(1)} custom-call(s32[1,16]{1,0:T(1,128)S(1)} %copy-done.2, s32[1,16]{1,0:T(1,128)S(1)} %copy-done.3, bf16[80,128]{1,0:T(8,128)(2,1)S(1)} %pad_maximum_fusion.1.sums_ref.refs_0_, f32[128,2048]{1,0:T(8,128)S(1)} %copy-done.1, bf16[64,16,2048]{2,1,0:T(8,128)(2,1)} %kd_hbm.3, bf16[64,16,2048]{2,1,0:T(8,128)(2,1)} %vd_hbm.3), custom_call_target="tpu_custom_call" | custom-call | tf_op jit(solution)/shard_map/add_adapters/pallas_call | solution.py:251
  34.8 0.0 collective-permute-done.5
  34.8 0.0 collective-permute-done.6.refs_5_.refs_9_
  34.8 0.0 collective-permute-done.8.refs_7_.refs_11_
  34.9 4.0 %adapter_grads.1 = (f32[16,16,2048]{2,1,0:T(8,128)}, f32[16,16,2048]{2,1,0:T(8,128)}, f32[16,16,256]{2,1,0:T(8,128)}, f32[16,16,256]{2,1,0:T(8,128)}) custom-call(s32[1]{0:T(128)} %bitcast.first_ref, bf16[80,128]{1,0:T(8,128)(2,1)S(1)} %pad_maximum_fusion.1.sums_ref.refs_0_, bf16[80,128]{1,0:T(8,128)(2,1)S(1)} %collective-permute-done.4.refs_1_, ...), custom_call_target="tpu_custom_call" | custom-call | tf_op jit(solution)/shard_map/adapter_grads/pallas_call | solution.py:312
  38.9 12.9 %collective-permute-done.9 = bf16[128,2048]{1,0:T(8,128)(2,1)} collective-permute-done((bf16[128,2048]{1,0:T(8,128)(2,1)}, bf16[128,2048]{1,0:T(8,128)(2,1)}, u32[]{:S(2)}, u32[]{:S(2)}) %collective-permute-start.9) | collective-permute-done | bytes 524320 | tf_op jit(solution)/shard_map/ppermute | solution.py:334
  51.7 1.2 %collective-permute-done.10 = bf16[128,2048]{1,0:T(8,128)(2,1)} collective-permute-done((bf16[128,2048]{1,0:T(8,128)(2,1)S(1)}, bf16[128,2048]{1,0:T(8,128)(2,1)}, u32[]{:S(2)}, u32[]{:S(2)}) %collective-permute-start.10) | collective-permute-done | bytes 524320 | tf_op jit(solution)/shard_map/ppermute | solution.py:334
  52.9 2.2 %add_convert_fusion = bf16[128,2048]{1,0:T(8,128)(2,1)} fusion(bf16[128,2048]{1,0:T(8,128)(2,1)} %collective-permute-done.10, f32[128,2048]{1,0:T(8,128)S(1)} %add_adapters.1, bf16[128,2048]{1,0:T(8,128)(2,1)} %collective-permute-done.9), kind=kLoop, calls=%fused_computation | loop fusion | flops 1310720 | bytes 2621440 | tf_op jit(solution)/shard_map/convert_element_type | solution.py:398
  (19 shorter events, 0.1 us)
Async XLA Ops:
  0.6 8.0 %copy-start.6 = (bf16[128,256]{1,0:T(8,128)(2,1)S(1)}, bf16[128,256]{1,0:T(8,128)(2,1)}, u32[]{:S(2)}) copy-start(bf16[128,256]{1,0:T(8,128)(2,1)} %gv_hbm.3) | copy-start | bytes 196612
  0.6 8.0 %copy-start.5 = (bf16[128,256]{1,0:T(8,128)(2,1)S(1)}, bf16[128,256]{1,0:T(8,128)(2,1)}, u32[]{:S(2)}) copy-start(bf16[128,256]{1,0:T(8,128)(2,1)} %gk_hbm.3) | copy-start | bytes 196612
  0.7 7.9 %copy-start.4 = (bf16[128,2048]{1,0:T(8,128)(2,1)S(1)}, bf16[128,2048]{1,0:T(8,128)(2,1)}, u32[]{:S(2)}) copy-start(bf16[128,2048]{1,0:T(8,128)(2,1)} %tok_hbm.1) | copy-start | bytes 1572868
  5.5 17.9 %collective-permute-start = (bf16[128,2048]{1,0:T(8,128)(2,1)S(1)}, bf16[128,2048]{1,0:T(8,128)(2,1)S(1)}, u32[]{:S(2)}, u32[]{:S(2)}) collective-permute-start(bf16[128,2048]{1,0:T(8,128)(2,1)S(1)} %get-tuple-element.29), channel_id=1, source_target_pairs={{0,4},{4,0},{8,12},{12,8},{1,5},{5,1},{9,13},{13,9},{2,6},{6,2},{1... | collective-permute-start | bytes 1572872 | tf_op jit(solution)/shard_map/ppermute | solution.py:334
  8.7 16.3 %collective-permute-start.7 = (bf16[128,2560]{1,0:T(8,128)(2,1)S(1)}, bf16[128,2560]{1,0:T(8,128)(2,1)S(1)}, u32[]{:S(2)}, u32[]{:S(2)}) collective-permute-start(bf16[128,2560]{1,0:T(8,128)(2,1)S(1)} %constant_dynamic-update-slice_fusion.refs_4_.refs_8_), channel_id=1, source_target_pairs={{0,2},{1,3},{2,0},{3,1},{4,6},{5,7},{6,4},{7,5},{8,10},{9,11},{10,... | collective-permute-start | bytes 1966088 | tf_op jit(solution)/shard_map/ppermute | solution.py:334
  10.2 13.2 %collective-permute-start.3 = (bf16[64,128]{1,0:T(8,128)(2,1)S(1)}, bf16[64,128]{1,0:T(8,128)(2,1)S(1)}, u32[]{:S(2)}, u32[]{:S(2)}) collective-permute-start(bf16[64,128]{1,0:T(8,128)(2,1)S(1)} %slice.12), channel_id=1, source_target_pairs={{0,12},{4,8},{8,4},{12,0},{1,13},{5,9},{9,5},{13,1},{2,14},{6,10},... | collective-permute-start | bytes 49160 | tf_op jit(solution)/shard_map/ppermute | solution.py:334
  12.7 10.7 %collective-permute-start.2 = (bf16[64,128]{1,0:T(8,128)(2,1)S(1)}, bf16[64,128]{1,0:T(8,128)(2,1)S(1)}, u32[]{:S(2)}, u32[]{:S(2)}) collective-permute-start(bf16[64,128]{1,0:T(8,128)(2,1)S(1)} %slice.12), channel_id=1, source_target_pairs={{0,8},{4,12},{8,0},{12,4},{1,9},{5,13},{9,1},{13,5},{2,10},{6,14},... | collective-permute-start | bytes 49160 | tf_op jit(solution)/shard_map/ppermute | solution.py:334
  12.8 10.6 %collective-permute-start.1 = (bf16[64,128]{1,0:T(8,128)(2,1)S(1)}, bf16[64,128]{1,0:T(8,128)(2,1)S(1)}, u32[]{:S(2)}, u32[]{:S(2)}) collective-permute-start(bf16[64,128]{1,0:T(8,128)(2,1)S(1)} %slice.12), channel_id=1, source_target_pairs={{0,4},{4,0},{8,12},{12,8},{1,5},{5,1},{9,13},{13,9},{2,6},{6,2},{1... | collective-permute-start | bytes 49160 | tf_op jit(solution)/shard_map/ppermute | solution.py:334
  14.6 16.1 %copy-start.2 = (s32[1,16]{1,0:T(1,128)S(1)}, s32[1,16]{1,0:T(1,128)}, u32[]{:S(2)}) copy-start(s32[1,16]{1,0:T(1,128)} %len_ref.1) | copy-start | bytes 196
  14.6 16.1 %copy-start.3 = (s32[1,16]{1,0:T(1,128)S(1)}, s32[1,16]{1,0:T(1,128)}, u32[]{:S(2)}) copy-start(s32[1,16]{1,0:T(1,128)} %tenant_ref.1) | copy-start | bytes 196
  18.7 6.2 %copy-start = (f32[128,2048]{1,0:T(8,128)}, f32[128,2048]{1,0:T(8,128)S(1)}, u32[]{:S(2)}) copy-start(f32[128,2048]{1,0:T(8,128)S(1)} %get-tuple-element.39.term_ref) | copy-start | bytes 3145732
  23.4 11.5 %collective-permute-start.6 = (bf16[128,2560]{1,0:T(8,128)(2,1)S(1)}, bf16[128,2560]{1,0:T(8,128)(2,1)S(1)}, u32[]{:S(2)}, u32[]{:S(2)}) collective-permute-start(bf16[128,2560]{1,0:T(8,128)(2,1)S(1)} %constant_dynamic-update-slice_fusion.refs_4_.refs_8_), channel_id=1, source_target_pairs={{0,1},{1,0},{2,3},{3,2},{4,5},{5,4},{6,7},{7,6},{8,9},{9,8},{10,11... | collective-permute-start | bytes 1966088 | tf_op jit(solution)/shard_map/ppermute | solution.py:334
  24.9 9.9 %collective-permute-start.8 = (bf16[128,2560]{1,0:T(8,128)(2,1)S(1)}, bf16[128,2560]{1,0:T(8,128)(2,1)S(1)}, u32[]{:S(2)}, u32[]{:S(2)}) collective-permute-start(bf16[128,2560]{1,0:T(8,128)(2,1)S(1)} %collective-permute-done.7.refs_6_.refs_10_), channel_id=1, source_target_pairs={{0,1},{1,0},{2,3},{3,2},{4,5},{5,4},{6,7},{7,6},{8,9},{9,8},{10,11... | collective-permute-start | bytes 1966088 | tf_op jit(solution)/shard_map/ppermute | solution.py:334
  24.9 26.8 %collective-permute-start.9 = (bf16[128,2048]{1,0:T(8,128)(2,1)}, bf16[128,2048]{1,0:T(8,128)(2,1)}, u32[]{:S(2)}, u32[]{:S(2)}) collective-permute-start(bf16[128,2048]{1,0:T(8,128)(2,1)} %add_convert_fusion.1), channel_id=1, source_target_pairs={{0,8},{4,12},{8,0},{12,4},{1,9},{5,13},{9,1},{13,5},{2,10},{6,14},... | collective-permute-start | bytes 1572872 | tf_op jit(solution)/shard_map/ppermute | solution.py:334
  27.6 25.3 %collective-permute-start.10 = (bf16[128,2048]{1,0:T(8,128)(2,1)S(1)}, bf16[128,2048]{1,0:T(8,128)(2,1)}, u32[]{:S(2)}, u32[]{:S(2)}) collective-permute-start(bf16[128,2048]{1,0:T(8,128)(2,1)S(1)} %get-tuple-element.48), channel_id=1, source_target_pairs={{0,4},{4,0},{8,12},{12,8},{1,5},{5,1},{9,13},{13,9},{2,6},{6,2},{1... | collective-permute-start | bytes 1572872 | tf_op jit(solution)/shard_map/ppermute | solution.py:334
  28.0 1.2 %collective-permute-start.4 = (bf16[80,128]{1,0:T(8,128)(2,1)S(1)}, bf16[80,128]{1,0:T(8,128)(2,1)S(1)}, u32[]{:S(2)}, u32[]{:S(2)}) collective-permute-start(bf16[80,128]{1,0:T(8,128)(2,1)S(1)} %pad_maximum_fusion.1.sums_ref.refs_0_), channel_id=1, source_target_pairs={{0,1},{1,0},{2,3},{3,2},{4,5},{5,4},{6,7},{7,6},{8,9},{9,8},{10,11... | collective-permute-start | bytes 61448 | tf_op jit(solution)/shard_map/ppermute | solution.py:334
  29.2 5.6 %collective-permute-start.5 = (bf16[160,128]{1,0:T(8,128)(2,1)S(1)}, bf16[160,128]{1,0:T(8,128)(2,1)S(1)}, u32[]{:S(2)}, u32[]{:S(2)}) collective-permute-start(bf16[160,128]{1,0:T(8,128)(2,1)S(1)} %pad_maximum_fusion), channel_id=1, source_target_pairs={{0,2},{1,3},{2,0},{3,1},{4,6},{5,7},{6,4},{7,5},{8,10},{9,11},{10,... | collective-permute-start | bytes 122888 | tf_op jit(solution)/shard_map/ppermute | solution.py:334
  30.7 1.2 %copy-start.1 = (f32[128,2048]{1,0:T(8,128)S(1)}, f32[128,2048]{1,0:T(8,128)}, u32[]{:S(2)}) copy-start(f32[128,2048]{1,0:T(8,128)} %copy-done) | copy-start | bytes 3145732

commit v3 on v2

--- a/solution.py
+++ b/solution.py
@@ -9,7 +9,7 @@
 
 ADAPTER_SCALE = 2.0
 LOSS_UNSCALE = 0.125
-VMEM_BYTES = 48 * 1024 * 1024
+VMEM_BYTES = 20 * 1024 * 1024
 COST = pl.CostEstimate(flops=0, bytes_accessed=0, transcendentals=0)
 
 f32 = jnp.float32
@@ -44,13 +44,15 @@
     ]
 
 
-def frozen_kernel(gk_hbm, gv_hbm, wk_hbm, wv_hbm, *refs):
-    *outs, gk, gv, wk, wv, sems = refs
-    width = outs[0].shape[1]
+def frozen_kernel(
+    first_ref, gk_hbm, gv_hbm, wk_hbm, wv_hbm, x2a_ref, x2b_ref, x1_ref, own_ref,
+    gk, gv, wk, wv, sems,
+):
+    rows, width = x1_ref.shape
     z = lax.axis_index("tensor")
     head = [
-        pltpu.make_async_copy(gk_hbm, gk, sems.at[len(outs), 0]),
-        pltpu.make_async_copy(gv_hbm, gv, sems.at[len(outs), 1]),
+        pltpu.make_async_copy(gk_hbm, gk, sems.at[3, 0]),
+        pltpu.make_async_copy(gv_hbm, gv, sems.at[3, 1]),
     ]
     body = [
         frozen_copies(block, width, wk_hbm, wv_hbm, wk.at[n], wv.at[n], sems.at[n])
@@ -59,35 +61,63 @@
     for copies in (head, *body):
         for copy in copies:
             copy.start()
-    for copy in head:
-        copy.wait()
-    for n, out in enumerate(outs):
+    ahead = x2a_ref.shape[1] - rows
+    x2a_ref[:, ahead:] = first_ref[:, ahead:].astype(f32)
+    for copy in head + body[0]:
+        copy.wait()
+    x2a_ref[:, :ahead] = frozen_part(gk[...], gv[...], wk[0, :ahead], wv[0, :ahead])
+    x2b_ref[...] = frozen_part(gk[...], gv[...], wk[0, ahead:], wv[0, ahead:])
+    for n, out in ((1, x1_ref), (2, own_ref)):
         for copy in body[n]:
             copy.wait()
         out[...] = frozen_part(gk[...], gv[...], wk[n], wv[n]).astype(out.dtype)
 
 
-def frozen_blocks(gk, gv, wk, wv, width, dtypes):
+def frozen_blocks(first_part, gk, gv, wk, wv, width):
     rows, feats = gk.shape
-    count = len(dtypes)
     hbm = pl.BlockSpec(memory_space=pltpu.HBM)
     vmem = pl.BlockSpec(memory_space=pltpu.VMEM)
     return pl.pallas_call(
         frozen_kernel,
-        in_specs=[hbm] * 4,
-        out_specs=[vmem] * count,
-        out_shape=[jax.ShapeDtypeStruct((rows, width), dtype) for dtype in dtypes],
+        in_specs=[vmem] + [hbm] * 4,
+        out_specs=[vmem] * 4,
+        out_shape=[
+            jax.ShapeDtypeStruct(first_part.shape, f32),
+            jax.ShapeDtypeStruct((rows, width + rows - first_part.shape[1]), f32),
+            jax.ShapeDtypeStruct((rows, width), bf16),
+            jax.ShapeDtypeStruct((rows, width), f32),
+        ],
         scratch_shapes=[
             pltpu.VMEM((rows, feats), bf16),
             pltpu.VMEM((rows, feats), bf16),
-            pltpu.VMEM((count, width, feats), bf16),
-            pltpu.VMEM((count, width, feats), bf16),
-            pltpu.SemaphoreType.DMA((count + 1, 2)),
+            pltpu.VMEM((3, width, feats), bf16),
+            pltpu.VMEM((3, width, feats), bf16),
+            pltpu.SemaphoreType.DMA((4, 2)),
         ],
         compiler_params=params(),
         cost_estimate=COST,
         name="frozen_blocks",
-    )(gk, gv, wk, wv)
+    )(first_part, gk, gv, wk, wv)
+
+
+def finish_kernel(own_ref, x1_ref, x2b_ref, out_ref):
+    ahead = own_ref.shape[1] - x2b_ref.shape[1]
+    total = own_ref[...] + x1_ref[...].astype(f32)
+    out_ref[:, :ahead] = total[:, :ahead].astype(bf16)
+    out_ref[:, ahead:] = (total[:, ahead:] + x2b_ref[...].astype(f32)).astype(bf16)
+
+
+def finish(own, x1, x2b):
+    vmem = pl.BlockSpec(memory_space=pltpu.VMEM)
+    return pl.pallas_call(
+        finish_kernel,
+        in_specs=[vmem] * 3,
+        out_specs=vmem,
+        out_shape=jax.ShapeDtypeStruct(own.shape, bf16),
+        compiler_params=params(),
+        cost_estimate=COST,
+        name="finish",
+    )(own, x1, x2b)
 
 
 def segment_masks(len_ref, shape, segments):
@@ -103,9 +133,13 @@
 
 def first_kernel(
     frozen, len_hbm, tenant_hbm, slot_hbm, tok_hbm, gk_hbm, gv_hbm, kd_hbm, vd_hbm, ku_hbm, vu_hbm,
-    wk_hbm, wv_hbm, out_ref, term_ref, len_ref, tenant_ref, slot_ref, tok, gk, gv, down, key_up,
-    value_up, wk, wv, products, sems,
+    wk_hbm, wv_hbm, out_ref, slots_ref, *refs,
 ):
+    if frozen:
+        last_ref, *refs = refs
+    (
+        len_ref, tenant_ref, slot_ref, tok, gk, gv, down, key_up, value_up, wk, wv, products, sems,
+    ) = refs
     segments = tenant_ref.shape[1]
     rank = kd_hbm.shape[1]
     rows, width = tok.shape
@@ -146,7 +180,13 @@
     for k in range(segments):
         slot = slot_ref[tenant_ref[0, k]].astype(f32)
         slot_of = jnp.where(masks[k], slot, slot_of)
-    out_ref[4 * rank :, :] = slot_of.astype(bf16)
+    slots_ref[...] = slot_of.astype(bf16)
+    ahead = out_ref.shape[1] - rows
+    if frozen:
+        out_ref[4 * rank :, ahead:] = jnp.zeros((rows - 4 * rank, rows), bf16)
+
+    def put(at, values):
+        out_ref[at * rank : (at + 1) * rank, ahead:] = values
 
     def fold(take):
         total = jnp.zeros((rank, rows), f32)
@@ -160,19 +200,18 @@
     for copy in grads + weights:
         copy.wait()
     if frozen:
-        term_ref[...] = frozen_part(gk[...], gv[...], wk[...], wv[...]).astype(term_ref.dtype)
+        out_ref[:, :ahead] = frozen_part(gk[...], gv[...], wk[:ahead], wv[:ahead]).astype(bf16)
+        last_ref[...] = frozen_part(gk[...], gv[...], wk[ahead:], wv[ahead:]).astype(bf16)
     for copy in ups:
         copy.wait()
     for at, up, grad in ((2, key_up, gk), (3, value_up, gv)):
         products[...] = dot_nt(up[...].reshape(products.shape[0], up.shape[2]), grad[...])
-        out_ref[at * rank : (at + 1) * rank, :] = fold(by_tenant)
+        put(at, fold(by_tenant))
     for copy in downs:
         copy.wait()
     both = dot_nt(down[...], tok[...])
     for at in (0, 1):
-        out_ref[at * rank : (at + 1) * rank, :] = fold(
-            lambda k: both[at * half + k * rank : at * half + (k + 1) * rank]
-        )
+        put(at, fold(lambda k: both[at * half + k * rank : at * half + (k + 1) * rank]))
 
 
 def first_products(frozen, tokens, gk, gv, kd, vd, ku, vu, wk, wv, lengths, tenants, slots):
@@ -183,15 +222,15 @@
     both = 2 * segments * rank
     hbm = pl.BlockSpec(memory_space=pltpu.HBM)
     vmem = pl.BlockSpec(memory_space=pltpu.VMEM)
-    term = (rows, width) if frozen else (16, 128)
+    shapes = [(4 * rank, rows), (rank, rows)]
+    if frozen:
+        ahead = width * 5 // 16
+        shapes = [(rows, ahead + rows), (rank, rows), (rows, width - ahead)]
     return pl.pallas_call(
         functools.partial(first_kernel, frozen),
         in_specs=[hbm] * 12,
-        out_specs=[vmem, vmem],
-        out_shape=[
-            jax.ShapeDtypeStruct((5 * rank, rows), bf16),
-            jax.ShapeDtypeStruct(term, bf16),
-        ],
+        out_specs=[vmem] * len(shapes),
+        out_shape=[jax.ShapeDtypeStruct(shape, bf16) for shape in shapes],
         scratch_shapes=[
             pltpu.SMEM(lengths.shape, jnp.int32),
             pltpu.SMEM(tenants.shape, jnp.int32),
@@ -214,8 +253,11 @@
 
 
 def adapter_kernel(
-    len_ref, tenant_ref, sums_ref, term_ref, kd_hbm, vd_hbm, out_ref, down, back, sems
+    frozen, len_ref, tenant_ref, sums_ref, term_ref, *refs
 ):
+    if frozen:
+        ahead_ref, *refs = refs
+    kd_hbm, vd_hbm, out_ref, down, back, sems = refs
     segments = tenant_ref.shape[1]
     rank = kd_hbm.shape[1]
     rows = out_ref.shape[0]
@@ -237,11 +279,15 @@
             back[start : start + rank, :] = jnp.where(masks[k], values, 0.0).astype(bf16)
     for copy in copies:
         copy.wait()
-    out_ref[...] = term_ref[...] + dot_tn(back[...], down[...])
-
-
-def add_adapters(term, sums, kd, vd, lengths, tenants):
-    rows, width = term.shape
+    total = term_ref[...] + dot_tn(back[...], down[...])
+    out_ref[...] = total
+    if frozen:
+        ahead = ahead_ref.shape[1] - rows
+        out_ref[:, :ahead] = total[:, :ahead] + ahead_ref[:, :ahead].astype(f32)
+
+
+def add_adapters(terms, sums, kd, vd, lengths, tenants):
+    rows, width = terms[0].shape
     segments = tenants.shape[1]
     rank = kd.shape[1]
     both = 2 * segments * rank
@@ -249,8 +295,8 @@
     vmem = pl.BlockSpec(memory_space=pltpu.VMEM)
     hbm = pl.BlockSpec(memory_space=pltpu.HBM)
     return pl.pallas_call(
-        adapter_kernel,
-        in_specs=[smem, smem, vmem, vmem, hbm, hbm],
+        functools.partial(adapter_kernel, len(terms) > 1),
+        in_specs=[smem, smem, vmem] + [vmem] * len(terms) + [hbm, hbm],
         out_specs=vmem,
         out_shape=jax.ShapeDtypeStruct((rows, width), f32),
         scratch_shapes=[
@@ -261,7 +307,7 @@
         compiler_params=params(),
         cost_estimate=COST,
         name="add_adapters",
-    )(lengths, tenants, sums, term, kd, vd)
+    )(lengths, tenants, sums, *terms, kd, vd)
 
 
 def grads_kernel(count, rank, per_owner, first_ref, *refs):
@@ -349,40 +395,43 @@
     large = [in_hbm(array) for array in (gk, gv, wk, wv)]
     halving = n_tensor == 4
 
-    part, x0 = first_products(
+    first_part, slot_rows, *second = first_products(
         halving, in_hbm(tokens), large[0], large[1], kd, vd, in_hbm(ku), in_hbm(vu), *large[2:],
         in_hbm(segment_length), in_hbm(segment_tenant), in_hbm(adapter_output_slot),
     )
-    products, slot_rows = part[: 4 * rank], part[4 * rank :]
+    tokens, first_part, *second = lax.optimization_barrier((tokens, first_part, *second))
+    sent = jnp.concatenate([tokens, gk, gv], axis=1)
     if halving:
-        r1 = swap(x0, "tensor", 1, 4)
-        others = [swap(products, "tensor", bit, 4) for bit in (1, 2, 3)]
-        tokens, wk, x0 = lax.optimization_barrier((tokens, wk, x0))
-        sent = jnp.concatenate([tokens, gk, gv], axis=1)
-        x2, x1, own = frozen_blocks(large[0], large[1], in_hbm(wk), large[3], width, (f32, bf16, f32))
-        x2, x1, r1, *others = lax.optimization_barrier((x2, x1, r1, *others))
-        x2 = (x2 + r1.astype(f32)).astype(bf16)
-        r3 = swap(x2, "tensor", 2, 4)
-        total = products.astype(f32)
-        for other in others:
-            total = total + other.astype(f32)
+        ahead = first_part.shape[1] - rows
+        r1a = swap(first_part, "tensor", 1, 4)
+        r1b = swap(second[0], "tensor", 1, 4)
+        x2a, x2b, x1, own = frozen_blocks(first_part, *large, width)
+        x2a, r1a = lax.optimization_barrier((x2a, r1a))
+        x2a = (x2a + r1a.astype(f32)).astype(bf16)
+        r3a = swap(x2a, "tensor", 2, 4)
+        x2b, x1, r1b = lax.optimization_barrier((x2b, x1, r1b))
+        x2b = (x2b + r1b.astype(f32)).astype(bf16)
+        r3b = swap(x2b, "tensor", 2, 4)
+        r4 = swap(x1, "tensor", 1, 4)
+        x2b, r3a, x2a = lax.optimization_barrier((x2b, r3a, x2a))
+        total = x2a[: 4 * rank, ahead:].astype(f32) + r3a[: 4 * rank, ahead:].astype(f32)
+        terms = [own, r3a]
     else:
-        sent = jnp.concatenate([tokens, gk, gv], axis=1)
-        total = lax.psum(products.astype(f32), "tensor")
+        total = lax.psum(first_part.astype(f32), "tensor")
         term = dot_nt(gk, wk) + dot_nt(gv, wv)
-        own = lax.psum_scatter(
-            term.astype(bf16), "tensor", scatter_dimension=1, tiled=True
-        ).astype(f32)
+        terms = [
+            lax.psum_scatter(
+                term.astype(bf16), "tensor", scatter_dimension=1, tiled=True
+            ).astype(f32)
+        ]
     sums = jnp.concatenate([total.astype(bf16), slot_rows], axis=0)
-    if halving:
-        x1, sums = lax.optimization_barrier((x1, sums))
-        r4 = swap(x1, "tensor", 1, 4)
 
     if n_dp == 4:
         sent_across, sent_core = swap(sent, "dp", 2, 4), swap(sent, "dp", 1, 4)
         pair = jnp.concatenate([sums, swap(sums, "dp", 1, 4)], axis=0)
         pairs = [pair, swap(pair, "dp", 2, 4)]
-        all_sums = [half[n * sums.shape[0] : (n + 1) * sums.shape[0]] for half in pairs for n in (0, 1)]
+        size = sums.shape[0]
+        all_sums = [two[n * size : (n + 1) * size] for two in pairs for n in (0, 1)]
         all_sent = [sent, sent_core, sent_across, swap(sent_across, "dp", 1, 4)]
     else:
         gathered = lax.all_gather(sent, "dp")
@@ -390,12 +439,13 @@
         gathered = lax.all_gather(sums, "dp")
         all_sums = [gathered[i] for i in range(n_dp)]
 
-    own = add_adapters(own, sums, kd, vd, segment_length, segment_tenant)
+    own = add_adapters(terms, sums, kd, vd, segment_length, segment_tenant)
     grads = adapter_grads(first, all_sums, all_sent, rank, per_owner, width, feats)
     if halving:
         own, *grads = lax.optimization_barrier((own, *grads))
-        own = own + r3.astype(f32) + r4.astype(f32)
-    input_gradient = own.astype(bf16)
+        input_gradient = finish(own, r4, r3b)
+    else:
+        input_gradient = own.astype(bf16)
     return (input_gradient, *grads)
 
 

time: 55.4 us -> 47.9 us (0.86)
  waiting for transfers between devices: 20.5 us -> 11.9 us
  local copies, waits for them, and re-layouts: 1.31 us -> 3.66 us
  other arithmetic: 3.13 us -> 1.47 us
  Pallas kernels: 15.8 us -> 16.6 us
    ppermute x11 -> x10, waiting for transfers between devices: 20.5 us -> 11.9 us  [swap(): return lax.ppermute(values, axis, [(i, i ^ bit) for i in range(size)])]
    convert_element_type x2, other arithmetic: 3.11 us -> 0.84 us  [the longest x1 0.8 us: local(): x2b = (x2b + r1b.astype(f32)).astype(bf16)]
    unnamed x16 -> x20, local copies, waits for them, and re-layouts: 1.3 us -> 2.9 us
    pallas_call x2 -> x3, Pallas kernels: 6.99 us -> 7.89 us  [the longest x1 4.06 us: frozen_blocks(): pl.pallas_call(frozen_kernel, in_specs=[vmem] + [hbm] * 4, out_specs=[vme...]
    slice x3 -> x1, local copies, waits for them, and re-layouts: 0.01 us -> 0.75 us  [local(): all_sums = [two[n * size:(n + 1) * size] for two in pairs for n in (0, 1)]]
    concatenate x1, other arithmetic: 0.01 us -> 0.62 us  [local(): pair = jnp.concatenate([sums, swap(sums, 'dp', 1, 4)], axis=0)]
    ppermute x11 -> x10, starting transfers between devices: 13.6 us -> 13.2 us  [swap(): return lax.ppermute(values, axis, [(i, i ^ bit) for i in range(size)])]
  transfers between devices with their start and end apart: 11 -> 10, of which waited for: 5 -> 2; matrix products, arithmetic and copies ran while one was open for 2% -> 5% of each run, Pallas kernels for 20% -> 23%
where the time goes in v3:
time: 47.9 us; the launch traced here: 47.6 us
  Pallas kernels  16.6 us (35%)
  starting transfers between devices  13.2 us (28%)
  waiting for transfers between devices  11.9 us (25%)
  local copies, waits for them, and re-layouts  3.66 us (8%)
  other arithmetic  1.47 us (3%)
  between operations  0.81 us (2%)
    ppermute x10, starting transfers between devices, swap(): return lax.ppermute(values, axis, [(i, i ^ bit) for i in range(size)])  13.2 us
    ppermute x10, waiting for transfers between devices, swap(): return lax.ppermute(values, axis, [(i, i ^ bit) for i in range(size)])  11.9 us
    pallas_call x1, Pallas kernels, first_products(): pl.pallas_call(functools.partial(first_kernel, frozen), in_specs=[hbm] *...  4.73 us
    pallas_call x1, Pallas kernels, frozen_blocks(): pl.pallas_call(frozen_kernel, in_specs=[vmem] + [hbm] * 4, out_specs=[vme...  4.06 us
    pallas_call x1, Pallas kernels, adapter_grads(): pl.pallas_call(functools.partial(grads_kernel, count, rank, per_owner), g...  3.99 us
    unnamed x20, local copies, waits for them, and re-layouts  2.9 us
    pallas_call x1, Pallas kernels, add_adapters(): pl.pallas_call(functools.partial(adapter_kernel, len(terms) > 1), in_spec...  2.87 us
    pallas_call x1, Pallas kernels, finish(): pl.pallas_call(finish_kernel, in_specs=[vmem] * 3, out_specs=vmem, out_sh...  0.97 us
  transfers between devices with their start and end apart: 10, of which 2 were waited for; matrix products, arithmetic and copies ran while one was open for 5% of the time, Pallas kernels for 23%

profile of v3, /device:TPU:0, one launch (start us, length us, event | category | flops | bytes accessed | tf_op | source)
XLA Modules:
  0.0 47.6 jit_solution(13400046653324463440)
XLA Ops:
  0.6 0.0 copy-start.8
  0.6 0.0 copy-start.7
  0.7 4.7 %first_products.1 = (bf16[128,768]{1,0:T(8,128)(2,1)S(1)}, bf16[16,128]{1,0:T(8,128)(2,1)S(1)}, bf16[128,1408]{1,0:T(8,128)(2,1)S(1)}) custom-call(s32[1,16]{1,0:T(1,128)} %len_ref.1, s32[1,16]{1,0:T(1,128)} %tenant_ref.1, s32[64]{0:T(128)} %slot_hbm.1, bf16[128,2048]{1,0:T(8,128)(2,1)} %tok_hbm.1, bf16[128,256]{1,0:T(8,128)(2,1)} %gk_hbm.3, ...), custom_call_target="tpu_custom_call" | custom-call | tf_op jit(solution)/shard_map/first_products/pallas_call | solution.py:229
  5.4 3.1 %collective-permute-start.1 = (bf16[128,768]{1,0:T(8,128)(2,1)S(1)}, bf16[128,768]{1,0:T(8,128)(2,1)S(1)}, u32[]{:S(2)}, u32[]{:S(2)}) collective-permute-start(bf16[128,768]{1,0:T(8,128)(2,1)S(1)} %get-tuple-element.33.first_ref), channel_id=1, source_target_pairs={{0,4},{4,0},{8,12},{12,8},{1,5},{5,1},{9,13},{13,9},{2,6},{6,2},{1... | collective-permute-start | bytes 589832 | tf_op jit(solution)/shard_map/ppermute | solution.py:380
  8.5 0.1 collective-permute-start
  8.7 0.0 copy-start.4
  8.7 0.0 copy-start.5
  8.7 1.9 %collective-permute-start.6 = (bf16[128,2560]{1,0:T(8,128)(2,1)S(1)}, bf16[128,2560]{1,0:T(8,128)(2,1)S(1)}, u32[]{:S(2)}, u32[]{:S(2)}) collective-permute-start(bf16[128,2560]{1,0:T(8,128)(2,1)S(1)} %constant_dynamic-update-slice_fusion.refs_4_.refs_8_), channel_id=1, source_target_pairs={{0,2},{1,3},{2,0},{3,1},{4,6},{5,7},{6,4},{7,5},{8,10},{9,11},{10,... | collective-permute-start | bytes 1966088 | tf_op jit(solution)/shard_map/ppermute | solution.py:380
  10.6 4.1 %frozen_blocks.1 = (f32[128,768]{1,0:T(8,128)S(1)}, f32[128,1408]{1,0:T(8,128)S(1)}, bf16[128,2048]{1,0:T(8,128)(2,1)}, f32[128,2048]{1,0:T(8,128)S(1)}) custom-call(bf16[128,768]{1,0:T(8,128)(2,1)S(1)} %get-tuple-element.33.first_ref, bf16[128,256]{1,0:T(8,128)(2,1)} %gk_hbm.3, bf16[128,256]{1,0:T(8,128)(2,1)} %gv_hbm.3, bf16[8192,256]{1,0:T(8,128)(2,1)} %wk_hbm.3, ...), custom_call_target="tpu_custom_call" | custom-call | tf_op jit(solution)/shard_map/frozen_blocks/pallas_call | solution.py:80
  14.7 0.0 copy-start
  14.7 0.0 collective-permute-done.1
  14.8 2.7 %collective-permute-start.2 = (bf16[128,768]{1,0:T(8,128)(2,1)S(1)}, bf16[128,768]{1,0:T(8,128)(2,1)S(1)}, u32[]{:S(2)}, u32[]{:S(2)}) collective-permute-start(bf16[128,768]{1,0:T(8,128)(2,1)S(1)} %add_convert_fusion.1), channel_id=1, source_target_pairs={{0,8},{4,12},{8,0},{12,4},{1,9},{5,13},{9,1},{13,5},{2,10},{6,14},... | collective-permute-start | bytes 589832 | tf_op jit(solution)/shard_map/ppermute | solution.py:380
  17.4 7.9 %collective-permute-done = bf16[128,1408]{1,0:T(8,128)(2,1)S(1)} collective-permute-done((bf16[128,1408]{1,0:T(8,128)(2,1)S(1)}, bf16[128,1408]{1,0:T(8,128)(2,1)S(1)}, u32[]{:S(2)}, u32[]{:S(2)}) %collective-permute-start) | collective-permute-done | bytes 360480 | tf_op jit(solution)/shard_map/ppermute | solution.py:380
  25.3 0.0 collective-permute-start.8
  25.3 0.8 %add_convert_fusion = bf16[128,1408]{1,0:T(8,128)(2,1)} fusion(f32[128,1408]{1,0:T(8,128)S(1)} %get-tuple-element.37, bf16[128,1408]{1,0:T(8,128)(2,1)S(1)} %collective-permute-done), kind=kLoop, calls=%fused_computation | loop fusion | flops 540672 | bytes 1441792 | tf_op jit(solution)/shard_map/convert_element_type | solution.py:413
  26.1 0.0 collective-permute-done.2.refs_0_
  26.1 0.0 collective-permute-done.6.refs_6_.refs_10_
  26.1 0.1 collective-permute-start.7
  26.2 0.0 copy-start.2
  26.3 0.7 %copy-done.2 = bf16[128,768]{1,0:T(8,128)(2,1)} copy-done((bf16[128,768]{1,0:T(8,128)(2,1)}, bf16[128,768]{1,0:T(8,128)(2,1)S(1)}, u32[]{:S(2)}) %copy-start.2) | copy-done | bytes 196632
  26.9 0.5 %collective-permute-start.3 = (bf16[80,128]{1,0:T(8,128)(2,1)S(1)}, bf16[80,128]{1,0:T(8,128)(2,1)S(1)}, u32[]{:S(2)}, u32[]{:S(2)}) collective-permute-start(bf16[80,128]{1,0:T(8,128)(2,1)S(1)} %pad_maximum_fusion.1.sums_ref.refs_0_), channel_id=1, source_target_pairs={{0,1},{1,0},{2,3},{3,2},{4,5},{5,4},{6,7},{7,6},{8,9},{9,8},{10,11... | collective-permute-start | bytes 61448 | tf_op jit(solution)/shard_map/ppermute | solution.py:380
  27.4 2.4 %collective-permute-start.9 = (bf16[128,1408]{1,0:T(8,128)(2,1)}, bf16[128,1408]{1,0:T(8,128)(2,1)S(1)}, u32[]{:S(2)}, u32[]{:S(2)}) collective-permute-start(bf16[128,1408]{1,0:T(8,128)(2,1)} %add_convert_fusion), channel_id=1, source_target_pairs={{0,8},{4,12},{8,0},{12,4},{1,9},{5,13},{9,1},{13,5},{2,10},{6,14},... | collective-permute-start | bytes 1081352 | tf_op jit(solution)/shard_map/ppermute | solution.py:380
  29.8 0.0 collective-permute-done.3.refs_1_
  29.8 0.6 %pad_maximum_fusion = bf16[160,128]{1,0:T(8,128)(2,1)} fusion(bf16[80,128]{1,0:T(8,128)(2,1)S(1)} %collective-permute-done.3.refs_1_, bf16[16,128]{1,0:T(8,128)(2,1)S(1)} %get-tuple-element.44, bf16[64,128]{1,0:T(8,128)(2,1)S(1)} %add_convert_fusion.2), kind=kLoop, calls=%fused_computation.2 | loop fusion | flops 122880 | bytes 81920 | tf_op jit(solution)/shard_map/concatenate | solution.py:431
  30.4 2.5 %collective-permute-start.4 = (bf16[160,128]{1,0:T(8,128)(2,1)}, bf16[160,128]{1,0:T(8,128)(2,1)}, u32[]{:S(2)}, u32[]{:S(2)}) collective-permute-start(bf16[160,128]{1,0:T(8,128)(2,1)} %pad_maximum_fusion), channel_id=1, source_target_pairs={{0,2},{1,3},{2,0},{3,1},{4,6},{5,7},{6,4},{7,5},{8,10},{9,11},{10,... | collective-permute-start | bytes 122888 | tf_op jit(solution)/shard_map/ppermute | solution.py:380
  32.9 1.2 %copy-done.1 = f32[128,2048]{1,0:T(8,128)S(1)} copy-done((f32[128,2048]{1,0:T(8,128)S(1)}, f32[128,2048]{1,0:T(8,128)}, u32[]{:S(2)}) %copy-start.1) | copy-done | bytes 1048600
  34.1 0.9 %copy-done.3 = bf16[128,768]{1,0:T(8,128)(2,1)S(1)} copy-done((bf16[128,768]{1,0:T(8,128)(2,1)S(1)}, bf16[128,768]{1,0:T(8,128)(2,1)}, u32[]{:S(2)}) %copy-start.3) | copy-done | bytes 196632
  35.1 2.9 %add_adapters.1.own_ref = f32[128,2048]{1,0:T(8,128)S(1)} custom-call(s32[1,16]{1,0:T(1,128)S(1)} %copy-done.4, s32[1,16]{1,0:T(1,128)S(1)} %copy-done.5, bf16[80,128]{1,0:T(8,128)(2,1)S(1)} %pad_maximum_fusion.1.sums_ref.refs_0_, f32[128,2048]{1,0:T(8,128)S(1)} %copy-done.1, bf16[128,768]{1,0:T(8,128)(2,1)S(1)} %copy-done.3, bf16[64,16,2048]{2,1,0:T(8,128)(2,1)} %refs_1_.1, ...), custom_call_target="tpu_custom_call" | custom-call | tf_op jit(solution)/shard_map/add_adapters/pallas_call | solution.py:297
  37.9 0.8 %fusion = (bf16[80,128]{1,0:T(8,128)(2,1)S(1)}, bf16[80,128]{1,0:T(8,128)(2,1)S(1)}) fusion(bf16[160,128]{1,0:T(8,128)(2,1)} %collective-permute-done.4), kind=kLoop, calls=%fused_computation.8 | loop fusion | bytes 81920 | tf_op jit(solution)/shard_map/slice | solution.py:434
  38.7 4.0 %adapter_grads.1 = (f32[16,16,2048]{2,1,0:T(8,128)}, f32[16,16,2048]{2,1,0:T(8,128)}, f32[16,16,256]{2,1,0:T(8,128)}, f32[16,16,256]{2,1,0:T(8,128)}) custom-call(s32[1]{0:T(128)} %bitcast.first_ref, bf16[80,128]{1,0:T(8,128)(2,1)S(1)} %pad_maximum_fusion.1.sums_ref.refs_0_, bf16[80,128]{1,0:T(8,128)(2,1)S(1)} %collective-permute-done.3.refs_1_, ...), custom_call_target="tpu_custom_call" | custom-call | tf_op jit(solution)/shard_map/adapter_grads/pallas_call | solution.py:358
  42.7 3.9 %collective-permute-done.9.x2b_ref = bf16[128,1408]{1,0:T(8,128)(2,1)S(1)} collective-permute-done((bf16[128,1408]{1,0:T(8,128)(2,1)}, bf16[128,1408]{1,0:T(8,128)(2,1)S(1)}, u32[]{:S(2)}, u32[]{:S(2)}) %collective-permute-start.9) | collective-permute-done | bytes 360480 | tf_op jit(solution)/shard_map/ppermute | solution.py:380
  46.6 1.0 %finish.1 = bf16[128,2048]{1,0:T(8,128)(2,1)} custom-call(f32[128,2048]{1,0:T(8,128)S(1)} %add_adapters.1.own_ref, bf16[128,2048]{1,0:T(8,128)(2,1)S(1)} %collective-permute-done.8.x1_ref, bf16[128,1408]{1,0:T(8,128)(2,1)S(1)} %collective-permute-done.9.x2b_ref), custom_call_target="tpu_custom_call" | custom-call | tf_op jit(solution)/shard_map/finish/pallas_call | solution.py:112
  (20 shorter events, 0.1 us)
Async XLA Ops:
  0.6 8.0 %copy-start.8 = (bf16[128,256]{1,0:T(8,128)(2,1)S(1)}, bf16[128,256]{1,0:T(8,128)(2,1)}, u32[]{:S(2)}) copy-start(bf16[128,256]{1,0:T(8,128)(2,1)} %gv_hbm.3) | copy-start | bytes 196612
  0.6 8.0 %copy-start.7 = (bf16[128,256]{1,0:T(8,128)(2,1)S(1)}, bf16[128,256]{1,0:T(8,128)(2,1)}, u32[]{:S(2)}) copy-start(bf16[128,256]{1,0:T(8,128)(2,1)} %gk_hbm.3) | copy-start | bytes 196612
  0.7 7.9 %copy-start.6 = (bf16[128,2048]{1,0:T(8,128)(2,1)S(1)}, bf16[128,2048]{1,0:T(8,128)(2,1)}, u32[]{:S(2)}) copy-start(bf16[128,2048]{1,0:T(8,128)(2,1)} %tok_hbm.1) | copy-start | bytes 1572868
  5.4 9.3 %collective-permute-start.1 = (bf16[128,768]{1,0:T(8,128)(2,1)S(1)}, bf16[128,768]{1,0:T(8,128)(2,1)S(1)}, u32[]{:S(2)}, u32[]{:S(2)}) collective-permute-start(bf16[128,768]{1,0:T(8,128)(2,1)S(1)} %get-tuple-element.33.first_ref), channel_id=1, source_target_pairs={{0,4},{4,0},{8,12},{12,8},{1,5},{5,1},{9,13},{13,9},{2,6},{6,2},{1... | collective-permute-start | bytes 589832 | tf_op jit(solution)/shard_map/ppermute | solution.py:380
  8.5 16.8 %collective-permute-start = (bf16[128,1408]{1,0:T(8,128)(2,1)S(1)}, bf16[128,1408]{1,0:T(8,128)(2,1)S(1)}, u32[]{:S(2)}, u32[]{:S(2)}) collective-permute-start(bf16[128,1408]{1,0:T(8,128)(2,1)S(1)} %get-tuple-element.36), channel_id=1, source_target_pairs={{0,4},{4,0},{8,12},{12,8},{1,5},{5,1},{9,13},{13,9},{2,6},{6,2},{1... | collective-permute-start | bytes 1081352 | tf_op jit(solution)/shard_map/ppermute | solution.py:380
  8.7 24.2 %copy-start.4 = (s32[1,16]{1,0:T(1,128)S(1)}, s32[1,16]{1,0:T(1,128)}, u32[]{:S(2)}) copy-start(s32[1,16]{1,0:T(1,128)} %len_ref.1) | copy-start | bytes 196
  8.7 24.2 %copy-start.5 = (s32[1,16]{1,0:T(1,128)S(1)}, s32[1,16]{1,0:T(1,128)}, u32[]{:S(2)}) copy-start(s32[1,16]{1,0:T(1,128)} %tenant_ref.1) | copy-start | bytes 196
  8.7 17.5 %collective-permute-start.6 = (bf16[128,2560]{1,0:T(8,128)(2,1)S(1)}, bf16[128,2560]{1,0:T(8,128)(2,1)S(1)}, u32[]{:S(2)}, u32[]{:S(2)}) collective-permute-start(bf16[128,2560]{1,0:T(8,128)(2,1)S(1)} %constant_dynamic-update-slice_fusion.refs_4_.refs_8_), channel_id=1, source_target_pairs={{0,2},{1,3},{2,0},{3,1},{4,6},{5,7},{6,4},{7,5},{8,10},{9,11},{10,... | collective-permute-start | bytes 1966088 | tf_op jit(solution)/shard_map/ppermute | solution.py:380
  10.6 28.1 %collective-permute-start.5 = (bf16[128,2560]{1,0:T(8,128)(2,1)S(1)}, bf16[128,2560]{1,0:T(8,128)(2,1)S(1)}, u32[]{:S(2)}, u32[]{:S(2)}) collective-permute-start(bf16[128,2560]{1,0:T(8,128)(2,1)S(1)} %constant_dynamic-update-slice_fusion.refs_4_.refs_8_), channel_id=1, source_target_pairs={{0,1},{1,0},{2,3},{3,2},{4,5},{5,4},{6,7},{7,6},{8,9},{9,8},{10,11... | collective-permute-start | bytes 1966088 | tf_op jit(solution)/shard_map/ppermute | solution.py:380
  14.7 11.5 %copy-start = (f32[128,2048]{1,0:T(8,128)}, f32[128,2048]{1,0:T(8,128)S(1)}, u32[]{:S(2)}) copy-start(f32[128,2048]{1,0:T(8,128)S(1)} %get-tuple-element.45.term_ref) | copy-start | bytes 3145732
  14.8 11.4 %collective-permute-start.2 = (bf16[128,768]{1,0:T(8,128)(2,1)S(1)}, bf16[128,768]{1,0:T(8,128)(2,1)S(1)}, u32[]{:S(2)}, u32[]{:S(2)}) collective-permute-start(bf16[128,768]{1,0:T(8,128)(2,1)S(1)} %add_convert_fusion.1), channel_id=1, source_target_pairs={{0,8},{4,12},{8,0},{12,4},{1,9},{5,13},{9,1},{13,5},{2,10},{6,14},... | collective-permute-start | bytes 589832 | tf_op jit(solution)/shard_map/ppermute | solution.py:380
  25.3 21.3 %collective-permute-start.8 = (bf16[128,2048]{1,0:T(8,128)(2,1)}, bf16[128,2048]{1,0:T(8,128)(2,1)S(1)}, u32[]{:S(2)}, u32[]{:S(2)}) collective-permute-start(bf16[128,2048]{1,0:T(8,128)(2,1)} %get-tuple-element.52), channel_id=1, source_target_pairs={{0,4},{4,0},{8,12},{12,8},{1,5},{5,1},{9,13},{13,9},{2,6},{6,2},{1... | collective-permute-start | bytes 1572872 | tf_op jit(solution)/shard_map/ppermute | solution.py:380
  26.1 12.6 %collective-permute-start.7 = (bf16[128,2560]{1,0:T(8,128)(2,1)S(1)}, bf16[128,2560]{1,0:T(8,128)(2,1)S(1)}, u32[]{:S(2)}, u32[]{:S(2)}) collective-permute-start(bf16[128,2560]{1,0:T(8,128)(2,1)S(1)} %collective-permute-done.6.refs_6_.refs_10_), channel_id=1, source_target_pairs={{0,1},{1,0},{2,3},{3,2},{4,5},{5,4},{6,7},{7,6},{8,9},{9,8},{10,11... | collective-permute-start | bytes 1966088 | tf_op jit(solution)/shard_map/ppermute | solution.py:380
  26.2 0.7 %copy-start.2 = (bf16[128,768]{1,0:T(8,128)(2,1)}, bf16[128,768]{1,0:T(8,128)(2,1)S(1)}, u32[]{:S(2)}) copy-start(bf16[128,768]{1,0:T(8,128)(2,1)S(1)} %collective-permute-done.2.refs_0_) | copy-start | bytes 589828
  26.9 2.9 %collective-permute-start.3 = (bf16[80,128]{1,0:T(8,128)(2,1)S(1)}, bf16[80,128]{1,0:T(8,128)(2,1)S(1)}, u32[]{:S(2)}, u32[]{:S(2)}) collective-permute-start(bf16[80,128]{1,0:T(8,128)(2,1)S(1)} %pad_maximum_fusion.1.sums_ref.refs_0_), channel_id=1, source_target_pairs={{0,1},{1,0},{2,3},{3,2},{4,5},{5,4},{6,7},{7,6},{8,9},{9,8},{10,11... | collective-permute-start | bytes 61448 | tf_op jit(solution)/shard_map/ppermute | solution.py:380
  27.4 19.2 %collective-permute-start.9 = (bf16[128,1408]{1,0:T(8,128)(2,1)}, bf16[128,1408]{1,0:T(8,128)(2,1)S(1)}, u32[]{:S(2)}, u32[]{:S(2)}) collective-permute-start(bf16[128,1408]{1,0:T(8,128)(2,1)} %add_convert_fusion), channel_id=1, source_target_pairs={{0,8},{4,12},{8,0},{12,4},{1,9},{5,13},{9,1},{13,5},{2,10},{6,14},... | collective-permute-start | bytes 1081352 | tf_op jit(solution)/shard_map/ppermute | solution.py:380
  30.4 7.5 %collective-permute-start.4 = (bf16[160,128]{1,0:T(8,128)(2,1)}, bf16[160,128]{1,0:T(8,128)(2,1)}, u32[]{:S(2)}, u32[]{:S(2)}) collective-permute-start(bf16[160,128]{1,0:T(8,128)(2,1)} %pad_maximum_fusion), channel_id=1, source_target_pairs={{0,2},{1,3},{2,0},{3,1},{4,6},{5,7},{6,4},{7,5},{8,10},{9,11},{10,... | collective-permute-start | bytes 122888 | tf_op jit(solution)/shard_map/ppermute | solution.py:380
  32.9 1.2 %copy-start.1 = (f32[128,2048]{1,0:T(8,128)S(1)}, f32[128,2048]{1,0:T(8,128)}, u32[]{:S(2)}) copy-start(f32[128,2048]{1,0:T(8,128)} %copy-done) | copy-start | bytes 3145732
  34.1 0.9 %copy-start.3 = (bf16[128,768]{1,0:T(8,128)(2,1)S(1)}, bf16[128,768]{1,0:T(8,128)(2,1)}, u32[]{:S(2)}) copy-start(bf16[128,768]{1,0:T(8,128)(2,1)} %copy-done.2) | copy-start | bytes 589828

commit v4 on v3

--- a/solution.py
+++ b/solution.py
@@ -9,7 +9,7 @@
 
 ADAPTER_SCALE = 2.0
 LOSS_UNSCALE = 0.125
-VMEM_BYTES = 20 * 1024 * 1024
+VMEM_BYTES = 16 * 1024 * 1024
 COST = pl.CostEstimate(flops=0, bytes_accessed=0, transcendentals=0)
 
 f32 = jnp.float32
@@ -36,45 +36,64 @@
     return dot_nt(gk, wk) + dot_nt(gv, wv)
 
 
-def frozen_copies(block, width, wk_hbm, wv_hbm, wk, wv, sems):
-    rows = pl.ds(pl.multiple_of(block * width, width), width)
+def frozen_copies(first, count, wk_hbm, wv_hbm, wk, wv, key_sem, value_sem):
+    rows = pl.ds(pl.multiple_of(first, 128), count)
     return [
-        pltpu.make_async_copy(wk_hbm.at[rows], wk, sems.at[0]),
-        pltpu.make_async_copy(wv_hbm.at[rows], wv, sems.at[1]),
+        pltpu.make_async_copy(wk_hbm.at[rows], wk, key_sem),
+        pltpu.make_async_copy(wv_hbm.at[rows], wv, value_sem),
     ]
 
 
 def frozen_kernel(
-    first_ref, gk_hbm, gv_hbm, wk_hbm, wv_hbm, x2a_ref, x2b_ref, x1_ref, own_ref,
-    gk, gv, wk, wv, sems,
+    first_ref, gk_hbm, gv_hbm, wk_hbm, wv_hbm, x0b_ref, x2a_ref, x2b_ref, x1_ref, gk, gv, wk, wv,
+    sems,
 ):
     rows, width = x1_ref.shape
+    tail = x0b_ref.shape[1]
     z = lax.axis_index("tensor")
     head = [
         pltpu.make_async_copy(gk_hbm, gk, sems.at[3, 0]),
         pltpu.make_async_copy(gv_hbm, gv, sems.at[3, 1]),
     ]
-    body = [
-        frozen_copies(block, width, wk_hbm, wv_hbm, wk.at[n], wv.at[n], sems.at[n])
-        for n, block in enumerate((z ^ 2, z ^ 1, z))
-    ]
+    body = []
+    first = 0
+    for n, (start, count) in enumerate(
+        (((z ^ 3) * width + width - tail, tail), ((z ^ 2) * width, width), ((z ^ 1) * width, width))
+    ):
+        at = slice(first, first + count)
+        body.append(
+            frozen_copies(
+                start, count, wk_hbm, wv_hbm, wk.at[at], wv.at[at], sems.at[n, 0], sems.at[n, 1]
+            )
+        )
+        first += count
     for copies in (head, *body):
         for copy in copies:
             copy.start()
-    ahead = x2a_ref.shape[1] - rows
-    x2a_ref[:, ahead:] = first_ref[:, ahead:].astype(f32)
-    for copy in head + body[0]:
-        copy.wait()
-    x2a_ref[:, :ahead] = frozen_part(gk[...], gv[...], wk[0, :ahead], wv[0, :ahead])
-    x2b_ref[...] = frozen_part(gk[...], gv[...], wk[0, ahead:], wv[0, ahead:])
-    for n, out in ((1, x1_ref), (2, own_ref)):
-        for copy in body[n]:
-            copy.wait()
-        out[...] = frozen_part(gk[...], gv[...], wk[n], wv[n]).astype(out.dtype)
-
-
-def frozen_blocks(first_part, gk, gv, wk, wv, width):
+    early = x2a_ref.shape[1] - rows
+    x2a_ref[:, early:] = first_ref[:, first_ref.shape[1] - rows :].astype(f32)
+    for copy in head:
+        copy.wait()
+
+    def term(first, count):
+        at = slice(first, first + count)
+        return frozen_part(gk[...], gv[...], wk[at], wv[at])
+
+    for copy in body[0]:
+        copy.wait()
+    x0b_ref[...] = term(0, tail).astype(bf16)
+    for copy in body[1]:
+        copy.wait()
+    x2a_ref[:, :early] = term(tail, early)
+    x2b_ref[...] = term(tail + early, width - early)
+    for copy in body[2]:
+        copy.wait()
+    x1_ref[...] = term(tail + width, width).astype(bf16)
+
+
+def frozen_blocks(first_part, gk, gv, wk, wv, width, early):
     rows, feats = gk.shape
+    tail = width + rows - first_part.shape[1]
     hbm = pl.BlockSpec(memory_space=pltpu.HBM)
     vmem = pl.BlockSpec(memory_space=pltpu.VMEM)
     return pl.pallas_call(
@@ -82,16 +101,16 @@
         in_specs=[vmem] + [hbm] * 4,
         out_specs=[vmem] * 4,
         out_shape=[
-            jax.ShapeDtypeStruct(first_part.shape, f32),
-            jax.ShapeDtypeStruct((rows, width + rows - first_part.shape[1]), f32),
+            jax.ShapeDtypeStruct((rows, tail), bf16),
+            jax.ShapeDtypeStruct((rows, early + rows), f32),
+            jax.ShapeDtypeStruct((rows, width - early), f32),
             jax.ShapeDtypeStruct((rows, width), bf16),
-            jax.ShapeDtypeStruct((rows, width), f32),
         ],
         scratch_shapes=[
             pltpu.VMEM((rows, feats), bf16),
             pltpu.VMEM((rows, feats), bf16),
-            pltpu.VMEM((3, width, feats), bf16),
-            pltpu.VMEM((3, width, feats), bf16),
+            pltpu.VMEM((2 * width + tail, feats), bf16),
+            pltpu.VMEM((2 * width + tail, feats), bf16),
             pltpu.SemaphoreType.DMA((4, 2)),
         ],
         compiler_params=params(),
@@ -135,8 +154,6 @@
     frozen, len_hbm, tenant_hbm, slot_hbm, tok_hbm, gk_hbm, gv_hbm, kd_hbm, vd_hbm, ku_hbm, vu_hbm,
     wk_hbm, wv_hbm, out_ref, slots_ref, *refs,
 ):
-    if frozen:
-        last_ref, *refs = refs
     (
         len_ref, tenant_ref, slot_ref, tok, gk, gv, down, key_up, value_up, wk, wv, products, sems,
     ) = refs
@@ -156,7 +173,8 @@
     weights = []
     if frozen:
         weights = frozen_copies(
-            lax.axis_index("tensor") ^ 3, width, wk_hbm, wv_hbm, wk, wv, sems.at[3]
+            (lax.axis_index("tensor") ^ 3) * width, out_ref.shape[1] - rows, wk_hbm, wv_hbm, wk, wv, sems.at[3, 0],
+            sems.at[3, 1],
         )
     ups = [
         pltpu.make_async_copy(ku_hbm, key_up, sems.at[0, 5]),
@@ -200,8 +218,7 @@
     for copy in grads + weights:
         copy.wait()
     if frozen:
-        out_ref[:, :ahead] = frozen_part(gk[...], gv[...], wk[:ahead], wv[:ahead]).astype(bf16)
-        last_ref[...] = frozen_part(gk[...], gv[...], wk[ahead:], wv[ahead:]).astype(bf16)
+        out_ref[:, :ahead] = frozen_part(gk[...], gv[...], wk[...], wv[...]).astype(bf16)
     for copy in ups:
         copy.wait()
     for at, up, grad in ((2, key_up, gk), (3, value_up, gv)):
@@ -223,9 +240,9 @@
     hbm = pl.BlockSpec(memory_space=pltpu.HBM)
     vmem = pl.BlockSpec(memory_space=pltpu.VMEM)
     shapes = [(4 * rank, rows), (rank, rows)]
+    weight = pltpu.VMEM((frozen or 16, feats), bf16)
     if frozen:
-        ahead = width * 5 // 16
-        shapes = [(rows, ahead + rows), (rank, rows), (rows, width - ahead)]
+        shapes = [(rows, frozen + rows), (rank, rows)]
     return pl.pallas_call(
         functools.partial(first_kernel, frozen),
         in_specs=[hbm] * 12,
@@ -241,8 +258,8 @@
             pltpu.VMEM((both, width), bf16),
             pltpu.VMEM(ku.shape, bf16),
             pltpu.VMEM(vu.shape, bf16),
-            pltpu.VMEM((width, feats), bf16),
-            pltpu.VMEM((width, feats), bf16),
+            weight,
+            weight,
             pltpu.VMEM((ku.shape[0] * rank, rows), f32),
             pltpu.SemaphoreType.DMA((4, max(segments, 8))),
         ],
@@ -253,16 +270,22 @@
 
 
 def adapter_kernel(
-    frozen, len_ref, tenant_ref, sums_ref, term_ref, *refs
+    frozen, len_ref, tenant_ref, sums_ref, ahead_ref, gk_hbm, gv_hbm, wk_hbm, wv_hbm, kd_hbm,
+    vd_hbm, out_ref, gk, gv, wk, wv, down, back, sems,
 ):
-    if frozen:
-        ahead_ref, *refs = refs
-    kd_hbm, vd_hbm, out_ref, down, back, sems = refs
     segments = tenant_ref.shape[1]
     rank = kd_hbm.shape[1]
-    rows = out_ref.shape[0]
+    rows, width = out_ref.shape
     half = segments * rank
     copies = []
+    if frozen:
+        copies = [
+            pltpu.make_async_copy(gk_hbm, gk, sems.at[2, 2]),
+            pltpu.make_async_copy(gv_hbm, gv, sems.at[2, 3]),
+        ] + frozen_copies(
+            lax.axis_index("tensor") * width, width, wk_hbm, wv_hbm, wk, wv, sems.at[2, 0],
+            sems.at[2, 1],
+        )
     for k in range(segments):
         tenant = tenant_ref[0, k]
         at = pl.ds(k * rank, rank)
@@ -279,35 +302,43 @@
             back[start : start + rank, :] = jnp.where(masks[k], values, 0.0).astype(bf16)
     for copy in copies:
         copy.wait()
-    total = term_ref[...] + dot_tn(back[...], down[...])
-    out_ref[...] = total
+    total = dot_tn(back[...], down[...])
     if frozen:
-        ahead = ahead_ref.shape[1] - rows
-        out_ref[:, :ahead] = total[:, :ahead] + ahead_ref[:, :ahead].astype(f32)
-
-
-def add_adapters(terms, sums, kd, vd, lengths, tenants):
-    rows, width = terms[0].shape
+        total += frozen_part(gk[...], gv[...], wk[...], wv[...])
+    ahead = min(width, ahead_ref.shape[1] - rows) if frozen else width
+    out_ref[:, :ahead] = total[:, :ahead] + ahead_ref[:, :ahead].astype(f32)
+    if ahead < width:
+        out_ref[:, ahead:] = total[:, ahead:]
+
+
+def add_adapters(frozen, ahead_sum, sums, gk, gv, wk, wv, kd, vd, lengths, tenants):
+    rows, feats = gk.shape
+    width = kd.shape[2]
     segments = tenants.shape[1]
     rank = kd.shape[1]
     both = 2 * segments * rank
     smem = pl.BlockSpec(memory_space=pltpu.SMEM)
     vmem = pl.BlockSpec(memory_space=pltpu.VMEM)
     hbm = pl.BlockSpec(memory_space=pltpu.HBM)
+    weight = pltpu.VMEM((width, feats) if frozen else (16, feats), bf16)
     return pl.pallas_call(
-        functools.partial(adapter_kernel, len(terms) > 1),
-        in_specs=[smem, smem, vmem] + [vmem] * len(terms) + [hbm, hbm],
+        functools.partial(adapter_kernel, frozen),
+        in_specs=[smem, smem, vmem, vmem] + [hbm] * 6,
         out_specs=vmem,
         out_shape=jax.ShapeDtypeStruct((rows, width), f32),
         scratch_shapes=[
+            pltpu.VMEM((rows, feats), bf16),
+            pltpu.VMEM((rows, feats), bf16),
+            weight,
+            weight,
             pltpu.VMEM((both, width), bf16),
             pltpu.VMEM((both, rows), bf16),
-            pltpu.SemaphoreType.DMA((2, segments)),
+            pltpu.SemaphoreType.DMA((3, max(segments, 8))),
         ],
         compiler_params=params(),
         cost_estimate=COST,
         name="add_adapters",
-    )(lengths, tenants, sums, *terms, kd, vd)
+    )(lengths, tenants, sums, ahead_sum, gk, gv, wk, wv, kd, vd)
 
 
 def grads_kernel(count, rank, per_owner, first_ref, *refs):
@@ -395,35 +426,35 @@
     large = [in_hbm(array) for array in (gk, gv, wk, wv)]
     halving = n_tensor == 4
 
-    first_part, slot_rows, *second = first_products(
-        halving, in_hbm(tokens), large[0], large[1], kd, vd, in_hbm(ku), in_hbm(vu), *large[2:],
+    ahead, early = width * 8 // 16, width * 3 // 16
+    first_part, slot_rows = first_products(
+        ahead if halving else 0, in_hbm(tokens), large[0], large[1], kd, vd, in_hbm(ku), in_hbm(vu), *large[2:],
         in_hbm(segment_length), in_hbm(segment_tenant), in_hbm(adapter_output_slot),
     )
-    tokens, first_part, *second = lax.optimization_barrier((tokens, first_part, *second))
+    tokens, first_part = lax.optimization_barrier((tokens, first_part))
     sent = jnp.concatenate([tokens, gk, gv], axis=1)
     if halving:
-        ahead = first_part.shape[1] - rows
         r1a = swap(first_part, "tensor", 1, 4)
-        r1b = swap(second[0], "tensor", 1, 4)
-        x2a, x2b, x1, own = frozen_blocks(first_part, *large, width)
+        x0b, x2a, x2b, x1 = frozen_blocks(first_part, *large, width, early)
+        r1b = swap(x0b, "tensor", 1, 4)
         x2a, r1a = lax.optimization_barrier((x2a, r1a))
-        x2a = (x2a + r1a.astype(f32)).astype(bf16)
+        here = jnp.concatenate([r1a[:, :early], r1a[:, ahead:]], axis=1)
+        x2a = (x2a + here.astype(f32)).astype(bf16)
         r3a = swap(x2a, "tensor", 2, 4)
-        x2b, x1, r1b = lax.optimization_barrier((x2b, x1, r1b))
-        x2b = (x2b + r1b.astype(f32)).astype(bf16)
+        x1, x2a = lax.optimization_barrier((x1, x2a))
+        here = jnp.concatenate([r1a[:, early:ahead], r1b], axis=1)
+        x2b = (x2b + here.astype(f32)).astype(bf16)
         r3b = swap(x2b, "tensor", 2, 4)
         r4 = swap(x1, "tensor", 1, 4)
         x2b, r3a, x2a = lax.optimization_barrier((x2b, r3a, x2a))
-        total = x2a[: 4 * rank, ahead:].astype(f32) + r3a[: 4 * rank, ahead:].astype(f32)
-        terms = [own, r3a]
+        total = x2a[: 4 * rank, early:].astype(f32) + r3a[: 4 * rank, early:].astype(f32)
+        ahead_sum = r3a
     else:
         total = lax.psum(first_part.astype(f32), "tensor")
         term = dot_nt(gk, wk) + dot_nt(gv, wv)
-        terms = [
-            lax.psum_scatter(
-                term.astype(bf16), "tensor", scatter_dimension=1, tiled=True
-            ).astype(f32)
-        ]
+        ahead_sum = lax.psum_scatter(
+            term.astype(bf16), "tensor", scatter_dimension=1, tiled=True
+        )
     sums = jnp.concatenate([total.astype(bf16), slot_rows], axis=0)
 
     if n_dp == 4:
@@ -439,7 +470,7 @@
         gathered = lax.all_gather(sums, "dp")
         all_sums = [gathered[i] for i in range(n_dp)]
 
-    own = add_adapters(terms, sums, kd, vd, segment_length, segment_tenant)
+    own = add_adapters(halving, ahead_sum, sums, *large, kd, vd, segment_length, segment_tenant)
     grads = adapter_grads(first, all_sums, all_sent, rank, per_owner, width, feats)
     if halving:
         own, *grads = lax.optimization_barrier((own, *grads))

time: 47.9 us -> 45.8 us (0.956)
  local copies, waits for them, and re-layouts: 3.66 us -> 0.12 us
  Pallas kernels: 16.6 us -> 18.6 us
  starting transfers between devices: 13.2 us -> 14.3 us
  waiting for transfers between devices: 11.9 us -> 10.9 us
  other arithmetic: 1.47 us -> 0.9 us
    unnamed x20 -> x12, local copies, waits for them, and re-layouts: 2.9 us -> 0.07 us
    pallas_call x1, Pallas kernels: 2.87 us -> 4.22 us  [add_adapters(): pl.pallas_call(functools.partial(adapter_kernel, frozen), in_specs=[smem,...]
    ppermute x10, starting transfers between devices: 13.2 us -> 14.3 us  [swap(): return lax.ppermute(values, axis, [(i, i ^ bit) for i in range(size)])]
    pallas_call x1, Pallas kernels: 0.97 us -> 1.97 us  [finish(): pl.pallas_call(finish_kernel, in_specs=[vmem] * 3, out_specs=vmem, out_sh...]
    ppermute x10, waiting for transfers between devices: 11.9 us -> 10.9 us  [swap(): return lax.ppermute(values, axis, [(i, i ^ bit) for i in range(size)])]
    slice x1, local copies, waits for them, and re-layouts: 0.75 us -> 0.01 us  [local(): all_sums = [two[n * size:(n + 1) * size] for two in pairs for n in (0, 1)]]
    pallas_call x1, Pallas kernels: 4.73 us -> 4.06 us  [first_products(): pl.pallas_call(functools.partial(first_kernel, frozen), in_specs=[hbm] *...]
    concatenate x1, other arithmetic: 0.62 us -> 0.01 us  [local(): pair = jnp.concatenate([sums, swap(sums, 'dp', 1, 4)], axis=0)]
  transfers between devices with their start and end apart: 10 -> 10, of which waited for: 2 -> 6; matrix products, arithmetic and copies ran while one was open for 5% -> 2% of each run, Pallas kernels for 23% -> 28%
where the time goes in v4:
time: 45.8 us; the launch traced here: 45.6 us
  Pallas kernels  18.6 us (41%)
  starting transfers between devices  14.3 us (31%)
  waiting for transfers between devices  10.9 us (24%)
  other arithmetic  0.9 us (2%)
  between operations  0.81 us (2%)
    ppermute x10, starting transfers between devices, swap(): return lax.ppermute(values, axis, [(i, i ^ bit) for i in range(size)])  14.3 us
    ppermute x10, waiting for transfers between devices, swap(): return lax.ppermute(values, axis, [(i, i ^ bit) for i in range(size)])  10.9 us
    pallas_call x1, Pallas kernels, frozen_blocks(): pl.pallas_call(frozen_kernel, in_specs=[vmem] + [hbm] * 4, out_specs=[vme...  4.34 us
    pallas_call x1, Pallas kernels, add_adapters(): pl.pallas_call(functools.partial(adapter_kernel, frozen), in_specs=[smem,...  4.22 us
    pallas_call x1, Pallas kernels, first_products(): pl.pallas_call(functools.partial(first_kernel, frozen), in_specs=[hbm] *...  4.06 us
    pallas_call x1, Pallas kernels, adapter_grads(): pl.pallas_call(functools.partial(grads_kernel, count, rank, per_owner), g...  4 us
    pallas_call x1, Pallas kernels, finish(): pl.pallas_call(finish_kernel, in_specs=[vmem] * 3, out_specs=vmem, out_sh...  1.97 us
  transfers between devices with their start and end apart: 10, of which 6 were waited for; matrix products, arithmetic and copies ran while one was open for 2% of the time, Pallas kernels for 28%

profile of v4, /device:TPU:0, one launch (start us, length us, event | category | flops | bytes accessed | tf_op | source)
XLA Modules:
  0.0 45.6 jit_solution(10508314250972935286)
XLA Ops:
  0.6 4.1 %first_products.1 = (bf16[128,1152]{1,0:T(8,128)(2,1)S(1)}, bf16[16,128]{1,0:T(8,128)(2,1)S(1)}) custom-call(s32[1,16]{1,0:T(1,128)} %len_ref.1, s32[1,16]{1,0:T(1,128)} %tenant_ref.1, s32[64]{0:T(128)} %slot_hbm.1, bf16[128,2048]{1,0:T(8,128)(2,1)} %tok_hbm.1, bf16[128,256]{1,0:T(8,128)(2,1)} %gk_hbm.5, bf16[128,256]{1,0:T(8,128)(2,1)} %gv_hbm.5, ...), custom_call_target="tpu_custom_call" | custom-call | tf_op jit(solution)/shard_map/first_products/pallas_call | solution.py:246
  4.7 0.0 copy-start.2
  4.7 0.0 copy-start.3
  4.7 0.0 copy-start.4
  4.7 3.1 %collective-permute-start = (bf16[128,1152]{1,0:T(8,128)(2,1)S(1)}, bf16[128,1152]{1,0:T(8,128)(2,1)S(1)}, u32[]{:S(2)}, u32[]{:S(2)}) collective-permute-start(bf16[128,1152]{1,0:T(8,128)(2,1)S(1)} %get-tuple-element.29.first_ref), channel_id=1, source_target_pairs={{0,4},{4,0},{8,12},{12,8},{1,5},{5,1},{9,13},{13,9},{2,6},{6,2},{1... | collective-permute-start | bytes 884744 | tf_op jit(solution)/shard_map/ppermute | solution.py:411
  7.8 4.3 %frozen_blocks.1 = (bf16[128,1024]{1,0:T(8,128)(2,1)S(1)}, f32[128,512]{1,0:T(8,128)S(1)}, f32[128,1664]{1,0:T(8,128)S(1)}, bf16[128,2048]{1,0:T(8,128)(2,1)}) custom-call(bf16[128,1152]{1,0:T(8,128)(2,1)S(1)} %get-tuple-element.29.first_ref, bf16[128,256]{1,0:T(8,128)(2,1)} %gk_hbm.5, bf16[128,256]{1,0:T(8,128)(2,1)} %gv_hbm.5, bf16[8192,256]{1,0:T(8,128)(2,1)} %wk_hbm.5, ...), custom_call_target="tpu_custom_call" | custom-call | tf_op jit(solution)/shard_map/frozen_blocks/pallas_call | solution.py:99
  12.2 0.0 copy-start
  12.2 0.0 copy-start.1
  12.2 0.2 collective-permute-start.1
  12.4 0.0 copy-done.3
  12.4 1.9 %collective-permute-start.6 = (bf16[128,2560]{1,0:T(8,128)(2,1)S(1)}, bf16[128,2560]{1,0:T(8,128)(2,1)S(1)}, u32[]{:S(2)}, u32[]{:S(2)}) collective-permute-start(bf16[128,2560]{1,0:T(8,128)(2,1)S(1)} %constant_dynamic-update-slice_fusion.refs_4_.refs_8_), channel_id=1, source_target_pairs={{0,2},{1,3},{2,0},{3,1},{4,6},{5,7},{6,4},{7,5},{8,10},{9,11},{10,... | collective-permute-start | bytes 1966088 | tf_op jit(solution)/shard_map/ppermute | solution.py:411
  14.4 0.0 collective-permute-start.5
  14.4 0.9 %collective-permute-done = bf16[128,1152]{1,0:T(8,128)(2,1)S(1)} collective-permute-done((bf16[128,1152]{1,0:T(8,128)(2,1)S(1)}, bf16[128,1152]{1,0:T(8,128)(2,1)S(1)}, u32[]{:S(2)}, u32[]{:S(2)}) %collective-permute-start) | collective-permute-done | bytes 294944 | tf_op jit(solution)/shard_map/ppermute | solution.py:411
  15.3 2.9 %collective-permute-start.2 = (bf16[128,512]{1,0:T(8,128)(2,1)S(1)}, bf16[128,512]{1,0:T(8,128)(2,1)S(1)}, u32[]{:S(2)}, u32[]{:S(2)}) collective-permute-start(bf16[128,512]{1,0:T(8,128)(2,1)S(1)} %add_convert_fusion.1), channel_id=1, source_target_pairs={{0,8},{4,12},{8,0},{12,4},{1,9},{5,13},{9,1},{13,5},{2,10},{6,14},... | collective-permute-start | bytes 393224 | tf_op jit(solution)/shard_map/ppermute | solution.py:411
  18.3 2.2 %collective-permute-start.8 = (bf16[128,2048]{1,0:T(8,128)(2,1)}, bf16[128,2048]{1,0:T(8,128)(2,1)S(1)}, u32[]{:S(2)}, u32[]{:S(2)}) collective-permute-start(bf16[128,2048]{1,0:T(8,128)(2,1)} %get-tuple-element.46), channel_id=1, source_target_pairs={{0,4},{4,0},{8,12},{12,8},{1,5},{5,1},{9,13},{13,9},{2,6},{6,2},{1... | collective-permute-start | bytes 1572872 | tf_op jit(solution)/shard_map/ppermute | solution.py:411
  20.5 3.8 %collective-permute-done.1 = bf16[128,1024]{1,0:T(8,128)(2,1)S(1)} collective-permute-done((bf16[128,1024]{1,0:T(8,128)(2,1)S(1)}, bf16[128,1024]{1,0:T(8,128)(2,1)S(1)}, u32[]{:S(2)}, u32[]{:S(2)}) %collective-permute-start.1) | collective-permute-done | bytes 262176 | tf_op jit(solution)/shard_map/ppermute | solution.py:411
  24.3 0.9 %add_convert_fusion = bf16[128,1664]{1,0:T(8,128)(2,1)} fusion(f32[128,1664]{1,0:T(8,128)S(1)} %get-tuple-element.30, bf16[128,1024]{1,0:T(8,128)(2,1)S(1)} %collective-permute-done.1, bf16[128,640]{1,0:T(8,128)(2,1)S(1)} %slice.21), kind=kLoop, calls=%fused_computation | loop fusion | flops 1277952 | bytes 1703936 | tf_op jit(solution)/shard_map/convert_element_type | solution.py:446
  25.2 1.8 %collective-permute-start.9 = (bf16[128,1664]{1,0:T(8,128)(2,1)}, bf16[128,1664]{1,0:T(8,128)(2,1)}, u32[]{:S(2)}, u32[]{:S(2)}) collective-permute-start(bf16[128,1664]{1,0:T(8,128)(2,1)} %add_convert_fusion), channel_id=1, source_target_pairs={{0,8},{4,12},{8,0},{12,4},{1,9},{5,13},{9,1},{13,5},{2,10},{6,14},... | collective-permute-start | bytes 1277960 | tf_op jit(solution)/shard_map/ppermute | solution.py:411
  27.0 0.0 collective-permute-done.2.ahead_ref
  27.0 1.7 %collective-permute-done.6.refs_6_.refs_10_ = bf16[128,2560]{1,0:T(8,128)(2,1)S(1)} collective-permute-done((bf16[128,2560]{1,0:T(8,128)(2,1)S(1)}, bf16[128,2560]{1,0:T(8,128)(2,1)S(1)}, u32[]{:S(2)}, u32[]{:S(2)}) %collective-permute-start.6) | collective-permute-done | bytes 655392 | tf_op jit(solution)/shard_map/ppermute | solution.py:411
  28.7 0.0 collective-permute-start.7
  28.7 0.6 %collective-permute-start.3 = (bf16[80,128]{1,0:T(8,128)(2,1)S(1)}, bf16[80,128]{1,0:T(8,128)(2,1)S(1)}, u32[]{:S(2)}, u32[]{:S(2)}) collective-permute-start(bf16[80,128]{1,0:T(8,128)(2,1)S(1)} %pad_maximum_fusion.1.sums_ref.refs_0_), channel_id=1, source_target_pairs={{0,1},{1,0},{2,3},{3,2},{4,5},{5,4},{6,7},{7,6},{8,9},{9,8},{10,11... | collective-permute-start | bytes 61448 | tf_op jit(solution)/shard_map/ppermute | solution.py:411
  29.3 1.5 %collective-permute-done.3.refs_1_ = bf16[80,128]{1,0:T(8,128)(2,1)S(1)} collective-permute-done((bf16[80,128]{1,0:T(8,128)(2,1)S(1)}, bf16[80,128]{1,0:T(8,128)(2,1)S(1)}, u32[]{:S(2)}, u32[]{:S(2)}) %collective-permute-start.3) | collective-permute-done | bytes 20512 | tf_op jit(solution)/shard_map/ppermute | solution.py:411
  30.8 1.6 %collective-permute-start.4 = (bf16[160,128]{1,0:T(8,128)(2,1)S(1)}, bf16[160,128]{1,0:T(8,128)(2,1)S(1)}, u32[]{:S(2)}, u32[]{:S(2)}) collective-permute-start(bf16[160,128]{1,0:T(8,128)(2,1)S(1)} %pad_maximum_fusion), channel_id=1, source_target_pairs={{0,2},{1,3},{2,0},{3,1},{4,6},{5,7},{6,4},{7,5},{8,10},{9,11},{10,... | collective-permute-start | bytes 122888 | tf_op jit(solution)/shard_map/ppermute | solution.py:411
  32.4 4.2 %add_adapters.1.own_ref = f32[128,2048]{1,0:T(8,128)S(1)} custom-call(s32[1,16]{1,0:T(1,128)S(1)} %copy-done, s32[1,16]{1,0:T(1,128)S(1)} %copy-done.1, bf16[80,128]{1,0:T(8,128)(2,1)S(1)} %pad_maximum_fusion.1.sums_ref.refs_0_, bf16[128,512]{1,0:T(8,128)(2,1)S(1)} %collective-permute-done.2.ahead_ref, bf16[128,256]{1,0:T(8,128)(2,1)} %gk_hbm.5, ...), custom_call_target="tpu_custom_call" | custom-call | tf_op jit(solution)/shard_map/add_adapters/pallas_call | solution.py:324
  36.7 0.0 collective-permute-done.4
  36.7 0.0 collective-permute-done.5.refs_5_.refs_9_
  36.7 0.0 collective-permute-done.7.refs_7_.refs_11_
  36.7 4.0 %adapter_grads.1 = (f32[16,16,2048]{2,1,0:T(8,128)}, f32[16,16,2048]{2,1,0:T(8,128)}, f32[16,16,256]{2,1,0:T(8,128)}, f32[16,16,256]{2,1,0:T(8,128)}) custom-call(s32[1]{0:T(128)} %bitcast.first_ref, bf16[80,128]{1,0:T(8,128)(2,1)S(1)} %pad_maximum_fusion.1.sums_ref.refs_0_, bf16[80,128]{1,0:T(8,128)(2,1)S(1)} %collective-permute-done.3.refs_1_, ...), custom_call_target="tpu_custom_call" | custom-call | tf_op jit(solution)/shard_map/adapter_grads/pallas_call | solution.py:389
  40.7 2.3 %collective-permute-done.9.x2b_ref = bf16[128,1664]{1,0:T(8,128)(2,1)} collective-permute-done((bf16[128,1664]{1,0:T(8,128)(2,1)}, bf16[128,1664]{1,0:T(8,128)(2,1)}, u32[]{:S(2)}, u32[]{:S(2)}) %collective-permute-start.9) | collective-permute-done | bytes 426016 | tf_op jit(solution)/shard_map/ppermute | solution.py:411
  43.0 0.6 %collective-permute-done.8.x1_ref = bf16[128,2048]{1,0:T(8,128)(2,1)S(1)} collective-permute-done((bf16[128,2048]{1,0:T(8,128)(2,1)}, bf16[128,2048]{1,0:T(8,128)(2,1)S(1)}, u32[]{:S(2)}, u32[]{:S(2)}) %collective-permute-start.8) | collective-permute-done | bytes 524320 | tf_op jit(solution)/shard_map/ppermute | solution.py:411
  43.6 2.0 %finish.1 = bf16[128,2048]{1,0:T(8,128)(2,1)} custom-call(f32[128,2048]{1,0:T(8,128)S(1)} %add_adapters.1.own_ref, bf16[128,2048]{1,0:T(8,128)(2,1)S(1)} %collective-permute-done.8.x1_ref, bf16[128,1664]{1,0:T(8,128)(2,1)} %collective-permute-done.9.x2b_ref), custom_call_target="tpu_custom_call" | custom-call | tf_op jit(solution)/shard_map/finish/pallas_call | solution.py:131
  (15 shorter events, 0.1 us)
Async XLA Ops:
  4.7 7.7 %copy-start.2 = (bf16[128,2048]{1,0:T(8,128)(2,1)S(1)}, bf16[128,2048]{1,0:T(8,128)(2,1)}, u32[]{:S(2)}) copy-start(bf16[128,2048]{1,0:T(8,128)(2,1)} %tok_hbm.1) | copy-start | bytes 1572868
  4.7 7.7 %copy-start.3 = (bf16[128,256]{1,0:T(8,128)(2,1)S(1)}, bf16[128,256]{1,0:T(8,128)(2,1)}, u32[]{:S(2)}) copy-start(bf16[128,256]{1,0:T(8,128)(2,1)} %gk_hbm.5) | copy-start | bytes 196612
  4.7 7.7 %copy-start.4 = (bf16[128,256]{1,0:T(8,128)(2,1)S(1)}, bf16[128,256]{1,0:T(8,128)(2,1)}, u32[]{:S(2)}) copy-start(bf16[128,256]{1,0:T(8,128)(2,1)} %gv_hbm.5) | copy-start | bytes 196612
  4.7 10.5 %collective-permute-start = (bf16[128,1152]{1,0:T(8,128)(2,1)S(1)}, bf16[128,1152]{1,0:T(8,128)(2,1)S(1)}, u32[]{:S(2)}, u32[]{:S(2)}) collective-permute-start(bf16[128,1152]{1,0:T(8,128)(2,1)S(1)} %get-tuple-element.29.first_ref), channel_id=1, source_target_pairs={{0,4},{4,0},{8,12},{12,8},{1,5},{5,1},{9,13},{13,9},{2,6},{6,2},{1... | collective-permute-start | bytes 884744 | tf_op jit(solution)/shard_map/ppermute | solution.py:411
  12.2 20.2 %copy-start = (s32[1,16]{1,0:T(1,128)S(1)}, s32[1,16]{1,0:T(1,128)}, u32[]{:S(2)}) copy-start(s32[1,16]{1,0:T(1,128)} %len_ref.1) | copy-start | bytes 196
  12.2 20.2 %copy-start.1 = (s32[1,16]{1,0:T(1,128)S(1)}, s32[1,16]{1,0:T(1,128)}, u32[]{:S(2)}) copy-start(s32[1,16]{1,0:T(1,128)} %tenant_ref.1) | copy-start | bytes 196
  12.2 12.1 %collective-permute-start.1 = (bf16[128,1024]{1,0:T(8,128)(2,1)S(1)}, bf16[128,1024]{1,0:T(8,128)(2,1)S(1)}, u32[]{:S(2)}, u32[]{:S(2)}) collective-permute-start(bf16[128,1024]{1,0:T(8,128)(2,1)S(1)} %get-tuple-element.33), channel_id=1, source_target_pairs={{0,4},{4,0},{8,12},{12,8},{1,5},{5,1},{9,13},{13,9},{2,6},{6,2},{1... | collective-permute-start | bytes 786440 | tf_op jit(solution)/shard_map/ppermute | solution.py:411
  12.4 16.3 %collective-permute-start.6 = (bf16[128,2560]{1,0:T(8,128)(2,1)S(1)}, bf16[128,2560]{1,0:T(8,128)(2,1)S(1)}, u32[]{:S(2)}, u32[]{:S(2)}) collective-permute-start(bf16[128,2560]{1,0:T(8,128)(2,1)S(1)} %constant_dynamic-update-slice_fusion.refs_4_.refs_8_), channel_id=1, source_target_pairs={{0,2},{1,3},{2,0},{3,1},{4,6},{5,7},{6,4},{7,5},{8,10},{9,11},{10,... | collective-permute-start | bytes 1966088 | tf_op jit(solution)/shard_map/ppermute | solution.py:411
  14.4 22.3 %collective-permute-start.5 = (bf16[128,2560]{1,0:T(8,128)(2,1)S(1)}, bf16[128,2560]{1,0:T(8,128)(2,1)S(1)}, u32[]{:S(2)}, u32[]{:S(2)}) collective-permute-start(bf16[128,2560]{1,0:T(8,128)(2,1)S(1)} %constant_dynamic-update-slice_fusion.refs_4_.refs_8_), channel_id=1, source_target_pairs={{0,1},{1,0},{2,3},{3,2},{4,5},{5,4},{6,7},{7,6},{8,9},{9,8},{10,11... | collective-permute-start | bytes 1966088 | tf_op jit(solution)/shard_map/ppermute | solution.py:411
  15.3 11.7 %collective-permute-start.2 = (bf16[128,512]{1,0:T(8,128)(2,1)S(1)}, bf16[128,512]{1,0:T(8,128)(2,1)S(1)}, u32[]{:S(2)}, u32[]{:S(2)}) collective-permute-start(bf16[128,512]{1,0:T(8,128)(2,1)S(1)} %add_convert_fusion.1), channel_id=1, source_target_pairs={{0,8},{4,12},{8,0},{12,4},{1,9},{5,13},{9,1},{13,5},{2,10},{6,14},... | collective-permute-start | bytes 393224 | tf_op jit(solution)/shard_map/ppermute | solution.py:411
  18.3 25.4 %collective-permute-start.8 = (bf16[128,2048]{1,0:T(8,128)(2,1)}, bf16[128,2048]{1,0:T(8,128)(2,1)S(1)}, u32[]{:S(2)}, u32[]{:S(2)}) collective-permute-start(bf16[128,2048]{1,0:T(8,128)(2,1)} %get-tuple-element.46), channel_id=1, source_target_pairs={{0,4},{4,0},{8,12},{12,8},{1,5},{5,1},{9,13},{13,9},{2,6},{6,2},{1... | collective-permute-start | bytes 1572872 | tf_op jit(solution)/shard_map/ppermute | solution.py:411
  25.2 17.9 %collective-permute-start.9 = (bf16[128,1664]{1,0:T(8,128)(2,1)}, bf16[128,1664]{1,0:T(8,128)(2,1)}, u32[]{:S(2)}, u32[]{:S(2)}) collective-permute-start(bf16[128,1664]{1,0:T(8,128)(2,1)} %add_convert_fusion), channel_id=1, source_target_pairs={{0,8},{4,12},{8,0},{12,4},{1,9},{5,13},{9,1},{13,5},{2,10},{6,14},... | collective-permute-start | bytes 1277960 | tf_op jit(solution)/shard_map/ppermute | solution.py:411
  28.7 8.0 %collective-permute-start.7 = (bf16[128,2560]{1,0:T(8,128)(2,1)S(1)}, bf16[128,2560]{1,0:T(8,128)(2,1)S(1)}, u32[]{:S(2)}, u32[]{:S(2)}) collective-permute-start(bf16[128,2560]{1,0:T(8,128)(2,1)S(1)} %collective-permute-done.6.refs_6_.refs_10_), channel_id=1, source_target_pairs={{0,1},{1,0},{2,3},{3,2},{4,5},{5,4},{6,7},{7,6},{8,9},{9,8},{10,11... | collective-permute-start | bytes 1966088 | tf_op jit(solution)/shard_map/ppermute | solution.py:411
  28.7 2.1 %collective-permute-start.3 = (bf16[80,128]{1,0:T(8,128)(2,1)S(1)}, bf16[80,128]{1,0:T(8,128)(2,1)S(1)}, u32[]{:S(2)}, u32[]{:S(2)}) collective-permute-start(bf16[80,128]{1,0:T(8,128)(2,1)S(1)} %pad_maximum_fusion.1.sums_ref.refs_0_), channel_id=1, source_target_pairs={{0,1},{1,0},{2,3},{3,2},{4,5},{5,4},{6,7},{7,6},{8,9},{9,8},{10,11... | collective-permute-start | bytes 61448 | tf_op jit(solution)/shard_map/ppermute | solution.py:411
  30.8 5.8 %collective-permute-start.4 = (bf16[160,128]{1,0:T(8,128)(2,1)S(1)}, bf16[160,128]{1,0:T(8,128)(2,1)S(1)}, u32[]{:S(2)}, u32[]{:S(2)}) collective-permute-start(bf16[160,128]{1,0:T(8,128)(2,1)S(1)} %pad_maximum_fusion), channel_id=1, source_target_pairs={{0,2},{1,3},{2,0},{3,1},{4,6},{5,7},{6,4},{7,5},{8,10},{9,11},{10,... | collective-permute-start | bytes 122888 | tf_op jit(solution)/shard_map/ppermute | solution.py:411
